TPU v7x, 32 devices: a whole 2x2x4 slice. The times are simulated.
32 devices in a mesh: seq: 8 (over z, core), dp: 4 (over y, x).
Axes of the slice: x: 2, y: 2, z: 4, core: 2. Of those that a mesh axis runs over, the one named last changes fastest.
Arguments:
- queries: bfloat16 [4, 1024, 1024], P('dp', 'seq'), may hold values from -6 to 6
- key_vectors: bfloat16 [4, 1024, 1024], P('dp', 'seq'), may hold values from -6 to 6
- value_vectors: bfloat16 [4, 1024, 1024], P('dp', 'seq'), may hold values from -64 to 64
- log_decay: float32 [4, 1024, 16], P('dp', 'seq'), may hold values from -1 to 0, as said below
- restart: int32 [4, 1024], P('dp', 'seq'), may hold values 0 or 1
- norm_gain: float32 [1024], replicated, may hold values from 0.5 to 1.5
- upstream: bfloat16 [4, 1024, 1024], P('dp', 'seq'), may hold values from -6 to 6
Outputs:
- layer_out: bfloat16 [4, 1024, 1024], P('dp', 'seq')
- grad_query: bfloat16 [4, 1024, 1024], P('dp', 'seq')
- grad_key: bfloat16 [4, 1024, 1024], P('dp', 'seq')
- grad_value: bfloat16 [4, 1024, 1024], P('dp', 'seq')
- grad_decay: float32 [4, 1024, 16], P('dp', 'seq')
- grad_gain: float32 [1024], replicated
Inputs may be any that keep to these rules, and one draw needn't show every extreme that they name: `log_decay`: never positive. `restart`: 1 marks a sample before which the state is cleared.
All inputs are finite; a program needn't handle non-finite values. No bound on the sum of `restart` on one device may be relied on, other than what follows from the above.
Results may differ from a plain program's by a relative error of at most 0.0096.
Values sent between devices are 32-bit elements; how exact they have to be, the bound alone decides.
No kernel may reach another device: no remote copies, remote signals or barrier semaphores. Data moves between devices by JAX's collectives and lax.ppermute only.
A program may use at most 128 MiB of HBM per device.

v0:
```python
import jax
import jax.numpy as jnp
from jax import lax
from jax.sharding import PartitionSpec as P

HEAD_TOTAL = 16


EPSILON = 1e-06
EXACT = lax.Precision.HIGHEST


def blend(pattern, first_operand, second_operand):
    return jnp.einsum(pattern, first_operand, second_operand, preferred_element_type=jnp.float32)


def exact(pattern, first_operand, second_operand):
    return jnp.einsum(pattern, first_operand, second_operand, precision=EXACT)


def split_heads(row_data, head_count):
    return row_data.reshape(
        row_data.shape[0], row_data.shape[1], head_count, row_data.shape[2] // head_count
    )


def decay_tables(log_decay, restart):
    summed = jnp.cumsum(log_decay, axis=1)
    resets = jnp.cumsum(restart, axis=1, dtype=jnp.int32)
    last_total = summed[:, -1, :]
    last_reset = resets[:, -1:]
    entry_decay = jnp.where((resets == 0)[:, :, None], jnp.exp(summed), 0.0)
    exit_decay = jnp.where(
        (resets == last_reset)[:, :, None], jnp.exp(last_total[:, None, :] - summed), 0.0
    )
    block_carry = jnp.where(last_reset == 0, jnp.exp(last_total), 0.0)
    by_head = jnp.transpose(summed, (0, 2, 1))
    spread = by_head[:, :, :, None] - by_head[:, :, None, :]
    row_index = lax.broadcasted_iota(jnp.int32, spread.shape, 2)
    col_index = lax.broadcasted_iota(jnp.int32, spread.shape, 3)
    allowed = (row_index >= col_index) & (resets[:, None, :, None] == resets[:, None, None, :])
    pair_decay = jnp.exp(jnp.where(allowed, spread, -1e30))
    return (entry_decay, exit_decay, block_carry, pair_decay)


def block_state(key_heads, value_heads, exit_decay):
    decayed_keys = key_heads.astype(jnp.float32) * exit_decay[..., None]
    return (exact("bjhe,bjhf->bhef", decayed_keys, value_heads.astype(jnp.float32)), decayed_keys)


def block_forward(
    query_heads,
    key_heads,
    value_heads,
    entry_decay,
    pair_decay,
    state_in,
    norm_gain,
    upstream_heads,
):
    head_count = query_heads.shape[2]
    scores = blend("bihe,bjhe->bhij", query_heads, key_heads)
    weights = (scores * pair_decay).astype(jnp.bfloat16)
    local_part = blend("bhij,bjhe->bihe", weights, value_heads)
    decayed_queries = query_heads.astype(jnp.float32) * entry_decay[..., None]
    carried_part = exact("bihe,bhef->bihf", decayed_queries, state_in)
    mixture = local_part + carried_part
    inverse = lax.rsqrt(jnp.mean(mixture * mixture, axis=-1, keepdims=True) + EPSILON)
    normed = mixture * inverse
    gain_heads = norm_gain.reshape(head_count, -1)
    layer_out = (normed * gain_heads).astype(jnp.bfloat16)
    upstream_float = upstream_heads.astype(jnp.float32)
    gain_part = jnp.sum(upstream_float * normed, axis=(0, 1))
    grad_normed = upstream_float * gain_heads
    grad_mixed = (
        inverse * (grad_normed - normed * jnp.mean(grad_normed * normed, axis=-1, keepdims=True))
    ).astype(jnp.bfloat16)
    query_state = exact("bihe,bihf->bhef", decayed_queries, grad_mixed.astype(jnp.float32))
    flat_out = layer_out.reshape(layer_out.shape[0], layer_out.shape[1], -1)
    return (scores, weights, carried_part, flat_out, gain_part, grad_mixed, query_state)


def block_backward(
    query_heads,
    key_heads,
    value_heads,
    entry_decay,
    exit_decay,
    block_carry,
    pair_decay,
    scores,
    weights,
    carried_part,
    decayed_keys,
    grad_mixed,
    state_in,
    state_grad,
):
    grad_pairs = blend("bihe,bjhe->bhij", grad_mixed, value_heads)
    grad_weights = (grad_pairs * pair_decay).astype(jnp.bfloat16)
    mixed_float = grad_mixed.astype(jnp.float32)
    values_float = value_heads.astype(jnp.float32)
    grad_query = blend("bhij,bjhe->bihe", grad_weights, key_heads) + exact(
        "bihf,bhef->bihe", mixed_float * entry_decay[..., None], state_in
    )
    grad_key = blend("bhij,bihe->bjhe", grad_weights, query_heads) + exact(
        "bjhf,bhef->bjhe", values_float * exit_decay[..., None], state_grad
    )
    carried_value = exact("bjhe,bhef->bjhf", decayed_keys, state_grad)
    grad_value = blend("bhij,bihe->bjhe", weights, grad_mixed) + carried_value
    pair_terms = scores * grad_pairs * pair_decay
    balance = jnp.sum(pair_terms, axis=3) - jnp.sum(pair_terms, axis=2)
    later_terms = jnp.transpose(balance, (0, 2, 1)) + jnp.sum(carried_part * mixed_float, axis=-1)
    earlier_terms = jnp.sum(carried_value * values_float, axis=-1)
    through = block_carry * jnp.sum(state_in * state_grad, axis=(2, 3))
    grad_decay = (
        jnp.flip(jnp.cumsum(jnp.flip(later_terms, 1), axis=1), 1)
        + (jnp.cumsum(earlier_terms, axis=1) - earlier_terms)
        + through[:, None, :]
    )
    row_shape = (grad_query.shape[0], grad_query.shape[1], -1)
    return (
        grad_query.reshape(row_shape).astype(jnp.bfloat16),
        grad_key.reshape(row_shape).astype(jnp.bfloat16),
        grad_value.reshape(row_shape).astype(jnp.bfloat16),
        grad_decay,
    )


def weighted_sum(block_weights, fragment):
    return jnp.sum(block_weights[..., None, None] * fragment, axis=0)


def local(queries, key_vectors, value_vectors, log_decay, restart, norm_gain, upstream):
    entry_decay, exit_decay, block_carry, pair_decay = decay_tables(log_decay, restart)
    query_heads = split_heads(queries, HEAD_TOTAL)
    key_heads = split_heads(key_vectors, HEAD_TOTAL)
    value_heads = split_heads(value_vectors, HEAD_TOTAL)
    upstream_heads = split_heads(upstream, HEAD_TOTAL)
    state_part, decayed_keys = block_state(key_heads, value_heads, exit_decay)
    every_carry = lax.all_gather(block_carry[None], "seq", axis=0, tiled=True)
    position = lax.axis_index("seq")
    ranks = jnp.arange(lax.axis_size("seq"), dtype=jnp.int32)
    source = ranks[:, None]
    middle = ranks[None, :]
    factors = every_carry[None]
    before_span = (middle > source) & (middle < position)
    before_weight = jnp.where(
        (ranks < position)[:, None, None],
        jnp.prod(jnp.where(before_span[:, :, None, None], factors, 1.0), axis=1),
        0.0,
    )
    after_span = (middle > position) & (middle < source)
    after_weight = jnp.where(
        (ranks > position)[:, None, None],
        jnp.prod(jnp.where(after_span[:, :, None, None], factors, 1.0), axis=1),
        0.0,
    )
    state_in = weighted_sum(
        before_weight, lax.all_gather(state_part[None], "seq", axis=0, tiled=True)
    )
    results = block_forward(
        query_heads,
        key_heads,
        value_heads,
        entry_decay,
        pair_decay,
        state_in,
        norm_gain,
        upstream_heads,
    )
    scores, weights, carried_part, layer_out, gain_part, grad_mixed, query_state = results
    grad_gain = lax.psum(gain_part.reshape(-1), ("seq", "dp"))
    state_grad = weighted_sum(
        after_weight, lax.all_gather(query_state[None], "seq", axis=0, tiled=True)
    )
    grad_query, grad_key, grad_value, grad_decay = block_backward(
        query_heads,
        key_heads,
        value_heads,
        entry_decay,
        exit_decay,
        block_carry,
        pair_decay,
        scores,
        weights,
        carried_part,
        decayed_keys,
        grad_mixed,
        state_in,
        state_grad,
    )
    return (layer_out, grad_query, grad_key, grad_value, grad_decay, grad_gain)


def solution(mesh):
    return jax.shard_map(
        local,
        mesh=mesh,
        in_specs=(
            P("dp", "seq", None),
            P("dp", "seq", None),
            P("dp", "seq", None),
            P("dp", "seq", None),
            P("dp", "seq"),
            P(),
            P("dp", "seq", None),
        ),
        out_specs=(
            P("dp", "seq", None),
            P("dp", "seq", None),
            P("dp", "seq", None),
            P("dp", "seq", None),
            P("dp", "seq", None),
            P(),
        ),
        check_vma=False,
    )
```

profile of v0, /device:TPU:0, one launch (start us, length us, event | category | flops | bytes accessed | tf_op | source)
XLA Modules:
  0.0 138.5 jit_solution(7165165894792473100)
XLA Ops:
  7.2 1.0 reduce_window_sum.36
  10.1 0.8 copy.78
  11.2 1.1 copy.77
  12.4 1.1 copy.81
  13.5 1.4 fusion.12
  15.8 1.1 copy.76
  16.9 1.1 copy.85
  18.0 13.5 %all_gather.9 = f32[8,1,16]{2,1,0:T(1,128)S(1)} all-gather(f32[1,1,16]{2,1,0:T(1,128)S(1)} %get-tuple-element.40), channel_id=1, replica_groups=mesh['seq'=8,'dp'=4] {'seq'}, dimensions={0}, use_global_device_ids=true | all-gather | bytes 576 | tf_op jit(solution)/shard_map/all_gather | solution.py:141
  31.8 1.3 fusion.31
  33.1 31.7 %all-gather.5.cloned.1.call-done = f32[128,64,64]{2,1,0:T(8,128)} async-done(((f32[16,64,64]{2,1,0:T(8,128)}), f32[128,64,64]{2,1,0:T(8,128)}) %all-gather.5.cloned.1.call-update) | async-done | bytes 2097168 | tf_op jit(solution)/shard_map/all_gather | solution.py:160
  64.9 2.8 %multiply_reduce_fusion.1 = f32[16,64,64]{2,1,0:T(8,128)S(1)} fusion(f32[8,1,16,64,64]{4,3,2,0,1:T(8,128)} %bitcast.107, f32[8,16]{1,0:T(8,128)S(1)} %broadcast_select_fusion.1), kind=kLoop, calls=%fused_computation.1 | loop fusion | flops 983040 | bytes 2359808 | tf_op jit(solution)/shard_map/reduce_sum | solution.py:131
  67.7 1.0 convolution_bitcast_fusion.5
  69.9 1.3 fusion.11
  71.6 0.8 copy.91
  72.5 2.9 %fusion.23 = (f32[16,128]{1,0:T(8,128)S(1)}, f32[16,128]{1,0:T(8,128)S(1)}, f32[16,128,128]{2,1,0:T(8,128)}) fusion(f32[16,128]{1,0:T(8,128)S(1)} %copy.79, pred[128,128]{1,0:T(8,128)(4,1)S(1)} %broadcast_compare_fusion, f32[16,128,128]{2,1,0:T(8,128)} %fusion.31, bf16[128,16,64]{0,2,1:T(8,128)(2,1)S(1)} %bitcast.118, ...), kind=kOutput, calls=%fused_computation.48 | convolution fusion | flops 35647488 | bytes 2662400 | tf_op jit(solution)/shard_map/bihe,bjhe->bhij/dot_general | solution.py:14
  75.8 1.8 %convolution_bitcast_fusion.2 = f32[16,64,128]{2,1,0:T(8,128)S(1)} fusion(bf16[128,16,64]{0,2,1:T(8,128)(2,1)S(1)} %bitcast.110, f32[16,128,128]{2,1,0:T(8,128)} %get-tuple-element.46, f32[16,128]{1,0:T(8,128)S(1)} %copy.79, pred[128,128]{1,0:T(8,128)(4,1)S(1)} %broadcast_compare_fusion), kind=kOutput, calls=%fused_computation.6 | convolution fusion | flops 35127296 | bytes 1859584 | tf_op jit(solution)/shard_map/bhij,bjhe->bihe/dot_general | solution.py:14
  78.3 0.9 copy.92
  79.2 41.6 %psum.7 = f32[1024]{0:T(1024)} all-reduce(f32[1024]{0:T(1024)S(1)} %reshape.556), channel_id=1, replica_groups=mesh['seq'=8,'dp'=4] {'seq','dp'}, use_global_device_ids=true, to_apply=%region_16.17 | all-reduce | flops 1024 | bytes 8192 | tf_op jit(solution)/shard_map/psum | solution.py:173
  120.8 1.8 %convolution_bitcast_fusion = f32[16,64,128]{2,1,0:T(8,128)S(1)} fusion(bf16[128,16,64]{0,2,1:T(8,128)(2,1)S(1)} %bitcast.115, f32[16,128,128]{2,1,0:T(8,128)} %get-tuple-element.46, f32[16,128]{1,0:T(8,128)S(1)} %copy.79, pred[128,128]{1,0:T(8,128)(4,1)S(1)} %broadcast_compare_fusion), kind=kOutput, calls=%fused_computation.2 | convolution fusion | flops 35127296 | bytes 1859584 | tf_op jit(solution)/shard_map/bhij,bihe->bjhe/dot_general | solution.py:14
  122.6 2.7 %multiply_reduce_fusion = f32[16,64,64]{2,1,0:T(8,128)S(1)} fusion(f32[8,1,16,64,64]{4,3,2,0,1:T(8,128)} %bitcast.106, f32[8,16]{1,0:T(8,128)S(1)} %broadcast_select_fusion), kind=kLoop, calls=%fused_computation | loop fusion | flops 983040 | bytes 2359808 | tf_op jit(solution)/shard_map/reduce_sum | solution.py:131
  125.5 1.0 multiply_reduce_fusion.4
  126.8 1.8 %fusion.2 = bf16[1,128,16,64]{1,3,2,0:T(8,128)(2,1)S(1)} fusion(f32[1,128,16,64]{1,3,2,0:T(8,128)S(1)} %get-tuple-element.48, bf16[1,128,16,64]{1,3,2,0:T(8,128)(2,1)S(1)} %get-tuple-element.36, f32[16,128,128]{2,1,0:T(8,128)} %fusion.31, f32[16,128]{1,0:T(8,128)S(1)} %copy.79, pred[128,128]{1,0:T(8,128)(4,1)S(1)} %broadcast_compare_fusion), kind=kOutput, calls=%fused_computation.12 | convolution fusion | flops 35389440 | bytes 2121728 | tf_op jit(solution)/shard_map/bhij,bihe->bjhe/dot_general | solution.py:14
  128.6 0.9 copy.94
  130.8 0.8 copy.93
  (46 shorter events, 7.3 us)
Async XLA Ops:
  7.2 57.7 %all-gather.5.cloned.1.call-start = ((), (), s32[]{:S(2)}) async-start(), calls=%async_computation | async-start | bytes 4718592 | tf_op jit(solution)/shard_map/all_gather | solution.py:160
  14.9 107.7 %all-gather.7.cloned.1.call-start = ((), (), s32[]{:S(2)}) async-start(), calls=%async_computation.1 | async-start | bytes 4718592 | tf_op jit(solution)/shard_map/all_gather | solution.py:175
  64.9 3.8 %copy-start.1 = (f32[16,128,128]{2,1,0:T(8,128)S(1)}, f32[16,128,128]{2,1,0:T(8,128)}, u32[]{:S(2)}) copy-start(f32[16,128,128]{2,1,0:T(8,128)} %fusion.31) | copy-start | bytes 3145732
  67.7 3.7 %copy-start = (bf16[1,128,1024]{2,1,0:T(8,128)(2,1)S(1)}, bf16[1,128,1024]{2,1,0:T(8,128)(2,1)}, u32[]{:S(2)}) copy-start(bf16[1,128,1024]{2,1,0:T(8,128)(2,1)} %param.9) | copy-start | bytes 786436
Sparse Core Ops, SparseCore 0:
  15.0 49.8 all-gather.4
  71.4 46.8 all-gather.6
where the time goes:
time: 139 us; the launch traced here: 138 us
  blocking collectives  55.1 us (40%)
  waiting for transfers between devices  31.8 us (23%)
  matrix products  16.2 us (12%)
  between operations  14.9 us (11%)
  local copies, waits for them, and re-layouts  11.4 us (8%)
  other arithmetic  9.02 us (6%)
    psum x1, blocking collectives, local(): grad_gain = lax.psum(gain_part.reshape(-1), ('seq', 'dp'))  41.6 us
    all_gather x1, waiting for transfers between devices, local(): lax.all_gather(state_part[None], 'seq', axis=0, tiled=True)  31.7 us
    all_gather x1, blocking collectives, local(): every_carry = lax.all_gather(block_carry[None], 'seq', axis=0, tiled=True)  13.5 us
    dot_general x6, matrix products, blend(): jnp.einsum(pattern, first_operand, second_operand, preferred_element_type...  10.2 us
    unnamed x13, local copies, waits for them, and re-layouts  8.28 us
    dot_general x6, matrix products, exact(): return jnp.einsum(pattern, first_operand, second_operand, precision=EXACT)  6.07 us
    reduce_sum x2, other arithmetic, weighted_sum(): return jnp.sum(block_weights[..., None, None] * fragment, axis=0)  5.48 us
  transfers between devices with their start and end apart: 2, of which 1 were waited for; matrix products, arithmetic and copies ran while one was open for 10% of the time, Pallas kernels for 0%

commit v1 on v0

v1 whole, which is shorter than its diff:
```python
import functools

import jax
import jax.numpy as jnp
from jax import lax
from jax.experimental import pallas as pl
from jax.experimental.pallas import tpu as pltpu
from jax.sharding import PartitionSpec as P

HEAD_TOTAL = 16
EPSILON = 1e-06
LANES = 128
F32 = jnp.float32
BF16 = jnp.bfloat16
COLUMNS, MASK, CUM_ROWS, CARRY_ROWS, TABLE_ROWS = 0, 128, 256, 272, 288


def dot(a, b, contract_a=1, contract_b=0):
    return lax.dot_general(
        a, b, (((contract_a,), (contract_b,)), ((), ())), preferred_element_type=F32
    )


def halves(x):
    high = x.astype(BF16)
    return high, (x - high.astype(F32)).astype(BF16)


def stacked(x, axis):
    return jnp.concatenate(halves(x), axis=axis)


def twice(x, axis):
    return jnp.concatenate([x, x], axis=axis)


def left_lanes(shape):
    return lax.broadcasted_iota(jnp.int32, shape, 1) < LANES // 2


def triangle(tokens, keep):
    rows = lax.broadcasted_iota(jnp.int32, (tokens, tokens), 0)
    columns = lax.broadcasted_iota(jnp.int32, (tokens, tokens), 1)
    return keep(rows, columns)


def by_head(x, axis):
    left = left_lanes(x.shape)
    zero = jnp.zeros_like(x)
    return jnp.concatenate([jnp.where(left, x, zero), jnp.where(left, zero, x)], axis=axis)


def fold(x):
    rows = x.shape[0] // 2
    return jnp.where(left_lanes((rows, LANES)), x[:rows], x[rows:])


def pair_columns(table, first, tokens):
    return jnp.where(
        left_lanes((tokens, LANES)),
        jnp.broadcast_to(table[:, first : first + 1], (tokens, LANES)),
        jnp.broadcast_to(table[:, first + 1 : first + 2], (tokens, LANES)),
    )


def make_tables(log_decay, restart):
    tokens = log_decay.shape[0]
    heads = log_decay.shape[1]
    lower = triangle(tokens, lambda t, s: s <= t).astype(F32).astype(BF16)
    upper = triangle(tokens, lambda t, s: t <= s).astype(F32).astype(BF16)
    marks = jnp.broadcast_to(restart.astype(F32), (tokens, tokens)).astype(BF16)
    resets_column = dot(lower, marks, 1, 1)
    resets_row = dot(marks, upper)
    padded = jnp.concatenate(
        [log_decay, jnp.zeros((tokens, LANES - heads), F32)], axis=1
    )
    first, rest = halves(padded)
    third = (padded - first.astype(F32) - rest.astype(F32)).astype(BF16)
    cum = dot(
        jnp.concatenate([lower, lower, lower], axis=1),
        jnp.concatenate([first, rest, third], axis=0),
    )
    last = cum[tokens - 1 :, :]
    last_reset = resets_column[tokens - 1 :, :]
    entry = jnp.where(resets_column == 0.0, jnp.exp(cum), 0.0)
    leave = jnp.where(resets_column == last_reset, jnp.exp(last - cum), 0.0)
    lane = lax.broadcasted_iota(jnp.int32, (tokens, LANES), 1)
    columns = jnp.where(
        lane < heads,
        cum,
        jnp.where(lane < 2 * heads, pltpu.roll(entry, heads, 1), pltpu.roll(leave, 2 * heads, 1)),
    )
    allowed = triangle(tokens, lambda t, s: t >= s) & (resets_column == resets_row)
    mask = jnp.where(allowed, 0.0, -1e30)
    cum_rows = jnp.transpose(cum)[:heads]
    carry = jnp.where(last_reset[:, :1] == 0.0, jnp.exp(cum_rows[:, tokens - 1 :]), 0.0)
    return columns, mask, cum_rows, jnp.broadcast_to(carry, (heads, LANES))


def pick_columns(columns, half):
    return jnp.where(half == 0, columns, pltpu.roll(columns, LANES - HEAD_TOTAL // 2, 1))


def pick_rows(rows, half):
    count = HEAD_TOTAL // 2
    return jnp.where(half == 0, rows[:count], rows[count:])


def write_states(half, columns, carry_rows, key_ref, value_ref, out_ref):
    tokens = key_ref.shape[1]
    table = pick_columns(columns, half)
    carry = pick_rows(carry_rows, half)
    left = left_lanes((1, LANES))
    rows = []
    for pair in range(HEAD_TOTAL // 4):
        lanes = pl.ds(pair * LANES, LANES)
        leave = pair_columns(table, 2 * HEAD_TOTAL + 2 * pair, tokens)
        decayed = key_ref[0, :, lanes].astype(F32) * leave
        state = dot(stacked(decayed, 0), twice(value_ref[0, :, lanes], 0), 0, 0)
        out_ref[pl.ds(pair * 64, 64), :] = fold(state)
        rows.append(jnp.where(left, carry[2 * pair : 2 * pair + 1], carry[2 * pair + 1 : 2 * pair + 2]))
    rows.append(jnp.zeros((8 - len(rows), LANES), F32))
    out_ref[pl.ds(HEAD_TOTAL // 4 * 64, 8), :] = jnp.concatenate(rows, axis=0)


def first_state_kernel(half_ref, key_ref, value_ref, decay_ref, restart_ref, out_ref, table_ref):
    columns, mask, cum_rows, carry_rows = make_tables(decay_ref[0], restart_ref[...])
    table_ref[pl.ds(COLUMNS, 128), :] = columns
    table_ref[pl.ds(MASK, 128), :] = mask
    table_ref[pl.ds(CUM_ROWS, 16), :] = cum_rows
    table_ref[pl.ds(CARRY_ROWS, 16), :] = carry_rows
    write_states(half_ref[0], columns, carry_rows, key_ref, value_ref, out_ref)


def second_state_kernel(half_ref, key_ref, value_ref, table_ref, out_ref):
    write_states(
        half_ref[0],
        table_ref[pl.ds(COLUMNS, 128), :],
        table_ref[pl.ds(CARRY_ROWS, 16), :],
        key_ref,
        value_ref,
        out_ref,
    )


def pair_decays(table, cum_rows, mask, pair, tokens):
    parts = []
    for head in (2 * pair, 2 * pair + 1):
        column = jnp.broadcast_to(table[:, head : head + 1], (tokens, tokens))
        parts.append(jnp.exp(column - cum_rows[head : head + 1] + mask))
    return jnp.concatenate(parts, axis=0)


def side_by_side(x):
    rows = x.shape[0] // 2
    return jnp.concatenate([x[:rows], x[rows:]], axis=1)


def mixture_kernel(half_ref, query_ref, key_ref, value_ref, table_ref, out_ref):
    tokens = query_ref.shape[1]
    half = half_ref[0]
    table = pick_columns(table_ref[pl.ds(COLUMNS, 128), :], half)
    cum_rows = pick_rows(table_ref[pl.ds(CUM_ROWS, 16), :], half)
    mask = table_ref[pl.ds(MASK, 128), :]
    for pair in range(HEAD_TOTAL // 4):
        lanes = pl.ds(pair * LANES, LANES)
        scores = dot(by_head(query_ref[0, :, lanes], 0), key_ref[0, :, lanes], 1, 1)
        weights = (scores * pair_decays(table, cum_rows, mask, pair, tokens)).astype(BF16)
        out_ref[:, lanes] = dot(side_by_side(weights), by_head(value_ref[0, :, lanes], 0))


def forward_kernel(
    half_ref,
    mixed_ref,
    query_ref,
    upstream_ref,
    gain_ref,
    state_ref,
    table_ref,
    before_ref,
    unused_ref,
    layer_ref,
    grad_mixed_ref,
    out_ref,
):
    tokens = query_ref.shape[1]
    half = half_ref[0]
    table = pick_columns(table_ref[pl.ds(COLUMNS, 128), :], half)
    pairs = HEAD_TOTAL // 4
    gains = jnp.where(half == 0, gain_ref[:pairs, :], gain_ref[pairs:, :])
    own = left_lanes((LANES, LANES)) == (lax.broadcasted_iota(jnp.int32, (LANES, LANES), 0) < 64)
    average = twice(jnp.where(own, 1.0 / 64.0, 0.0).astype(BF16), 0)
    gain_parts = []
    for pair in range(pairs):
        lanes = pl.ds(pair * LANES, LANES)
        query = query_ref[0, :, lanes]
        entry = pair_columns(table, HEAD_TOTAL + 2 * pair, tokens)
        state = by_head(state_ref[pl.ds(pair * 64, 64), :], 0)
        mixture = mixed_ref[:, lanes] + entry * dot(twice(query, 1), stacked(state, 0))
        square = dot(stacked(mixture * mixture, 1), average)
        inverse = lax.rsqrt(square + EPSILON)
        normed = mixture * inverse
        gain = gains[pair : pair + 1]
        layer_ref[0, :, lanes] = (normed * gain).astype(BF16)
        upstream = upstream_ref[0, :, lanes].astype(F32)
        gain_parts.append(jnp.sum(upstream * normed, axis=0, keepdims=True))
        grad_normed = upstream * gain
        shared = dot(stacked(grad_normed * normed, 1), average)
        grad_mixed = (inverse * (grad_normed - normed * shared)).astype(BF16)
        grad_mixed_ref[:, lanes] = grad_mixed
        decayed = query.astype(F32) * entry
        out_ref[pl.ds(pair * 64, 64), :] = fold(
            dot(stacked(decayed, 0), twice(grad_mixed, 0), 0, 0)
        )
    part = jnp.concatenate(gain_parts, axis=0)
    blank = jnp.zeros_like(part)
    part = jnp.where(
        half == 0,
        jnp.concatenate([part, blank], axis=0),
        jnp.concatenate([blank, part], axis=0),
    )
    out_ref[pl.ds(pairs * 64, 8), :] = part + before_ref[...]


def backward_kernel(
    half_ref,
    query_ref,
    key_ref,
    value_ref,
    grad_mixed_ref,
    state_ref,
    table_ref,
    unused_ref,
    grad_query_ref,
    grad_key_ref,
    grad_value_ref,
    later_ref,
):
    tokens = query_ref.shape[1]
    half = half_ref[0]
    table = pick_columns(table_ref[pl.ds(COLUMNS, 128), :], half)
    cum_rows = pick_rows(table_ref[pl.ds(CUM_ROWS, 16), :], half)
    mask = table_ref[pl.ds(MASK, 128), :]
    earlier = twice(triangle(tokens, lambda s, t: s < t).astype(F32).astype(BF16), 0)
    reached = triangle(tokens, lambda u, t: u >= t)
    chooser = twice(head_chooser(), 1)
    balance_rows = []
    entry_rows = []
    for pair in range(HEAD_TOTAL // 4):
        lanes = pl.ds(pair * LANES, LANES)
        query = query_ref[0, :, lanes]
        key = key_ref[0, :, lanes]
        value = value_ref[0, :, lanes]
        grad_mixed = grad_mixed_ref[:, lanes]
        query_rows = by_head(query, 0)
        mixed_rows = by_head(grad_mixed, 0)
        decay = pair_decays(table, cum_rows, mask, pair, tokens)
        decayed_scores = dot(query_rows, key, 1, 1) * decay
        grad_pairs = dot(mixed_rows, value, 1, 1)
        weights = decayed_scores.astype(BF16)
        grad_weights = (grad_pairs * decay).astype(BF16)
        entry = pair_columns(table, HEAD_TOTAL + 2 * pair, tokens)
        state = by_head(state_ref[pl.ds(pair * 64, 64), :], 0)
        carried = entry * dot(twice(grad_mixed, 1), stacked(state, 1), 1, 1)
        grad_query_ref[0, :, lanes] = (
            dot(side_by_side(grad_weights), by_head(key, 0)) + carried
        ).astype(BF16)
        grad_key_ref[:, lanes] = dot(grad_weights, query_rows, 0, 0)
        grad_value_ref[:, lanes] = dot(weights, mixed_rows, 0, 0)
        before = dot(stacked(decayed_scores * grad_pairs, 1), earlier)
        for head in range(2):
            part = before[head * tokens : (head + 1) * tokens]
            balance_rows.append(jnp.sum(jnp.where(reached, part, 0.0), axis=0, keepdims=True))
        terms = dot(chooser, stacked(query.astype(F32) * carried, 1), 1, 1)
        entry_rows.append(terms[:2])
    later_ref[...] = jnp.concatenate(balance_rows, axis=0) + row_sums(
        jnp.concatenate(entry_rows, axis=0), reached
    )


def head_chooser():
    rows = lax.broadcasted_iota(jnp.int32, (8, LANES), 0)
    left = left_lanes((8, LANES))
    chosen = ((rows == 0) & left) | ((rows == 1) & ~left)
    return jnp.where(chosen, 1.0, 0.0).astype(BF16)


def row_sums(rows, keep):
    first, second = halves(rows)
    third = (rows - first.astype(F32) - second.astype(F32)).astype(BF16)
    weight = jnp.where(keep, 1.0, 0.0).astype(BF16)
    return dot(
        jnp.concatenate([first, second, third], axis=1),
        jnp.concatenate([weight, weight, weight], axis=0),
    )


def final_kernel(
    half_ref,
    key_ref,
    value_ref,
    grad_key_part_ref,
    grad_value_part_ref,
    later_ref,
    state_ref,
    grad_ref,
    table_ref,
    other_ref,
    unused_key_ref,
    unused_value_ref,
    grad_key_ref,
    grad_value_ref,
    rows_ref,
    decay_ref,
):
    tokens = key_ref.shape[1]
    half = half_ref[0]
    table = pick_columns(table_ref[pl.ds(COLUMNS, 128), :], half)
    carry = pick_rows(table_ref[pl.ds(CARRY_ROWS, 16), :], half)
    chooser = twice(head_chooser(), 1)
    left = left_lanes((1, LANES))
    earlier_rows = []
    through_rows = []
    for pair in range(HEAD_TOTAL // 4):
        lanes = pl.ds(pair * LANES, LANES)
        key = key_ref[0, :, lanes]
        value = value_ref[0, :, lanes]
        leave = pair_columns(table, 2 * HEAD_TOTAL + 2 * pair, tokens)
        packed = grad_ref[pl.ds(pair * 64, 64), :]
        high, low = halves(by_head(packed, 0))
        key_part = leave * dot(twice(value, 1), jnp.concatenate([high, low], axis=1), 1, 1)
        carried = leave * dot(twice(key, 1), jnp.concatenate([high, low], axis=0))
        grad_key_ref[0, :, lanes] = (grad_key_part_ref[:, lanes] + key_part).astype(BF16)
        grad_value_ref[0, :, lanes] = (grad_value_part_ref[:, lanes] + carried).astype(BF16)
        terms = dot(chooser, stacked(carried * value.astype(F32), 1), 1, 1)
        earlier_rows.append(terms[:2])
        product = jnp.sum(packed * state_ref[pl.ds(pair * 64, 64), :], axis=0, keepdims=True)
        for side in (left, ~left):
            through_rows.append(jnp.sum(jnp.where(side, product, 0.0), axis=1, keepdims=True))
    rows = (
        later_ref[...]
        + row_sums(
            jnp.concatenate(earlier_rows, axis=0), triangle(tokens, lambda u, t: u < t)
        )
        + carry * jnp.concatenate(through_rows, axis=0)
    )
    rows_ref[...] = rows
    other = other_ref[...]
    every = jnp.where(
        half == 0,
        jnp.concatenate([rows, other], axis=0),
        jnp.concatenate([other, rows], axis=0),
    )
    square = jnp.concatenate([every, jnp.zeros((LANES - HEAD_TOTAL, LANES), F32)], axis=0)
    decay_ref[0] = jnp.transpose(square)[:, :HEAD_TOTAL]


def call(kernel, half, operands, results, aliases=None, flops=0):
    def spec(shape, kind):
        if kind == "columns":
            return pl.BlockSpec((1, shape[1], shape[2] // 2), lambda i, h: (0, 0, h[0]))
        if kind == "unread":
            return pl.BlockSpec(memory_space=pl.ANY)
        if kind == "top":
            return pl.BlockSpec((8, shape[1]), lambda i, h: (shape[0] // 8 - 1, 0))
        return pl.BlockSpec(shape, lambda i, h: (0,) * len(shape))

    read = sum(a.size * a.dtype.itemsize for a, kind in operands if kind != "unread")
    return pl.pallas_call(
        kernel,
        grid_spec=pltpu.PrefetchScalarGridSpec(
            num_scalar_prefetch=1,
            grid=(1,),
            in_specs=[spec(a.shape, kind) for a, kind in operands],
            out_specs=[spec(shape, kind) for shape, dtype, kind in results],
        ),
        out_shape=[jax.ShapeDtypeStruct(shape, dtype) for shape, dtype, kind in results],
        input_output_aliases=aliases or {},
        compiler_params=pltpu.CompilerParams(vmem_limit_bytes=32 * 1024 * 1024),
        cost_estimate=pl.CostEstimate(flops=flops, bytes_accessed=read, transcendentals=0),
    )(half, *[a for a, kind in operands])


def local(queries, key_vectors, value_vectors, log_decay, restart, norm_gain, upstream):
    tokens, width = queries.shape[1], queries.shape[2]
    pairs = HEAD_TOTAL // 4
    state_rows = pairs * 64
    buffer_rows = state_rows + 8
    blocks = lax.axis_size("seq")
    scans = lax.axis_size("dp")
    position = lax.axis_index("seq")
    core = position & 1
    on_first = core == 0
    own = core.reshape(1).astype(jnp.int32)
    other = 1 - own
    half_width = width // 2

    def exchange(x, bit, axis="seq"):
        size = blocks if axis == "seq" else scans
        return lax.ppermute(x, axis, [(i, i ^ bit) for i in range(size)])

    def parts(buffer):
        state = buffer[:state_rows].reshape(pairs, 64, LANES)
        return state, buffer[state_rows : state_rows + pairs].reshape(pairs, 1, LANES)

    def joined(state, carry):
        return jnp.concatenate(
            [
                state.reshape(state_rows, LANES),
                carry.reshape(pairs, LANES),
                jnp.zeros((8 - pairs, LANES), F32),
            ],
            axis=0,
        )

    def flat(state):
        return state.reshape(state_rows, LANES)

    whole = (1, tokens, width)
    part = (tokens, half_width)
    buffer = (buffer_rows, LANES)

    state_other, tables = call(
        first_state_kernel,
        other,
        [
            (key_vectors, "columns"),
            (value_vectors, "columns"),
            (log_decay, "all"),
            (restart, "all"),
        ],
        [(buffer, F32, "all"), ((TABLE_ROWS, LANES), F32, "all")],
    )
    swapped = exchange(state_other, 1)
    (state_own,) = call(
        second_state_kernel,
        own,
        [(key_vectors, "columns"), (value_vectors, "columns"), (tables, "all")],
        [(buffer, F32, "all")],
    )
    first_state, first_carry = parts(jnp.where(on_first, state_own, swapped))
    second_state, second_carry = parts(jnp.where(on_first, swapped, state_own))
    total = second_carry * first_state + second_state
    carry = first_carry * second_carry
    prefix = jnp.zeros_like(total)
    prefix_carry = jnp.ones_like(carry)
    levels = []
    bit = 2
    while bit < blocks:
        is_upper = (position & bit) != 0
        theirs, their_carry = parts(exchange(joined(total, carry), bit))
        prefix = jnp.where(is_upper, prefix_carry * theirs + prefix, prefix)
        prefix_carry = jnp.where(is_upper, prefix_carry * their_carry, prefix_carry)
        levels.append((bit, is_upper, carry, their_carry))
        total = jnp.where(is_upper, carry * theirs + total, their_carry * total + theirs)
        carry = carry * their_carry
        bit *= 2
    after_first = first_carry * prefix + first_state
    state_in_own = flat(jnp.where(on_first, prefix, after_first))
    state_in_other = exchange(flat(jnp.where(on_first, after_first, prefix)), 1)

    mixed = {}
    for name, half in (("own", own), ("other", other)):
        (mixed[name],) = call(
            mixture_kernel,
            half,
            [
                (queries, "columns"),
                (key_vectors, "columns"),
                (value_vectors, "columns"),
                (tables, "all"),
            ],
            [(part, F32, "all")],
        )

    gain_rows = norm_gain.reshape(2 * pairs, LANES)
    layer_out = None
    results = {}
    before = jnp.zeros((8, LANES), F32)
    for name, half, state_in in (("own", own, state_in_own), ("other", other, state_in_other)):
        operands = [
            (mixed[name], "all"),
            (queries, "columns"),
            (upstream, "columns"),
            (gain_rows, "all"),
            (state_in, "all"),
            (tables, "all"),
            (before, "all" if name == "own" else "top"),
        ]
        if name == "own":
            kernel = lambda *refs: forward_kernel(*refs[:8], None, *refs[8:])
            aliases = None
        else:
            operands.append((layer_out, "unread"))
            kernel = forward_kernel
            aliases = {len(operands): 0}
        layer_out, grad_mixed, query_state = call(
            kernel,
            half,
            operands,
            [(whole, BF16, "columns"), (part, BF16, "all"), (buffer, F32, "all")],
            aliases,
        )
        before = query_state
        results[name] = (grad_mixed, query_state, state_in)

    query_state_own = results["own"][1]
    query_state_other = results["other"][1]
    swapped = exchange(query_state_other, 1)
    first_query, _ = parts(jnp.where(on_first, query_state_own, swapped))
    second_query, _ = parts(jnp.where(on_first, swapped, query_state_own))
    gain = query_state_other[state_rows:] + swapped[state_rows:]
    total = first_query + first_carry * second_query
    suffix = jnp.zeros_like(total)
    suffix_carry = jnp.ones_like(carry)
    for bit, is_upper, carry, their_carry in levels:
        received = exchange(jnp.concatenate([flat(total), gain], axis=0), bit)
        theirs, _ = parts(received)
        gain = gain + received[state_rows:]
        suffix = jnp.where(is_upper, suffix, suffix_carry * theirs + suffix)
        suffix_carry = jnp.where(is_upper, suffix_carry, suffix_carry * their_carry)
        total = jnp.where(is_upper, theirs + their_carry * total, total + carry * theirs)
    before_second = second_query + second_carry * suffix
    state_grad_own = flat(jnp.where(on_first, before_second, suffix))
    state_grad_other = exchange(flat(jnp.where(on_first, suffix, before_second)), 1)
    bit = 1
    while bit < scans:
        gain = gain + sum(exchange(gain, k * bit, "dp") for k in range(1, min(4, scans // bit)))
        bit *= 4

    grad_query = None
    local_parts = {}
    for name, half in (("own", own), ("other", other)):
        grad_mixed, _, state_in = results[name]
        operands = [
            (queries, "columns"),
            (key_vectors, "columns"),
            (value_vectors, "columns"),
            (grad_mixed, "all"),
            (state_in, "all"),
            (tables, "all"),
        ]
        if name == "own":
            kernel = lambda *refs: backward_kernel(*refs[:7], None, *refs[7:])
            aliases = None
        else:
            operands.append((grad_query, "unread"))
            kernel = backward_kernel
            aliases = {len(operands): 0}
        grad_query, *local_parts[name] = call(
            kernel,
            half,
            operands,
            [
                (whole, BF16, "columns"),
                (part, F32, "all"),
                (part, F32, "all"),
                ((HEAD_TOTAL // 2, LANES), F32, "all"),
            ],
            aliases,
        )

    rows = jnp.zeros((HEAD_TOTAL // 2, LANES), F32)
    for name, half, state_grad in (
        ("own", own, state_grad_own),
        ("other", other, state_grad_other),
    ):
        grad_key_part, grad_value_part, later = local_parts[name]
        operands = [
            (key_vectors, "columns"),
            (value_vectors, "columns"),
            (grad_key_part, "all"),
            (grad_value_part, "all"),
            (later, "all"),
            (results[name][2], "all"),
            (state_grad, "all"),
            (tables, "all"),
            (rows, "all"),
        ]
        if name == "own":
            kernel = lambda *refs: final_kernel(*refs[:10], None, None, *refs[10:])
            aliases = None
        else:
            operands += [(grad_key, "unread"), (grad_value, "unread")]
            kernel = final_kernel
            aliases = {len(operands) - 1: 0, len(operands): 1}
        grad_key, grad_value, rows, grad_decay = call(
            kernel,
            half,
            operands,
            [
                (whole, BF16, "columns"),
                (whole, BF16, "columns"),
                ((HEAD_TOTAL // 2, LANES), F32, "all"),
                ((1, tokens, HEAD_TOTAL), F32, "all"),
            ],
            aliases,
        )
    return (layer_out, grad_query, grad_key, grad_value, grad_decay, gain.reshape(-1))


def solution(mesh):
    rows = P("dp", "seq", None)
    return jax.shard_map(
        local,
        mesh=mesh,
        in_specs=(rows, rows, rows, rows, P("dp", "seq"), P(), rows),
        out_specs=(rows, rows, rows, rows, rows, P()),
        check_vma=False,
    )
```

time: 139 us -> 57.6 us (0.41)
  blocking collectives: 55.1 us -> 0 us
  matrix products: 16.2 us -> 0 us
  between operations: 14.9 us -> 0.82 us
  Pallas kernels: 0 us -> 13.6 us
  starting transfers between devices: 0.08 us -> 12.8 us
  waiting for transfers between devices: 31.8 us -> 23.3 us
  other arithmetic: 9.02 us -> 1.07 us
  local copies, waits for them, and re-layouts: 11.4 us -> 5.61 us
    psum x1 -> x0, blocking collectives: 41.6 us -> none  [local(): grad_gain = lax.psum(gain_part.reshape(-1), ('seq', 'dp'))]
    all_gather x2 -> x0, waiting for transfers between devices: 31.7 us -> none  [the longest x1 31.7 us: local(): lax.all_gather(state_part[None], 'seq', axis=0, tiled=True)]
    ppermute x0 -> x11, waiting for transfers between devices: none -> 23.3 us  [exchange(): return lax.ppermute(x, axis, [(i, i ^ bit) for i in range(size)])]
    dot_general x12 -> x0, matrix products: 16.2 us -> none  [the longest x6 10.2 us: blend(): jnp.einsum(pattern, first_operand, second_operand, preferred_element_type...]
    pallas_call x0 -> x10, Pallas kernels: none -> 13.6 us  [call(): pl.pallas_call(kernel, grid_spec=pltpu.PrefetchScalarGridSpec(num_scalar_...]
    all_gather x1 -> x0, blocking collectives: 13.5 us -> none  [local(): every_carry = lax.all_gather(block_carry[None], 'seq', axis=0, tiled=True)]
    ppermute x0 -> x11, starting transfers between devices: none -> 12.8 us  [exchange(): return lax.ppermute(x, axis, [(i, i ^ bit) for i in range(size)])]
    reduce_sum x5 -> x0, other arithmetic: 6.15 us -> none  [the longest x2 5.48 us: weighted_sum(): return jnp.sum(block_weights[..., None, None] * fragment, axis=0)]
  transfers between devices with their start and end apart: 2 -> 11, of which waited for: 1 -> 6; matrix products, arithmetic and copies ran while one was open for 10% -> 1% of each run, Pallas kernels for 0% -> 16%
where the time goes in v1:
time: 57.6 us; the launch traced here: 57.2 us
  waiting for transfers between devices  23.3 us (40%)
  Pallas kernels  13.6 us (24%)
  starting transfers between devices  12.8 us (22%)
  local copies, waits for them, and re-layouts  5.61 us (10%)
  other arithmetic  1.07 us (2%)
  between operations  0.82 us (1%)
    ppermute x11, waiting for transfers between devices, exchange(): return lax.ppermute(x, axis, [(i, i ^ bit) for i in range(size)])  23.3 us
    pallas_call x10, Pallas kernels, call(): pl.pallas_call(kernel, grid_spec=pltpu.PrefetchScalarGridSpec(num_scalar_...  13.6 us
    ppermute x11, starting transfers between devices, exchange(): return lax.ppermute(x, axis, [(i, i ^ bit) for i in range(size)])  12.8 us
    unnamed x18, local copies, waits for them, and re-layouts  5.53 us
  transfers between devices with their start and end apart: 11, of which 6 were waited for; matrix products, arithmetic and copies ran while one was open for 1% of the time, Pallas kernels for 16%

profile of v1, /device:TPU:0, one launch (start us, length us, event | category | flops | bytes accessed | tf_op | source)
XLA Modules:
  0.0 57.2 jit_solution(9145104334884562229)
XLA Ops:
  0.6 0.8 %copy.17.decay_ref = f32[1,128,16]{2,1,0:T(8,128)S(1)} copy(f32[1,128,16]{1,2,0:T(8,128)} %param.10) | data formatting | bytes 16384 | tf_op args[3]
  1.4 0.6 %copy-done.7 = s32[1,128]{1,0:T(1,128)S(1)} copy-done((s32[1,128]{1,0:T(1,128)S(1)}, s32[1,128]{1,0:T(1,128)}, u32[]{:S(2)}) %copy-start.7) | copy-done | bytes 536
  2.1 0.9 %copy-done = bf16[1,128,1024]{2,1,0:T(8,128)(2,1)S(1)} copy-done((bf16[1,128,1024]{2,1,0:T(8,128)(2,1)S(1)}, bf16[1,128,1024]{2,1,0:T(8,128)(2,1)}, u32[]{:S(2)}) %copy-start) | copy-done | bytes 262168
  3.0 0.9 %copy-done.2 = bf16[1,128,1024]{2,1,0:T(8,128)(2,1)S(1)} copy-done((bf16[1,128,1024]{2,1,0:T(8,128)(2,1)S(1)}, bf16[1,128,1024]{2,1,0:T(8,128)(2,1)}, u32[]{:S(2)}) %copy-start.2) | copy-done | bytes 262168
  4.0 0.9 %shard_map.118 = (f32[264,128]{1,0:T(8,128)S(1)}, f32[288,128]{1,0:T(8,128)S(1)}) custom-call(s32[1]{0:T(128)S(6)} %sub.3.half_ref, bf16[1,128,1024]{2,1,0:T(8,128)(2,1)S(1)} %copy-done, bf16[1,128,1024]{2,1,0:T(8,128)(2,1)S(1)} %copy-done.2, f32[1,128,16]{2,1,0:T(8,128)S(1)} %copy.17.decay_ref, s32[1,128]{1,0:T(1,128)S(1)} %copy-done.7), custom_call_target="tpu_custom_call" | custom-call | bytes 532992 | tf_op jit(solution)/shard_map/pallas_call | solution.py:369
  6.5 3.0 %collective-permute-start.1 = (f32[264,128]{1,0:T(8,128)S(1)}, f32[264,128]{1,0:T(8,128)S(1)}, u32[]{:S(2)}, u32[]{:S(2)}) collective-permute-start(f32[264,128]{1,0:T(8,128)S(1)} %maximum_maximum_fusion), channel_id=1, source_target_pairs={{0,8},{4,12},{8,0},{12,4},{16,24},{20,28},{24,16},{28,20},{1,9},{5... | collective-permute-start | bytes 405512 | tf_op jit(solution)/shard_map/ppermute | solution.py:400
  9.5 3.9 %collective-permute-done.1 = f32[264,128]{1,0:T(8,128)S(1)} collective-permute-done((f32[264,128]{1,0:T(8,128)S(1)}, f32[264,128]{1,0:T(8,128)S(1)}, u32[]{:S(2)}, u32[]{:S(2)}) %collective-permute-start.1) | collective-permute-done | bytes 135200 | tf_op jit(solution)/shard_map/ppermute | solution.py:400
  13.6 2.8 %collective-permute-start.2 = (f32[264,128]{1,0:T(8,128)S(1)}, f32[264,128]{1,0:T(8,128)S(1)}, u32[]{:S(2)}, u32[]{:S(2)}) collective-permute-start(f32[264,128]{1,0:T(8,128)S(1)} %maximum_maximum_fusion.1), channel_id=1, source_target_pairs={{0,16},{4,20},{8,24},{12,28},{16,0},{20,4},{24,8},{28,12},{1,17},{... | collective-permute-start | bytes 405512 | tf_op jit(solution)/shard_map/ppermute | solution.py:400
  16.4 6.2 %collective-permute-done.2 = f32[264,128]{1,0:T(8,128)S(1)} collective-permute-done((f32[264,128]{1,0:T(8,128)S(1)}, f32[264,128]{1,0:T(8,128)S(1)}, u32[]{:S(2)}, u32[]{:S(2)}) %collective-permute-start.2) | collective-permute-done | bytes 135200 | tf_op jit(solution)/shard_map/ppermute | solution.py:400
  22.7 0.8 %copy-done.4 = bf16[1,128,1024]{2,1,0:T(8,128)(2,1)S(1)} copy-done((bf16[1,128,1024]{2,1,0:T(8,128)(2,1)S(1)}, bf16[1,128,1024]{2,1,0:T(8,128)(2,1)}, u32[]{:S(2)}) %copy-start.4) | copy-done | bytes 262168
  25.4 2.0 %shard_map.122 = (bf16[1,128,1024]{2,1,0:T(8,128)(2,1)}, bf16[128,512]{1,0:T(8,128)(2,1)S(1)}, f32[264,128]{1,0:T(8,128)S(1)}) custom-call(s32[1]{0:T(128)} %bitcast.half_ref.refs_0_, f32[128,512]{1,0:T(8,128)S(1)} %shard_map.121.refs_1_, bf16[1,128,1024]{2,1,0:T(8,128)(2,1)S(1)} %copy-done.4, bf16[1,128,1024]{2,1,0:T(8,128)(2,1)S(1)} %copy-done.5, ...), custom_call_target="tpu_custom_call" | custom-call | bytes 1073152 | tf_op jit(solution)/shard_map/pallas_call | solution.py:369
  27.4 2.0 %shard_map.123 = (bf16[1,128,1024]{2,1,0:T(8,128)(2,1)}, bf16[128,512]{1,0:T(8,128)(2,1)S(1)}, f32[264,128]{1,0:T(8,128)S(1)}) custom-call(s32[1]{0:T(128)S(6)} %sub.3.half_ref, f32[128,512]{1,0:T(8,128)S(1)} %shard_map.119.mixed_ref, bf16[1,128,1024]{2,1,0:T(8,128)(2,1)S(1)} %copy-done.4, ...), custom_call_target="tpu_custom_call", output_to_operand_aliasing={{0}: (8, {})} | custom-call | bytes 1204224 | tf_op jit(solution)/shard_map/pallas_call | solution.py:369
  29.3 1.4 %collective-permute-done.4 = f32[264,128]{1,0:T(8,128)S(1)} collective-permute-done((f32[264,128]{1,0:T(8,128)S(1)}, f32[264,128]{1,0:T(8,128)S(1)}, u32[]{:S(2)}, u32[]{:S(2)}) %collective-permute-start.4) | collective-permute-done | bytes 135200 | tf_op jit(solution)/shard_map/ppermute | solution.py:400
  31.3 5.1 %collective-permute-done.5 = f32[264,128]{1,0:T(8,128)S(1)} collective-permute-done((f32[264,128]{1,0:T(8,128)S(1)}, f32[264,128]{1,0:T(8,128)S(1)}, u32[]{:S(2)}, u32[]{:S(2)}) %collective-permute-start.5) | collective-permute-done | bytes 135200 | tf_op jit(solution)/shard_map/ppermute | solution.py:400
  36.5 2.2 %collective-permute-start.6 = (f32[264,128]{1,0:T(8,128)S(1)}, f32[264,128]{1,0:T(8,128)S(1)}, u32[]{:S(2)}, u32[]{:S(2)}) collective-permute-start(f32[264,128]{1,0:T(8,128)S(1)} %pad_maximum_fusion.1), channel_id=1, source_target_pairs={{0,16},{4,20},{8,24},{12,28},{16,0},{20,4},{24,8},{28,12},{1,17},{... | collective-permute-start | bytes 405512 | tf_op jit(solution)/shard_map/ppermute | solution.py:400
  38.7 6.4 %collective-permute-done.6 = f32[264,128]{1,0:T(8,128)S(1)} collective-permute-done((f32[264,128]{1,0:T(8,128)S(1)}, f32[264,128]{1,0:T(8,128)S(1)}, u32[]{:S(2)}, u32[]{:S(2)}) %collective-permute-start.6) | collective-permute-done | bytes 135200 | tf_op jit(solution)/shard_map/ppermute | solution.py:400
  45.2 2.3 %collective-permute-start.10 = (f32[8,128]{1,0:T(8,128)S(1)}, f32[8,128]{1,0:T(8,128)S(1)}, u32[]{:S(2)}, u32[]{:S(2)}) collective-permute-start(f32[8,128]{1,0:T(8,128)S(1)} %slice_add_fusion), channel_id=1, source_target_pairs={{0,3},{1,2},{2,1},{3,0},{4,7},{5,6},{6,5},{7,4},{8,11},{9,10},{10,... | collective-permute-start | bytes 12296 | tf_op jit(solution)/shard_map/ppermute | solution.py:400
  48.0 0.7 %collective-permute-start.8 = (f32[8,128]{1,0:T(8,128)S(1)}, f32[8,128]{1,0:T(8,128)S(1)}, u32[]{:S(2)}, u32[]{:S(2)}) collective-permute-start(f32[8,128]{1,0:T(8,128)S(1)} %slice_add_fusion), channel_id=1, source_target_pairs={{0,1},{1,0},{2,3},{3,2},{4,5},{5,4},{6,7},{7,6},{8,9},{9,8},{10,11... | collective-permute-start | bytes 12296 | tf_op jit(solution)/shard_map/ppermute | solution.py:400
  48.7 1.9 %shard_map.124 = (bf16[1,128,1024]{2,1,0:T(8,128)(2,1)}, f32[128,512]{1,0:T(8,128)S(1)}, f32[128,512]{1,0:T(8,128)S(1)}, f32[8,128]{1,0:T(8,128)S(1)}) custom-call(s32[1]{0:T(128)} %bitcast.half_ref.refs_0_, bf16[1,128,1024]{2,1,0:T(8,128)(2,1)S(1)} %copy-done.4, bf16[1,128,1024]{2,1,0:T(8,128)(2,1)S(1)} %copy-done.1, bf16[1,128,1024]{2,1,0:T(8,128)(2,1)S(1)} %copy-done.3, ...), custom_call_target="tpu_custom_call" | custom-call | bytes 1196032 | tf_op jit(solution)/shard_map/pallas_call | solution.py:369
  50.6 1.9 %shard_map.125 = (bf16[1,128,1024]{2,1,0:T(8,128)(2,1)}, f32[128,512]{1,0:T(8,128)S(1)}, f32[128,512]{1,0:T(8,128)S(1)}, f32[8,128]{1,0:T(8,128)S(1)}) custom-call(s32[1]{0:T(128)S(6)} %sub.3.half_ref, bf16[1,128,1024]{2,1,0:T(8,128)(2,1)S(1)} %copy-done.4, bf16[1,128,1024]{2,1,0:T(8,128)(2,1)S(1)} %copy-done.1, ...), custom_call_target="tpu_custom_call", output_to_operand_aliasing={{0}: (7, {})} | custom-call | bytes 1196032 | tf_op jit(solution)/shard_map/pallas_call | solution.py:369
  52.7 1.7 %shard_map.126 = (bf16[1,128,1024]{2,1,0:T(8,128)(2,1)}, bf16[1,128,1024]{2,1,0:T(8,128)(2,1)}, f32[8,128]{1,0:T(8,128)S(1)}, f32[1,128,16]{2,1,0:T(8,128)}) custom-call(s32[1]{0:T(128)} %bitcast.half_ref.refs_0_, bf16[1,128,1024]{2,1,0:T(8,128)(2,1)S(1)} %copy-done.1, bf16[1,128,1024]{2,1,0:T(8,128)(2,1)S(1)} %copy-done.3, ...), custom_call_target="tpu_custom_call" | custom-call | bytes 1466368 | tf_op jit(solution)/shard_map/pallas_call | solution.py:369
  54.4 0.6 %add_bitcast_fusion = f32[1024]{0:T(1024)} fusion(f32[8,128]{1,0:T(8,128)S(1)} %slice_add_fusion, f32[8,128]{1,0:T(8,128)S(1)} %collective-permute-done.10, f32[8,128]{1,0:T(8,128)S(1)} %collective-permute-done.8, f32[8,128]{1,0:T(8,128)S(1)} %collective-permute-done.9), kind=kLoop, calls=%fused_computation.36 | loop fusion | flops 3072 | bytes 20480 | tf_op jit(solution)/shard_map/reshape | solution.py:599
  55.0 1.6 %shard_map.127 = (bf16[1,128,1024]{2,1,0:T(8,128)(2,1)}, bf16[1,128,1024]{2,1,0:T(8,128)(2,1)}, f32[8,128]{1,0:T(8,128)}, f32[1,128,16]{2,1,0:T(8,128)S(1)}) custom-call(s32[1]{0:T(128)S(6)} %sub.3.half_ref, bf16[1,128,1024]{2,1,0:T(8,128)(2,1)S(1)} %copy-done.1, ...), custom_call_target="tpu_custom_call", output_to_operand_aliasing={{0}: (10, {}), {1}: (11, {})} | custom-call | bytes 1466368 | tf_op jit(solution)/shard_map/pallas_call | solution.py:369
  56.6 0.7 %copy.18 = f32[1,128,16]{1,2,0:T(8,128)} copy(f32[1,128,16]{2,1,0:T(8,128)S(1)} %get-tuple-element.54) | data formatting | bytes 16384
  (46 shorter events, 5.1 us)
Async XLA Ops:
  1.4 0.7 %copy-start.7 = (s32[1,128]{1,0:T(1,128)S(1)}, s32[1,128]{1,0:T(1,128)}, u32[]{:S(2)}) copy-start(s32[1,128]{1,0:T(1,128)} %restart_ref.1) | copy-start | bytes 1540
  2.1 0.9 %copy-start = (bf16[1,128,1024]{2,1,0:T(8,128)(2,1)S(1)}, bf16[1,128,1024]{2,1,0:T(8,128)(2,1)}, u32[]{:S(2)}) copy-start(bf16[1,128,1024]{2,1,0:T(8,128)(2,1)} %key_ref.11) | copy-start | bytes 786436
  3.0 0.9 %copy-start.2 = (bf16[1,128,1024]{2,1,0:T(8,128)(2,1)S(1)}, bf16[1,128,1024]{2,1,0:T(8,128)(2,1)}, u32[]{:S(2)}) copy-start(bf16[1,128,1024]{2,1,0:T(8,128)(2,1)} %value_ref.11) | copy-start | bytes 786436
  4.0 1.4 %copy-start.1 = (bf16[1,128,1024]{2,1,0:T(8,128)(2,1)S(1)}, bf16[1,128,1024]{2,1,0:T(8,128)(2,1)}, u32[]{:S(2)}) copy-start(bf16[1,128,1024]{2,1,0:T(8,128)(2,1)} %key_ref.11) | copy-start | bytes 786436
  4.0 1.4 %copy-start.3 = (bf16[1,128,1024]{2,1,0:T(8,128)(2,1)S(1)}, bf16[1,128,1024]{2,1,0:T(8,128)(2,1)}, u32[]{:S(2)}) copy-start(bf16[1,128,1024]{2,1,0:T(8,128)(2,1)} %value_ref.11) | copy-start | bytes 786436
  4.9 1.5 %collective-permute-start = (f32[264,128]{1,0:T(8,128)S(1)}, f32[264,128]{1,0:T(8,128)S(1)}, u32[]{:S(2)}, u32[]{:S(2)}) collective-permute-start(f32[264,128]{1,0:T(8,128)S(1)} %get-tuple-element.29), channel_id=1, source_target_pairs={{0,4},{4,0},{8,12},{12,8},{16,20},{20,16},{24,28},{28,24},{1,5},{5... | collective-permute-start | bytes 405512 | tf_op jit(solution)/shard_map/ppermute | solution.py:400
  6.5 6.9 %collective-permute-start.1 = (f32[264,128]{1,0:T(8,128)S(1)}, f32[264,128]{1,0:T(8,128)S(1)}, u32[]{:S(2)}, u32[]{:S(2)}) collective-permute-start(f32[264,128]{1,0:T(8,128)S(1)} %maximum_maximum_fusion), channel_id=1, source_target_pairs={{0,8},{4,12},{8,0},{12,4},{16,24},{20,28},{24,16},{28,20},{1,9},{5... | collective-permute-start | bytes 405512 | tf_op jit(solution)/shard_map/ppermute | solution.py:400
  13.6 9.0 %collective-permute-start.2 = (f32[264,128]{1,0:T(8,128)S(1)}, f32[264,128]{1,0:T(8,128)S(1)}, u32[]{:S(2)}, u32[]{:S(2)}) collective-permute-start(f32[264,128]{1,0:T(8,128)S(1)} %maximum_maximum_fusion.1), channel_id=1, source_target_pairs={{0,16},{4,20},{8,24},{12,28},{16,0},{20,4},{24,8},{28,12},{1,17},{... | collective-permute-start | bytes 405512 | tf_op jit(solution)/shard_map/ppermute | solution.py:400
  22.6 1.0 %copy-start.4 = (bf16[1,128,1024]{2,1,0:T(8,128)(2,1)S(1)}, bf16[1,128,1024]{2,1,0:T(8,128)(2,1)}, u32[]{:S(2)}) copy-start(bf16[1,128,1024]{2,1,0:T(8,128)(2,1)} %query_ref.7) | copy-start | bytes 786436
  22.6 4.7 %collective-permute-start.3 = (f32[256,128]{1,0:T(8,128)S(1)}, f32[256,128]{1,0:T(8,128)S(1)}, u32[]{:S(2)}, u32[]{:S(2)}) collective-permute-start(f32[256,128]{1,0:T(8,128)S(1)} %get-tuple-element.59), channel_id=1, source_target_pairs={{0,4},{4,0},{8,12},{12,8},{16,20},{20,16},{24,28},{28,24},{1,5},{5... | collective-permute-start | bytes 393224 | tf_op jit(solution)/shard_map/ppermute | solution.py:400
  24.1 1.0 %copy-start.5 = (bf16[1,128,1024]{2,1,0:T(8,128)(2,1)S(1)}, bf16[1,128,1024]{2,1,0:T(8,128)(2,1)}, u32[]{:S(2)}) copy-start(bf16[1,128,1024]{2,1,0:T(8,128)(2,1)} %upstream_ref.1) | copy-start | bytes 786436
  24.7 0.7 %copy-start.6 = (f32[1024]{0:T(1024)S(1)}, f32[1024]{0:T(1024)}, u32[]{:S(2)}) copy-start(f32[1024]{0:T(1024)} %param.12) | copy-start | bytes 12292
  29.3 1.4 %collective-permute-start.4 = (f32[264,128]{1,0:T(8,128)S(1)}, f32[264,128]{1,0:T(8,128)S(1)}, u32[]{:S(2)}, u32[]{:S(2)}) collective-permute-start(f32[264,128]{1,0:T(8,128)S(1)} %get-tuple-element.40), channel_id=1, source_target_pairs={{0,4},{4,0},{8,12},{12,8},{16,20},{20,16},{24,28},{28,24},{1,5},{5... | collective-permute-start | bytes 405512 | tf_op jit(solution)/shard_map/ppermute | solution.py:400
  30.7 5.7 %collective-permute-start.5 = (f32[264,128]{1,0:T(8,128)S(1)}, f32[264,128]{1,0:T(8,128)S(1)}, u32[]{:S(2)}, u32[]{:S(2)}) collective-permute-start(f32[264,128]{1,0:T(8,128)S(1)} %pad_maximum_fusion), channel_id=1, source_target_pairs={{0,8},{4,12},{8,0},{12,4},{16,24},{20,28},{24,16},{28,20},{1,9},{5... | collective-permute-start | bytes 405512 | tf_op jit(solution)/shard_map/ppermute | solution.py:400
  36.5 8.7 %collective-permute-start.6 = (f32[264,128]{1,0:T(8,128)S(1)}, f32[264,128]{1,0:T(8,128)S(1)}, u32[]{:S(2)}, u32[]{:S(2)}) collective-permute-start(f32[264,128]{1,0:T(8,128)S(1)} %pad_maximum_fusion.1), channel_id=1, source_target_pairs={{0,16},{4,20},{8,24},{12,28},{16,0},{20,4},{24,8},{28,12},{1,17},{... | collective-permute-start | bytes 405512 | tf_op jit(solution)/shard_map/ppermute | solution.py:400
  45.2 9.2 %collective-permute-start.10 = (f32[8,128]{1,0:T(8,128)S(1)}, f32[8,128]{1,0:T(8,128)S(1)}, u32[]{:S(2)}, u32[]{:S(2)}) collective-permute-start(f32[8,128]{1,0:T(8,128)S(1)} %slice_add_fusion), channel_id=1, source_target_pairs={{0,3},{1,2},{2,1},{3,0},{4,7},{5,6},{6,5},{7,4},{8,11},{9,10},{10,... | collective-permute-start | bytes 12296 | tf_op jit(solution)/shard_map/ppermute | solution.py:400
  47.5 6.9 %collective-permute-start.9 = (f32[8,128]{1,0:T(8,128)S(1)}, f32[8,128]{1,0:T(8,128)S(1)}, u32[]{:S(2)}, u32[]{:S(2)}) collective-permute-start(f32[8,128]{1,0:T(8,128)S(1)} %slice_add_fusion), channel_id=1, source_target_pairs={{0,2},{1,3},{2,0},{3,1},{4,6},{5,7},{6,4},{7,5},{8,10},{9,11},{10,... | collective-permute-start | bytes 12296 | tf_op jit(solution)/shard_map/ppermute | solution.py:400
  48.0 6.4 %collective-permute-start.8 = (f32[8,128]{1,0:T(8,128)S(1)}, f32[8,128]{1,0:T(8,128)S(1)}, u32[]{:S(2)}, u32[]{:S(2)}) collective-permute-start(f32[8,128]{1,0:T(8,128)S(1)} %slice_add_fusion), channel_id=1, source_target_pairs={{0,1},{1,0},{2,3},{3,2},{4,5},{5,4},{6,7},{7,6},{8,9},{9,8},{10,11... | collective-permute-start | bytes 12296 | tf_op jit(solution)/shard_map/ppermute | solution.py:400
  52.6 2.4 %collective-permute-start.7 = (f32[256,128]{1,0:T(8,128)S(1)}, f32[256,128]{1,0:T(8,128)S(1)}, u32[]{:S(2)}, u32[]{:S(2)}) collective-permute-start(f32[256,128]{1,0:T(8,128)S(1)} %get-tuple-element.57), channel_id=1, source_target_pairs={{0,4},{4,0},{8,12},{12,8},{16,20},{20,16},{24,28},{28,24},{1,5},{5... | collective-permute-start | bytes 393224 | tf_op jit(solution)/shard_map/ppermute | solution.py:400

commit v2 on v1

--- a/solution.py
+++ b/solution.py
@@ -63,22 +63,16 @@
     )
 
 
-def make_tables(log_decay, restart):
-    tokens = log_decay.shape[0]
-    heads = log_decay.shape[1]
+def make_tables(decay_rows, restart):
+    heads, tokens = decay_rows.shape
     lower = triangle(tokens, lambda t, s: s <= t).astype(F32).astype(BF16)
     upper = triangle(tokens, lambda t, s: t <= s).astype(F32).astype(BF16)
     marks = jnp.broadcast_to(restart.astype(F32), (tokens, tokens)).astype(BF16)
     resets_column = dot(lower, marks, 1, 1)
     resets_row = dot(marks, upper)
-    padded = jnp.concatenate(
-        [log_decay, jnp.zeros((tokens, LANES - heads), F32)], axis=1
-    )
-    first, rest = halves(padded)
-    third = (padded - first.astype(F32) - rest.astype(F32)).astype(BF16)
-    cum = dot(
-        jnp.concatenate([lower, lower, lower], axis=1),
-        jnp.concatenate([first, rest, third], axis=0),
+    cum_rows = row_sums(decay_rows, triangle(tokens, lambda s, t: s <= t))
+    cum = jnp.transpose(
+        jnp.concatenate([cum_rows, jnp.zeros((LANES - heads, tokens), F32)], axis=0)
     )
     last = cum[tokens - 1 :, :]
     last_reset = resets_column[tokens - 1 :, :]
@@ -92,7 +86,6 @@
     )
     allowed = triangle(tokens, lambda t, s: t >= s) & (resets_column == resets_row)
     mask = jnp.where(allowed, 0.0, -1e30)
-    cum_rows = jnp.transpose(cum)[:heads]
     carry = jnp.where(last_reset[:, :1] == 0.0, jnp.exp(cum_rows[:, tokens - 1 :]), 0.0)
     return columns, mask, cum_rows, jnp.broadcast_to(carry, (heads, LANES))
 
@@ -351,8 +344,7 @@
         jnp.concatenate([rows, other], axis=0),
         jnp.concatenate([other, rows], axis=0),
     )
-    square = jnp.concatenate([every, jnp.zeros((LANES - HEAD_TOTAL, LANES), F32)], axis=0)
-    decay_ref[0] = jnp.transpose(square)[:, :HEAD_TOTAL]
+    decay_ref[0] = every
 
 
 def call(kernel, half, operands, results, aliases=None, flops=0):
@@ -401,6 +393,8 @@
 
     def parts(buffer):
         state = buffer[:state_rows].reshape(pairs, 64, LANES)
+        if buffer.shape[0] == state_rows:
+            return state, None
         return state, buffer[state_rows : state_rows + pairs].reshape(pairs, 1, LANES)
 
     def joined(state, carry):
@@ -426,7 +420,7 @@
         [
             (key_vectors, "columns"),
             (value_vectors, "columns"),
-            (log_decay, "all"),
+            (jnp.swapaxes(log_decay, 1, 2), "all"),
             (restart, "all"),
         ],
         [(buffer, F32, "all"), ((TABLE_ROWS, LANES), F32, "all")],
@@ -448,7 +442,7 @@
     bit = 2
     while bit < blocks:
         is_upper = (position & bit) != 0
-        theirs, their_carry = parts(exchange(joined(total, carry), bit))
+        theirs, their_carry = parts(exchange(joined(total, carry), 2 * bit - 2))
         prefix = jnp.where(is_upper, prefix_carry * theirs + prefix, prefix)
         prefix_carry = jnp.where(is_upper, prefix_carry * their_carry, prefix_carry)
         levels.append((bit, is_upper, carry, their_carry))
@@ -471,6 +465,7 @@
                 (tables, "all"),
             ],
             [(part, F32, "all")],
+            flops=1_000_000_000,
         )
 
     gain_rows = norm_gain.reshape(2 * pairs, LANES)
@@ -514,20 +509,29 @@
     suffix = jnp.zeros_like(total)
     suffix_carry = jnp.ones_like(carry)
     for bit, is_upper, carry, their_carry in levels:
-        received = exchange(jnp.concatenate([flat(total), gain], axis=0), bit)
-        theirs, _ = parts(received)
-        gain = gain + received[state_rows:]
+        partner = 2 * bit - 2
+        if bit == 2:
+            theirs = parts(exchange(flat(total), partner))[0]
+            step = 1
+            while step < scans:
+                gain = gain + sum(
+                    exchange(gain, k * step, "dp") for k in range(1, min(4, scans // step))
+                )
+                step *= 4
+            if len(levels) == 1:
+                gain = gain + exchange(gain, partner)
+        else:
+            received = exchange(jnp.concatenate([flat(total), gain], axis=0), partner)
+            theirs = parts(received)[0]
+            if 2 * bit == blocks:
+                gain = gain + exchange(gain, 2) + exchange(gain, partner ^ 2)
+            gain = gain + received[state_rows:]
         suffix = jnp.where(is_upper, suffix, suffix_carry * theirs + suffix)
         suffix_carry = jnp.where(is_upper, suffix_carry, suffix_carry * their_carry)
         total = jnp.where(is_upper, theirs + their_carry * total, total + carry * theirs)
     before_second = second_query + second_carry * suffix
     state_grad_own = flat(jnp.where(on_first, before_second, suffix))
     state_grad_other = exchange(flat(jnp.where(on_first, suffix, before_second)), 1)
-    bit = 1
-    while bit < scans:
-        gain = gain + sum(exchange(gain, k * bit, "dp") for k in range(1, min(4, scans // bit)))
-        bit *= 4
-
     grad_query = None
     local_parts = {}
     for name, half in (("own", own), ("other", other)):
@@ -558,6 +562,7 @@
                 ((HEAD_TOTAL // 2, LANES), F32, "all"),
             ],
             aliases,
+            flops=2_000_000_000,
         )
 
     rows = jnp.zeros((HEAD_TOTAL // 2, LANES), F32)
@@ -592,10 +597,11 @@
                 (whole, BF16, "columns"),
                 (whole, BF16, "columns"),
                 ((HEAD_TOTAL // 2, LANES), F32, "all"),
-                ((1, tokens, HEAD_TOTAL), F32, "all"),
+                ((1, HEAD_TOTAL, tokens), F32, "all"),
             ],
             aliases,
         )
+    grad_decay = jnp.swapaxes(grad_decay, 1, 2)
     return (layer_out, grad_query, grad_key, grad_value, grad_decay, gain.reshape(-1))
 
 

time: 57.6 us -> 50.6 us (0.88)
  waiting for transfers between devices: 23.3 us -> 10.9 us
  starting transfers between devices: 12.8 us -> 19.7 us
  local copies, waits for them, and re-layouts: 5.61 us -> 4.18 us
    ppermute x11 -> x13, waiting for transfers between devices: 23.3 us -> 10.9 us  [exchange(): return lax.ppermute(x, axis, [(i, i ^ bit) for i in range(size)])]
    ppermute x11 -> x13, starting transfers between devices: 12.8 us -> 19.7 us  [exchange(): return lax.ppermute(x, axis, [(i, i ^ bit) for i in range(size)])]
    unnamed x18, local copies, waits for them, and re-layouts: 5.53 us -> 4.1 us
  transfers between devices with their start and end apart: 11 -> 13, of which waited for: 6 -> 5; matrix products, arithmetic and copies ran while one was open for 1% -> 2% of each run, Pallas kernels for 16% -> 18%
where the time goes in v2:
time: 50.6 us; the launch traced here: 50.3 us
  starting transfers between devices  19.7 us (39%)
  Pallas kernels  13.6 us (27%)
  waiting for transfers between devices  10.9 us (22%)
  local copies, waits for them, and re-layouts  4.18 us (8%)
  other arithmetic  1.07 us (2%)
  between operations  0.81 us (2%)
    ppermute x13, starting transfers between devices, exchange(): return lax.ppermute(x, axis, [(i, i ^ bit) for i in range(size)])  19.7 us
    pallas_call x10, Pallas kernels, call(): pl.pallas_call(kernel, grid_spec=pltpu.PrefetchScalarGridSpec(num_scalar_...  13.6 us
    ppermute x13, waiting for transfers between devices, exchange(): return lax.ppermute(x, axis, [(i, i ^ bit) for i in range(size)])  10.9 us
    unnamed x18, local copies, waits for them, and re-layouts  4.1 us
  transfers between devices with their start and end apart: 13, of which 5 were waited for; matrix products, arithmetic and copies ran while one was open for 2% of the time, Pallas kernels for 18%

profile of v2, /device:TPU:0, one launch (start us, length us, event | category | flops | bytes accessed | tf_op | source)
XLA Modules:
  0.0 50.3 jit_solution(13272102909755447452)
XLA Ops:
  0.7 0.7 %copy-done.7 = f32[1,128,16]{1,2,0:T(8,128)S(1)} copy-done((f32[1,128,16]{1,2,0:T(8,128)S(1)}, f32[1,128,16]{1,2,0:T(8,128)}, u32[]{:S(2)}) %copy-start.7) | copy-done | bytes 8216
  1.3 0.9 %copy-done = bf16[1,128,1024]{2,1,0:T(8,128)(2,1)S(1)} copy-done((bf16[1,128,1024]{2,1,0:T(8,128)(2,1)S(1)}, bf16[1,128,1024]{2,1,0:T(8,128)(2,1)}, u32[]{:S(2)}) %copy-start) | copy-done | bytes 262168
  2.3 0.9 %copy-done.2 = bf16[1,128,1024]{2,1,0:T(8,128)(2,1)S(1)} copy-done((bf16[1,128,1024]{2,1,0:T(8,128)(2,1)S(1)}, bf16[1,128,1024]{2,1,0:T(8,128)(2,1)}, u32[]{:S(2)}) %copy-start.2) | copy-done | bytes 262168
  3.2 0.9 %shard_map.118 = (f32[264,128]{1,0:T(8,128)S(1)}, f32[288,128]{1,0:T(8,128)S(1)}) custom-call(s32[1]{0:T(128)S(6)} %sub.3.half_ref, bf16[1,128,1024]{2,1,0:T(8,128)(2,1)S(1)} %copy-done, bf16[1,128,1024]{2,1,0:T(8,128)(2,1)S(1)} %copy-done.2, f32[1,16,128]{2,1,0:T(8,128)S(1)} %bitcast.64, s32[1,128]{1,0:T(1,128)S(1)} %copy-done.8), custom_call_target="tpu_custom_call" | custom-call | bytes 532992 | tf_op jit(solution)/shard_map/pallas_call | solution.py:361
  4.7 0.6 %shard_map.120 = f32[264,128]{1,0:T(8,128)S(1)} custom-call(s32[1]{0:T(128)} %bitcast.half_ref.refs_0_, bf16[1,128,1024]{2,1,0:T(8,128)(2,1)S(1)} %copy-done.1, bf16[1,128,1024]{2,1,0:T(8,128)(2,1)S(1)} %copy-done.3, f32[288,128]{1,0:T(8,128)S(1)} %get-tuple-element.28.table_ref.refs_6_.refs_8_), custom_call_target="tpu_custom_call" | custom-call | bytes 671744 | tf_op jit(solution)/shard_map/pallas_call | solution.py:361
  5.8 3.0 %collective-permute-start.1 = (f32[264,128]{1,0:T(8,128)S(1)}, f32[264,128]{1,0:T(8,128)S(1)}, u32[]{:S(2)}, u32[]{:S(2)}) collective-permute-start(f32[264,128]{1,0:T(8,128)S(1)} %maximum_maximum_fusion), channel_id=1, source_target_pairs={{0,8},{4,12},{8,0},{12,4},{16,24},{20,28},{24,16},{28,20},{1,9},{5... | collective-permute-start | bytes 405512 | tf_op jit(solution)/shard_map/ppermute | solution.py:392
  8.8 3.9 %collective-permute-done.1 = f32[264,128]{1,0:T(8,128)S(1)} collective-permute-done((f32[264,128]{1,0:T(8,128)S(1)}, f32[264,128]{1,0:T(8,128)S(1)}, u32[]{:S(2)}, u32[]{:S(2)}) %collective-permute-start.1) | collective-permute-done | bytes 135200 | tf_op jit(solution)/shard_map/ppermute | solution.py:392
  12.9 3.8 %collective-permute-start.2 = (f32[264,128]{1,0:T(8,128)S(1)}, f32[264,128]{1,0:T(8,128)S(1)}, u32[]{:S(2)}, u32[]{:S(2)}) collective-permute-start(f32[264,128]{1,0:T(8,128)S(1)} %maximum_maximum_fusion.1), channel_id=1, source_target_pairs={{0,24},{4,28},{8,16},{12,20},{16,8},{20,12},{24,0},{28,4},{1,25},{... | collective-permute-start | bytes 405512 | tf_op jit(solution)/shard_map/ppermute | solution.py:392
  16.7 3.3 %collective-permute-done.2 = f32[264,128]{1,0:T(8,128)S(1)} collective-permute-done((f32[264,128]{1,0:T(8,128)S(1)}, f32[264,128]{1,0:T(8,128)S(1)}, u32[]{:S(2)}, u32[]{:S(2)}) %collective-permute-start.2) | collective-permute-done | bytes 135200 | tf_op jit(solution)/shard_map/ppermute | solution.py:392
  20.1 0.8 %copy-done.5 = bf16[1,128,1024]{2,1,0:T(8,128)(2,1)S(1)} copy-done((bf16[1,128,1024]{2,1,0:T(8,128)(2,1)S(1)}, bf16[1,128,1024]{2,1,0:T(8,128)(2,1)}, u32[]{:S(2)}) %copy-start.5) | copy-done | bytes 262168
  22.8 2.0 %shard_map.122 = (bf16[1,128,1024]{2,1,0:T(8,128)(2,1)}, bf16[128,512]{1,0:T(8,128)(2,1)S(1)}, f32[264,128]{1,0:T(8,128)S(1)}) custom-call(s32[1]{0:T(128)} %bitcast.half_ref.refs_0_, f32[128,512]{1,0:T(8,128)S(1)} %shard_map.121.refs_1_, bf16[1,128,1024]{2,1,0:T(8,128)(2,1)S(1)} %copy-done.5, bf16[1,128,1024]{2,1,0:T(8,128)(2,1)S(1)} %copy-done.4, ...), custom_call_target="tpu_custom_call" | custom-call | bytes 1073152 | tf_op jit(solution)/shard_map/pallas_call | solution.py:361
  24.7 2.0 %shard_map.123 = (bf16[1,128,1024]{2,1,0:T(8,128)(2,1)}, bf16[128,512]{1,0:T(8,128)(2,1)S(1)}, f32[264,128]{1,0:T(8,128)S(1)}) custom-call(s32[1]{0:T(128)S(6)} %sub.3.half_ref, f32[128,512]{1,0:T(8,128)S(1)} %shard_map.119.mixed_ref, bf16[1,128,1024]{2,1,0:T(8,128)(2,1)S(1)} %copy-done.5, ...), custom_call_target="tpu_custom_call", output_to_operand_aliasing={{0}: (8, {})} | custom-call | bytes 1204224 | tf_op jit(solution)/shard_map/pallas_call | solution.py:361
  26.7 1.4 %collective-permute-done.4 = f32[264,128]{1,0:T(8,128)S(1)} collective-permute-done((f32[264,128]{1,0:T(8,128)S(1)}, f32[264,128]{1,0:T(8,128)S(1)}, u32[]{:S(2)}, u32[]{:S(2)}) %collective-permute-start.4) | collective-permute-done | bytes 135200 | tf_op jit(solution)/shard_map/ppermute | solution.py:392
  28.1 2.4 %collective-permute-start.8 = (f32[8,128]{1,0:T(8,128)S(1)}, f32[8,128]{1,0:T(8,128)S(1)}, u32[]{:S(2)}, u32[]{:S(2)}) collective-permute-start(f32[8,128]{1,0:T(8,128)S(1)} %slice_add_fusion.1), channel_id=1, source_target_pairs={{0,3},{1,2},{2,1},{3,0},{4,7},{5,6},{6,5},{7,4},{8,11},{9,10},{10,... | collective-permute-start | bytes 12296 | tf_op jit(solution)/shard_map/ppermute | solution.py:392
  31.5 1.9 %shard_map.124 = (bf16[1,128,1024]{2,1,0:T(8,128)(2,1)}, f32[128,512]{1,0:T(8,128)S(1)}, f32[128,512]{1,0:T(8,128)S(1)}, f32[8,128]{1,0:T(8,128)S(1)}) custom-call(s32[1]{0:T(128)} %bitcast.half_ref.refs_0_, bf16[1,128,1024]{2,1,0:T(8,128)(2,1)S(1)} %copy-done.5, bf16[1,128,1024]{2,1,0:T(8,128)(2,1)S(1)} %copy-done.1, bf16[1,128,1024]{2,1,0:T(8,128)(2,1)S(1)} %copy-done.3, ...), custom_call_target="tpu_custom_call" | custom-call | flops 2000000000 | bytes 1196032 | tf_op jit(solution)/shard_map/pallas_call | solution.py:361
  33.5 2.5 %collective-permute-start.5 = (f32[256,128]{1,0:T(8,128)S(1)}, f32[256,128]{1,0:T(8,128)S(1)}, u32[]{:S(2)}, u32[]{:S(2)}) collective-permute-start(f32[256,128]{1,0:T(8,128)S(1)} %fusion.3), channel_id=1, source_target_pairs={{0,8},{4,12},{8,0},{12,4},{16,24},{20,28},{24,16},{28,20},{1,9},{5... | collective-permute-start | bytes 393224 | tf_op jit(solution)/shard_map/ppermute | solution.py:392
  36.0 2.2 %collective-permute-start.12 = (f32[8,128]{1,0:T(8,128)S(1)}, f32[8,128]{1,0:T(8,128)S(1)}, u32[]{:S(2)}, u32[]{:S(2)}) collective-permute-start(f32[8,128]{1,0:T(8,128)S(1)} %add_add_fusion), channel_id=1, source_target_pairs={{0,16},{4,20},{8,24},{12,28},{16,0},{20,4},{24,8},{28,12},{1,17},{... | collective-permute-start | bytes 12296 | tf_op jit(solution)/shard_map/ppermute | solution.py:392
  38.3 1.1 %collective-permute-start.11 = (f32[8,128]{1,0:T(8,128)S(1)}, f32[8,128]{1,0:T(8,128)S(1)}, u32[]{:S(2)}, u32[]{:S(2)}) collective-permute-start(f32[8,128]{1,0:T(8,128)S(1)} %add_add_fusion), channel_id=1, source_target_pairs={{0,8},{4,12},{8,0},{12,4},{16,24},{20,28},{24,16},{28,20},{1,9},{5... | collective-permute-start | bytes 12296 | tf_op jit(solution)/shard_map/ppermute | solution.py:392
  39.4 2.9 %collective-permute-start.9 = (f32[264,128]{1,0:T(8,128)S(1)}, f32[264,128]{1,0:T(8,128)S(1)}, u32[]{:S(2)}, u32[]{:S(2)}) collective-permute-start(f32[264,128]{1,0:T(8,128)S(1)} %pad_maximum_fusion), channel_id=1, source_target_pairs={{0,24},{4,28},{8,16},{12,20},{16,8},{20,12},{24,0},{28,4},{1,25},{... | collective-permute-start | bytes 405512 | tf_op jit(solution)/shard_map/ppermute | solution.py:392
  42.3 1.9 %shard_map.125 = (bf16[1,128,1024]{2,1,0:T(8,128)(2,1)}, f32[128,512]{1,0:T(8,128)S(1)}, f32[128,512]{1,0:T(8,128)S(1)}, f32[8,128]{1,0:T(8,128)S(1)}) custom-call(s32[1]{0:T(128)S(6)} %sub.3.half_ref, bf16[1,128,1024]{2,1,0:T(8,128)(2,1)S(1)} %copy-done.5, bf16[1,128,1024]{2,1,0:T(8,128)(2,1)S(1)} %copy-done.1, ...), custom_call_target="tpu_custom_call", output_to_operand_aliasing={{0}: (7, {})} | custom-call | flops 2000000000 | bytes 1196032 | tf_op jit(solution)/shard_map/pallas_call | solution.py:361
  44.3 2.1 %collective-permute-done.9 = f32[264,128]{1,0:T(8,128)S(1)} collective-permute-done((f32[264,128]{1,0:T(8,128)S(1)}, f32[264,128]{1,0:T(8,128)S(1)}, u32[]{:S(2)}, u32[]{:S(2)}) %collective-permute-start.9) | collective-permute-done | bytes 135200 | tf_op jit(solution)/shard_map/ppermute | solution.py:392
  46.5 1.6 %shard_map.126 = (bf16[1,128,1024]{2,1,0:T(8,128)(2,1)}, bf16[1,128,1024]{2,1,0:T(8,128)(2,1)}, f32[8,128]{1,0:T(8,128)S(1)}, f32[1,16,128]{2,1,0:T(8,128)}) custom-call(s32[1]{0:T(128)} %bitcast.half_ref.refs_0_, bf16[1,128,1024]{2,1,0:T(8,128)(2,1)S(1)} %copy-done.1, bf16[1,128,1024]{2,1,0:T(8,128)(2,1)S(1)} %copy-done.3, ...), custom_call_target="tpu_custom_call" | custom-call | bytes 1466368 | tf_op jit(solution)/shard_map/pallas_call | solution.py:361
  48.1 0.6 %fusion.14 = f32[1024]{0:T(1024)} fusion(f32[264,128]{1,0:T(8,128)S(1)} %collective-permute-done.9, f32[8,128]{1,0:T(8,128)S(1)} %collective-permute-done.12, f32[8,128]{1,0:T(8,128)S(1)} %add_add_fusion, f32[8,128]{1,0:T(8,128)S(1)} %collective-permute-done.11), kind=kLoop, calls=%fused_computation.33 | loop fusion | flops 3072 | bytes 20480 | tf_op jit(solution)/shard_map/reshape | solution.py:605
  48.7 1.6 %shard_map.127 = (bf16[1,128,1024]{2,1,0:T(8,128)(2,1)}, bf16[1,128,1024]{2,1,0:T(8,128)(2,1)}, f32[8,128]{1,0:T(8,128)}, f32[1,16,128]{2,1,0:T(8,128)}) custom-call(s32[1]{0:T(128)S(6)} %sub.3.half_ref, bf16[1,128,1024]{2,1,0:T(8,128)(2,1)S(1)} %copy-done.1, bf16[1,128,1024]{2,1,0:T(8,128)(2,1)S(1)} %copy-done.3, ...), custom_call_target="tpu_custom_call", output_to_operand_aliasing={{0}: (10, {}), {1}: (11, {})} | custom-call | bytes 1466368 | tf_op jit(solution)/shard_map/pallas_call | solution.py:361
  (48 shorter events, 4.4 us)
Async XLA Ops:
  0.6 0.7 %copy-start.7 = (f32[1,128,16]{1,2,0:T(8,128)S(1)}, f32[1,128,16]{1,2,0:T(8,128)}, u32[]{:S(2)}) copy-start(f32[1,128,16]{1,2,0:T(8,128)} %param.10) | copy-start | bytes 24580
  0.7 0.7 %copy-start.8 = (s32[1,128]{1,0:T(1,128)S(1)}, s32[1,128]{1,0:T(1,128)}, u32[]{:S(2)}) copy-start(s32[1,128]{1,0:T(1,128)} %restart_ref.1) | copy-start | bytes 1540
  1.3 1.0 %copy-start = (bf16[1,128,1024]{2,1,0:T(8,128)(2,1)S(1)}, bf16[1,128,1024]{2,1,0:T(8,128)(2,1)}, u32[]{:S(2)}) copy-start(bf16[1,128,1024]{2,1,0:T(8,128)(2,1)} %key_ref.11) | copy-start | bytes 786436
  2.3 0.9 %copy-start.2 = (bf16[1,128,1024]{2,1,0:T(8,128)(2,1)S(1)}, bf16[1,128,1024]{2,1,0:T(8,128)(2,1)}, u32[]{:S(2)}) copy-start(bf16[1,128,1024]{2,1,0:T(8,128)(2,1)} %value_ref.11) | copy-start | bytes 786436
  3.2 1.4 %copy-start.1 = (bf16[1,128,1024]{2,1,0:T(8,128)(2,1)S(1)}, bf16[1,128,1024]{2,1,0:T(8,128)(2,1)}, u32[]{:S(2)}) copy-start(bf16[1,128,1024]{2,1,0:T(8,128)(2,1)} %key_ref.11) | copy-start | bytes 786436
  3.2 1.4 %copy-start.3 = (bf16[1,128,1024]{2,1,0:T(8,128)(2,1)S(1)}, bf16[1,128,1024]{2,1,0:T(8,128)(2,1)}, u32[]{:S(2)}) copy-start(bf16[1,128,1024]{2,1,0:T(8,128)(2,1)} %value_ref.11) | copy-start | bytes 786436
  4.1 1.5 %collective-permute-start = (f32[264,128]{1,0:T(8,128)S(1)}, f32[264,128]{1,0:T(8,128)S(1)}, u32[]{:S(2)}, u32[]{:S(2)}) collective-permute-start(f32[264,128]{1,0:T(8,128)S(1)} %get-tuple-element.29), channel_id=1, source_target_pairs={{0,4},{4,0},{8,12},{12,8},{16,20},{20,16},{24,28},{28,24},{1,5},{5... | collective-permute-start | bytes 405512 | tf_op jit(solution)/shard_map/ppermute | solution.py:392
  5.8 6.9 %collective-permute-start.1 = (f32[264,128]{1,0:T(8,128)S(1)}, f32[264,128]{1,0:T(8,128)S(1)}, u32[]{:S(2)}, u32[]{:S(2)}) collective-permute-start(f32[264,128]{1,0:T(8,128)S(1)} %maximum_maximum_fusion), channel_id=1, source_target_pairs={{0,8},{4,12},{8,0},{12,4},{16,24},{20,28},{24,16},{28,20},{1,9},{5... | collective-permute-start | bytes 405512 | tf_op jit(solution)/shard_map/ppermute | solution.py:392
  12.9 7.1 %collective-permute-start.2 = (f32[264,128]{1,0:T(8,128)S(1)}, f32[264,128]{1,0:T(8,128)S(1)}, u32[]{:S(2)}, u32[]{:S(2)}) collective-permute-start(f32[264,128]{1,0:T(8,128)S(1)} %maximum_maximum_fusion.1), channel_id=1, source_target_pairs={{0,24},{4,28},{8,16},{12,20},{16,8},{20,12},{24,0},{28,4},{1,25},{... | collective-permute-start | bytes 405512 | tf_op jit(solution)/shard_map/ppermute | solution.py:392
  20.0 1.0 %copy-start.5 = (bf16[1,128,1024]{2,1,0:T(8,128)(2,1)S(1)}, bf16[1,128,1024]{2,1,0:T(8,128)(2,1)}, u32[]{:S(2)}) copy-start(bf16[1,128,1024]{2,1,0:T(8,128)(2,1)} %query_ref.7) | copy-start | bytes 786436
  20.0 4.7 %collective-permute-start.3 = (f32[256,128]{1,0:T(8,128)S(1)}, f32[256,128]{1,0:T(8,128)S(1)}, u32[]{:S(2)}, u32[]{:S(2)}) collective-permute-start(f32[256,128]{1,0:T(8,128)S(1)} %get-tuple-element.53), channel_id=1, source_target_pairs={{0,4},{4,0},{8,12},{12,8},{16,20},{20,16},{24,28},{28,24},{1,5},{5... | collective-permute-start | bytes 393224 | tf_op jit(solution)/shard_map/ppermute | solution.py:392
  21.5 1.0 %copy-start.4 = (bf16[1,128,1024]{2,1,0:T(8,128)(2,1)S(1)}, bf16[1,128,1024]{2,1,0:T(8,128)(2,1)}, u32[]{:S(2)}) copy-start(bf16[1,128,1024]{2,1,0:T(8,128)(2,1)} %upstream_ref.1) | copy-start | bytes 786436
  22.1 0.7 %copy-start.6 = (f32[1024]{0:T(1024)S(1)}, f32[1024]{0:T(1024)}, u32[]{:S(2)}) copy-start(f32[1024]{0:T(1024)} %param.12) | copy-start | bytes 12292
  26.7 1.4 %collective-permute-start.4 = (f32[264,128]{1,0:T(8,128)S(1)}, f32[264,128]{1,0:T(8,128)S(1)}, u32[]{:S(2)}, u32[]{:S(2)}) collective-permute-start(f32[264,128]{1,0:T(8,128)S(1)} %get-tuple-element.40), channel_id=1, source_target_pairs={{0,4},{4,0},{8,12},{12,8},{16,20},{20,16},{24,28},{28,24},{1,5},{5... | collective-permute-start | bytes 405512 | tf_op jit(solution)/shard_map/ppermute | solution.py:392
  28.1 7.9 %collective-permute-start.8 = (f32[8,128]{1,0:T(8,128)S(1)}, f32[8,128]{1,0:T(8,128)S(1)}, u32[]{:S(2)}, u32[]{:S(2)}) collective-permute-start(f32[8,128]{1,0:T(8,128)S(1)} %slice_add_fusion.1), channel_id=1, source_target_pairs={{0,3},{1,2},{2,1},{3,0},{4,7},{5,6},{6,5},{7,4},{8,11},{9,10},{10,... | collective-permute-start | bytes 12296 | tf_op jit(solution)/shard_map/ppermute | solution.py:392
  30.5 5.5 %collective-permute-start.7 = (f32[8,128]{1,0:T(8,128)S(1)}, f32[8,128]{1,0:T(8,128)S(1)}, u32[]{:S(2)}, u32[]{:S(2)}) collective-permute-start(f32[8,128]{1,0:T(8,128)S(1)} %slice_add_fusion.1), channel_id=1, source_target_pairs={{0,2},{1,3},{2,0},{3,1},{4,6},{5,7},{6,4},{7,5},{8,10},{9,11},{10,... | collective-permute-start | bytes 12296 | tf_op jit(solution)/shard_map/ppermute | solution.py:392
  31.0 5.0 %collective-permute-start.6 = (f32[8,128]{1,0:T(8,128)S(1)}, f32[8,128]{1,0:T(8,128)S(1)}, u32[]{:S(2)}, u32[]{:S(2)}) collective-permute-start(f32[8,128]{1,0:T(8,128)S(1)} %slice_add_fusion.1), channel_id=1, source_target_pairs={{0,1},{1,0},{2,3},{3,2},{4,5},{5,4},{6,7},{7,6},{8,9},{9,8},{10,11... | collective-permute-start | bytes 12296 | tf_op jit(solution)/shard_map/ppermute | solution.py:392
  33.5 5.8 %collective-permute-start.5 = (f32[256,128]{1,0:T(8,128)S(1)}, f32[256,128]{1,0:T(8,128)S(1)}, u32[]{:S(2)}, u32[]{:S(2)}) collective-permute-start(f32[256,128]{1,0:T(8,128)S(1)} %fusion.3), channel_id=1, source_target_pairs={{0,8},{4,12},{8,0},{12,4},{16,24},{20,28},{24,16},{28,20},{1,9},{5... | collective-permute-start | bytes 393224 | tf_op jit(solution)/shard_map/ppermute | solution.py:392
  36.0 12.1 %collective-permute-start.12 = (f32[8,128]{1,0:T(8,128)S(1)}, f32[8,128]{1,0:T(8,128)S(1)}, u32[]{:S(2)}, u32[]{:S(2)}) collective-permute-start(f32[8,128]{1,0:T(8,128)S(1)} %add_add_fusion), channel_id=1, source_target_pairs={{0,16},{4,20},{8,24},{12,28},{16,0},{20,4},{24,8},{28,12},{1,17},{... | collective-permute-start | bytes 12296 | tf_op jit(solution)/shard_map/ppermute | solution.py:392
  38.3 9.8 %collective-permute-start.11 = (f32[8,128]{1,0:T(8,128)S(1)}, f32[8,128]{1,0:T(8,128)S(1)}, u32[]{:S(2)}, u32[]{:S(2)}) collective-permute-start(f32[8,128]{1,0:T(8,128)S(1)} %add_add_fusion), channel_id=1, source_target_pairs={{0,8},{4,12},{8,0},{12,4},{16,24},{20,28},{24,16},{28,20},{1,9},{5... | collective-permute-start | bytes 12296 | tf_op jit(solution)/shard_map/ppermute | solution.py:392
  39.4 7.0 %collective-permute-start.9 = (f32[264,128]{1,0:T(8,128)S(1)}, f32[264,128]{1,0:T(8,128)S(1)}, u32[]{:S(2)}, u32[]{:S(2)}) collective-permute-start(f32[264,128]{1,0:T(8,128)S(1)} %pad_maximum_fusion), channel_id=1, source_target_pairs={{0,24},{4,28},{8,16},{12,20},{16,8},{20,12},{24,0},{28,4},{1,25},{... | collective-permute-start | bytes 405512 | tf_op jit(solution)/shard_map/ppermute | solution.py:392
  46.4 2.3 %collective-permute-start.10 = (f32[256,128]{1,0:T(8,128)S(1)}, f32[256,128]{1,0:T(8,128)S(1)}, u32[]{:S(2)}, u32[]{:S(2)}) collective-permute-start(f32[256,128]{1,0:T(8,128)S(1)} %get-tuple-element.51), channel_id=1, source_target_pairs={{0,4},{4,0},{8,12},{12,8},{16,20},{20,16},{24,28},{28,24},{1,5},{5... | collective-permute-start | bytes 393224 | tf_op jit(solution)/shard_map/ppermute | solution.py:392

commit v3 on v2

v3 whole, which is shorter than its diff:
```python
import functools

import jax
import jax.numpy as jnp
from jax import lax
from jax.experimental import pallas as pl
from jax.experimental.pallas import tpu as pltpu
from jax.sharding import PartitionSpec as P

HEAD_TOTAL = 16
EPSILON = 1e-06
LANES = 128
PAIRS = HEAD_TOTAL // 4
VMEM_BYTES = 12 * 1024 * 1024
F32 = jnp.float32
BF16 = jnp.bfloat16
COLUMNS, MASK, CUM_ROWS, CARRY_ROWS, TABLE_ROWS = 0, 128, 256, 272, 288


def dot(a, b, contract_a=1, contract_b=0):
    return lax.dot_general(
        a, b, (((contract_a,), (contract_b,)), ((), ())), preferred_element_type=F32
    )


def halves(x):
    high = x.astype(BF16)
    return high, (x - high.astype(F32)).astype(BF16)


def stacked(x, axis):
    return jnp.concatenate(halves(x), axis=axis)


def twice(x, axis):
    return jnp.concatenate([x, x], axis=axis)


def left_lanes(shape):
    return lax.broadcasted_iota(jnp.int32, shape, 1) < LANES // 2


def triangle(tokens, keep):
    rows = lax.broadcasted_iota(jnp.int32, (tokens, tokens), 0)
    columns = lax.broadcasted_iota(jnp.int32, (tokens, tokens), 1)
    return keep(rows, columns)


def by_head(x, axis):
    left = left_lanes(x.shape)
    zero = jnp.zeros_like(x)
    return jnp.concatenate([jnp.where(left, x, zero), jnp.where(left, zero, x)], axis=axis)


def fold(x):
    rows = x.shape[0] // 2
    return jnp.where(left_lanes((rows, LANES)), x[:rows], x[rows:])


def pair_columns(table, first, tokens):
    return jnp.where(
        left_lanes((tokens, LANES)),
        jnp.broadcast_to(table[:, first : first + 1], (tokens, LANES)),
        jnp.broadcast_to(table[:, first + 1 : first + 2], (tokens, LANES)),
    )


def make_tables(decay_rows, restart):
    heads, tokens = decay_rows.shape
    lower = triangle(tokens, lambda t, s: s <= t).astype(F32).astype(BF16)
    upper = triangle(tokens, lambda t, s: t <= s).astype(F32).astype(BF16)
    marks = jnp.broadcast_to(restart.astype(F32), (tokens, tokens)).astype(BF16)
    resets_column = dot(lower, marks, 1, 1)
    resets_row = dot(marks, upper)
    cum_rows = row_sums(decay_rows, triangle(tokens, lambda s, t: s <= t))
    cum = jnp.transpose(
        jnp.concatenate([cum_rows, jnp.zeros((LANES - heads, tokens), F32)], axis=0)
    )
    last = cum[tokens - 1 :, :]
    last_reset = resets_column[tokens - 1 :, :]
    entry = jnp.where(resets_column == 0.0, jnp.exp(cum), 0.0)
    leave = jnp.where(resets_column == last_reset, jnp.exp(last - cum), 0.0)
    lane = lax.broadcasted_iota(jnp.int32, (tokens, LANES), 1)
    columns = jnp.where(
        lane < heads,
        cum,
        jnp.where(lane < 2 * heads, pltpu.roll(entry, heads, 1), pltpu.roll(leave, 2 * heads, 1)),
    )
    allowed = triangle(tokens, lambda t, s: t >= s) & (resets_column == resets_row)
    mask = jnp.where(allowed, 0.0, -1e30)
    carry = jnp.where(last_reset[:, :1] == 0.0, jnp.exp(cum_rows[:, tokens - 1 :]), 0.0)
    return columns, mask, cum_rows, jnp.broadcast_to(carry, (heads, LANES))


def pick_columns(columns, half):
    return jnp.where(half == 0, columns, pltpu.roll(columns, LANES - HEAD_TOTAL // 2, 1))


def pick_rows(rows, half):
    count = HEAD_TOTAL // 2
    return jnp.where(half == 0, rows[:count], rows[count:])


def own_half(mine):
    core = lax.axis_index("seq") & 1
    return core if mine else 1 - core


def half_lanes(half, width):
    return pl.ds(pl.multiple_of(half * (width // 2), LANES), width // 2)


def pair_lanes(half, width, pair):
    return pl.ds(pl.multiple_of(half * (width // 2) + pair * LANES, LANES), LANES)


def write_states(half, columns, carry_rows, keys, values, out_ref):
    tokens = keys.shape[0]
    table = pick_columns(columns, half)
    carry = pick_rows(carry_rows, half)
    left = left_lanes((1, LANES))
    scaled = []
    for pair in range(PAIRS):
        leave = pair_columns(table, 2 * HEAD_TOTAL + 2 * pair, tokens)
        lanes = slice(pair * LANES, (pair + 1) * LANES)
        scaled.append(stacked(values[:, lanes].astype(F32) * leave, 1))
    states = []
    for pair in range(PAIRS):
        lanes = slice(pair * LANES, (pair + 1) * LANES)
        states.append(dot(keys[:, lanes], scaled[pair], 0, 0))
    rows = []
    for pair in range(PAIRS):
        out_ref[pl.ds(pair * 64, 64), :] = fold(states[pair][:, :LANES] + states[pair][:, LANES:])
        rows.append(jnp.where(left, carry[2 * pair : 2 * pair + 1], carry[2 * pair + 1 : 2 * pair + 2]))
    rows.append(jnp.zeros((8 - len(rows), LANES), F32))
    out_ref[pl.ds(PAIRS * 64, 8), :] = jnp.concatenate(rows, axis=0)


def first_state_kernel(
    key_ref,
    value_ref,
    decay_ref,
    restart_ref,
    out_ref,
    table_ref,
    keys,
    values,
    decays,
    restarts,
    arrived,
):
    half = own_half(False)
    lanes = half_lanes(half, key_ref.shape[2])
    decay_copy = pltpu.make_async_copy(decay_ref.at[0], decays, arrived.at[2])
    restart_copy = pltpu.make_async_copy(restart_ref, restarts, arrived.at[3])
    value_copy = pltpu.make_async_copy(value_ref.at[0, :, lanes], values, arrived.at[1])
    key_copy = pltpu.make_async_copy(key_ref.at[0, :, lanes], keys, arrived.at[0])
    decay_copy.start()
    restart_copy.start()
    value_copy.start()
    key_copy.start()
    decay_copy.wait()
    restart_copy.wait()
    columns, mask, cum_rows, carry_rows = make_tables(decays[...], restarts[...])
    table_ref[pl.ds(COLUMNS, 128), :] = columns
    table_ref[pl.ds(MASK, 128), :] = mask
    table_ref[pl.ds(CUM_ROWS, 16), :] = cum_rows
    table_ref[pl.ds(CARRY_ROWS, 16), :] = carry_rows
    value_copy.wait()
    key_copy.wait()
    write_states(half, columns, carry_rows, keys[...], values[...], out_ref)


def second_state_kernel(key_ref, value_ref, table_ref, out_ref):
    half = own_half(True)
    lanes = half_lanes(half, key_ref.shape[2])
    write_states(
        half,
        table_ref[pl.ds(COLUMNS, 128), :],
        table_ref[pl.ds(CARRY_ROWS, 16), :],
        key_ref[0, :, lanes],
        value_ref[0, :, lanes],
        out_ref,
    )


def pair_decays(table, cum_rows, mask, pair, tokens):
    parts = []
    for head in (2 * pair, 2 * pair + 1):
        column = jnp.broadcast_to(table[:, head : head + 1], (tokens, tokens))
        parts.append(jnp.exp(column - cum_rows[head : head + 1] + mask))
    return jnp.concatenate(parts, axis=0)


def side_by_side(x):
    rows = x.shape[0] // 2
    return jnp.concatenate([x[:rows], x[rows:]], axis=1)


def pick_gains(gain_ref, half):
    return jnp.where(half == 0, gain_ref[:PAIRS, :], gain_ref[PAIRS:, :])


def mixture_kernel(
    mine,
    query_ref,
    key_ref,
    value_ref,
    upstream_ref,
    gain_ref,
    table_ref,
    out_ref,
    turned_ref,
    entry_ref,
    grad_ref,
):
    tokens, width = query_ref.shape[1:]
    half = own_half(mine)
    table = pick_columns(table_ref[pl.ds(COLUMNS, 128), :], half)
    cum_rows = pick_rows(table_ref[pl.ds(CUM_ROWS, 16), :], half)
    mask = table_ref[pl.ds(MASK, 128), :]
    gains = pick_gains(gain_ref, half)
    for pair in range(PAIRS):
        lanes = pair_lanes(half, width, pair)
        query = query_ref[0, :, lanes]
        decay = pair_decays(table, cum_rows, mask, pair, tokens)
        scores = dot(by_head(query, 0), key_ref[0, :, lanes], 1, 1) * decay
        weights = scores.astype(BF16)
        here = pl.ds(pair * LANES, LANES)
        grad_ref[:, here] = upstream_ref[0, :, lanes].astype(F32) * gains[pair : pair + 1]
        out_ref[:, here] = dot(side_by_side(weights), by_head(value_ref[0, :, lanes], 0))
        turned_ref[here, :] = jnp.transpose(query)
        entry_ref[:, here] = pair_columns(table, HEAD_TOTAL + 2 * pair, tokens)


def forward_kernel(
    mine,
    mixed_ref,
    turned_ref,
    entry_ref,
    grad_ref,
    query_ref,
    upstream_ref,
    gain_ref,
    state_ref,
    before_ref,
    layer_ref,
    grad_mixed_ref,
    out_ref,
):
    tokens, width = query_ref.shape[1:]
    half = own_half(mine)
    gains = pick_gains(gain_ref, half)
    own = left_lanes((LANES, LANES)) == (lax.broadcasted_iota(jnp.int32, (LANES, LANES), 0) < 64)
    average = twice(jnp.where(own, 1.0 / 64.0, 0.0).astype(BF16), 0)
    places = [pl.ds(pair * LANES, LANES) for pair in range(PAIRS)]
    lanes = [pair_lanes(half, width, pair) for pair in range(PAIRS)]
    states = [
        stacked(by_head(state_ref[pl.ds(pair * 64, 64), :], 0), 0) for pair in range(PAIRS)
    ]
    carried = [
        dot(twice(query_ref[0, :, lanes[pair]], 1), states[pair]) for pair in range(PAIRS)
    ]
    mixtures = [
        mixed_ref[:, places[pair]] + entry_ref[:, places[pair]] * carried[pair]
        for pair in range(PAIRS)
    ]
    squares = dot(
        jnp.concatenate([stacked(mixture * mixture, 1) for mixture in mixtures], axis=0), average
    )
    normeds, inverses, grads, products, gain_parts = [], [], [], [], []
    for pair in range(PAIRS):
        inverse = lax.rsqrt(squares[pair * tokens : (pair + 1) * tokens] + EPSILON)
        normed = mixtures[pair] * inverse
        gain = gains[pair : pair + 1]
        upstream = upstream_ref[0, :, lanes[pair]].astype(F32)
        grad_normed = grad_ref[:, places[pair]]
        products.append(stacked(grad_normed * normed, 1))
        layer_ref[:, places[pair]] = (normed * gain).astype(BF16)
        gain_parts.append(jnp.sum(upstream * normed, axis=0, keepdims=True))
        normeds.append(normed)
        inverses.append(inverse)
        grads.append(grad_normed)
    shared = dot(jnp.concatenate(products, axis=0), average)
    sides = []
    for pair in range(PAIRS):
        part = shared[pair * tokens : (pair + 1) * tokens]
        grad_mixed = (inverses[pair] * (grads[pair] - normeds[pair] * part)).astype(BF16)
        grad_mixed_ref[:, places[pair]] = grad_mixed
        sides.append(stacked(entry_ref[:, places[pair]] * grad_mixed.astype(F32), 1))
    for pair in range(PAIRS):
        both = dot(turned_ref[places[pair], :], sides[pair])
        out_ref[pl.ds(pair * 64, 64), :] = fold(both[:, :LANES] + both[:, LANES:])
    part = jnp.concatenate(gain_parts, axis=0)
    blank = jnp.zeros_like(part)
    part = jnp.where(
        half == 0,
        jnp.concatenate([part, blank], axis=0),
        jnp.concatenate([blank, part], axis=0),
    )
    if before_ref is not None:
        part = part + before_ref[pl.ds(PAIRS * 64, 8), :]
    out_ref[pl.ds(PAIRS * 64, 8), :] = part


def backward_kernel(
    mine,
    query_ref,
    key_ref,
    value_ref,
    grad_mixed_ref,
    state_ref,
    entry_ref,
    table_ref,
    layer_part_ref,
    layer_ref,
    grad_query_ref,
    grad_key_ref,
    grad_value_ref,
    later_ref,
    leave_ref,
    grad_query_part,
    sent,
):
    tokens, width = query_ref.shape[1:]
    half = own_half(mine)
    copies = [
        pltpu.make_async_copy(
            layer_part_ref, layer_ref.at[0, :, half_lanes(half, width)], sent.at[0]
        )
    ]
    copies[0].start()
    table = pick_columns(table_ref[pl.ds(COLUMNS, 128), :], half)
    cum_rows = pick_rows(table_ref[pl.ds(CUM_ROWS, 16), :], half)
    mask = table_ref[pl.ds(MASK, 128), :]
    earlier = twice(triangle(tokens, lambda s, t: s < t).astype(F32).astype(BF16), 0)
    reached = triangle(tokens, lambda u, t: u >= t)
    chooser = twice(head_chooser(), 1)
    balance_rows = []
    entry_rows = []
    for pair in range(PAIRS):
        lanes = pair_lanes(half, width, pair)
        here = pl.ds(pair * LANES, LANES)
        query = query_ref[0, :, lanes]
        key = key_ref[0, :, lanes]
        value = value_ref[0, :, lanes]
        grad_mixed = grad_mixed_ref[:, here]
        query_rows = by_head(query, 0)
        mixed_rows = by_head(grad_mixed, 0)
        decay = pair_decays(table, cum_rows, mask, pair, tokens)
        decayed_scores = dot(query_rows, key, 1, 1) * decay
        grad_pairs = dot(mixed_rows, value, 1, 1)
        weights = decayed_scores.astype(BF16)
        grad_weights = (grad_pairs * decay).astype(BF16)
        state = by_head(state_ref[pl.ds(pair * 64, 64), :], 0)
        carried = entry_ref[:, here] * dot(twice(grad_mixed, 1), stacked(state, 1), 1, 1)
        grad_query_part[:, here] = (
            dot(side_by_side(grad_weights), by_head(key, 0)) + carried
        ).astype(BF16)
        copies.append(
            pltpu.make_async_copy(
                grad_query_part.at[:, here], grad_query_ref.at[0, :, lanes], sent.at[1 + pair]
            )
        )
        copies[-1].start()
        grad_key_ref[:, here] = dot(grad_weights, query_rows, 0, 0)
        grad_value_ref[:, here] = dot(weights, mixed_rows, 0, 0)
        leave_ref[:, here] = pair_columns(table, 2 * HEAD_TOTAL + 2 * pair, tokens)
        before = dot(stacked(decayed_scores * grad_pairs, 1), earlier)
        for head in range(2):
            part = before[head * tokens : (head + 1) * tokens]
            balance_rows.append(jnp.sum(jnp.where(reached, part, 0.0), axis=0, keepdims=True))
        terms = dot(chooser, stacked(query.astype(F32) * carried, 1), 1, 1)
        entry_rows.append(terms[:2])
    later_ref[...] = jnp.concatenate(balance_rows, axis=0) + row_sums(
        jnp.concatenate(entry_rows, axis=0), reached
    )
    for copy in copies:
        copy.wait()


def head_chooser():
    rows = lax.broadcasted_iota(jnp.int32, (8, LANES), 0)
    left = left_lanes((8, LANES))
    chosen = ((rows == 0) & left) | ((rows == 1) & ~left)
    return jnp.where(chosen, 1.0, 0.0).astype(BF16)


def row_sums(rows, keep):
    first, second = halves(rows)
    third = (rows - first.astype(F32) - second.astype(F32)).astype(BF16)
    weight = jnp.where(keep, 1.0, 0.0).astype(BF16)
    return dot(
        jnp.concatenate([first, second, third], axis=1),
        jnp.concatenate([weight, weight, weight], axis=0),
    )


def final_kernel(
    mine,
    key_ref,
    value_ref,
    grad_key_part_ref,
    grad_value_part_ref,
    later_ref,
    leave_ref,
    state_ref,
    grad_ref,
    table_ref,
    other_ref,
    gain_refs,
    grad_key_ref,
    grad_value_ref,
    rows_ref,
    decay_ref,
    gain_ref,
    key_out,
    value_out,
    decay_out,
    gain_out,
    sent,
):
    tokens, width = key_ref.shape[1:]
    half = own_half(mine)
    copies = []

    def send(source, target):
        copies.append(pltpu.make_async_copy(source, target, sent.at[len(copies)]))
        copies[-1].start()

    if gain_refs:
        gain_out[...] = sum(ref[...] for ref in gain_refs[1:]) + gain_refs[0][...]
        send(gain_out, gain_ref)
    carry = pick_rows(table_ref[pl.ds(CARRY_ROWS, 16), :], half)
    chooser = twice(head_chooser(), 1)
    left = left_lanes((1, LANES))
    lanes = [pair_lanes(half, width, pair) for pair in range(PAIRS)]
    places = [pl.ds(pair * LANES, LANES) for pair in range(PAIRS)]
    grads = [halves(by_head(grad_ref[pl.ds(pair * 64, 64), :], 0)) for pair in range(PAIRS)]
    carried, terms = [], []
    for pair in range(PAIRS):
        carried.append(
            leave_ref[:, places[pair]]
            * dot(twice(key_ref[0, :, lanes[pair]], 1), jnp.concatenate(grads[pair], axis=0))
        )
    for pair in range(PAIRS):
        value_out[:, places[pair]] = (
            grad_value_part_ref[:, places[pair]] + carried[pair]
        ).astype(BF16)
        terms.append(stacked(carried[pair] * value_ref[0, :, lanes[pair]].astype(F32), 1))
    send(value_out, grad_value_ref.at[0, :, half_lanes(half, width)])
    key_parts = [
        dot(twice(value_ref[0, :, lanes[pair]], 1), jnp.concatenate(grads[pair], axis=1), 1, 1)
        for pair in range(PAIRS)
    ]
    earlier = [dot(chooser, terms[pair], 1, 1)[:2] for pair in range(PAIRS)]
    for pair in range(PAIRS):
        key_out[:, places[pair]] = (
            grad_key_part_ref[:, places[pair]] + leave_ref[:, places[pair]] * key_parts[pair]
        ).astype(BF16)
    send(key_out, grad_key_ref.at[0, :, half_lanes(half, width)])
    through_rows = []
    for pair in range(PAIRS):
        block = pl.ds(pair * 64, 64)
        product = jnp.sum(grad_ref[block, :] * state_ref[block, :], axis=0, keepdims=True)
        for side in (left, ~left):
            through_rows.append(jnp.sum(jnp.where(side, product, 0.0), axis=1, keepdims=True))
    rows = (
        later_ref[...]
        + row_sums(jnp.concatenate(earlier, axis=0), triangle(tokens, lambda u, t: u < t))
        + carry * jnp.concatenate(through_rows, axis=0)
    )
    if rows_ref is not None:
        rows_ref[...] = rows
    else:
        other = other_ref[...]
        decay_out[...] = jnp.where(
            half == 0,
            jnp.concatenate([rows, other], axis=0),
            jnp.concatenate([other, rows], axis=0),
        )
        send(decay_out, decay_ref.at[0])
    for copy in copies:
        copy.wait()


VMEM, HBM = pltpu.VMEM, pltpu.HBM


def call(kernel, operands, results, scratch=(), aliases=None, flops=0, constrain=False):
    read = sum(a.size * a.dtype.itemsize for a, memory in operands if memory is VMEM)
    return pl.pallas_call(
        kernel,
        in_specs=[pl.BlockSpec(memory_space=memory) for a, memory in operands],
        out_specs=[pl.BlockSpec(memory_space=memory) for shape, dtype, memory in results],
        out_shape=[jax.ShapeDtypeStruct(shape, dtype) for shape, dtype, memory in results],
        scratch_shapes=list(scratch),
        input_output_aliases=aliases or {},
        compiler_params=pltpu.CompilerParams(vmem_limit_bytes=VMEM_BYTES),
        cost_estimate=pl.CostEstimate(flops=flops, bytes_accessed=read, transcendentals=0),
    )(
        *[
            pltpu.with_memory_space_constraint(a, HBM) if memory is HBM and constrain else a
            for a, memory in operands
        ]
    )


def local(queries, key_vectors, value_vectors, log_decay, restart, norm_gain, upstream):
    tokens, width = queries.shape[1], queries.shape[2]
    state_rows = PAIRS * 64
    buffer_rows = state_rows + 8
    blocks = lax.axis_size("seq")
    scans = lax.axis_size("dp")
    position = lax.axis_index("seq")
    on_first = (position & 1) == 0

    def exchange(x, bit, axis="seq"):
        size = blocks if axis == "seq" else scans
        return lax.ppermute(x, axis, [(i, i ^ bit) for i in range(size)])

    def parts(buffer):
        state = buffer[:state_rows].reshape(PAIRS, 64, LANES)
        if buffer.shape[0] == state_rows:
            return state, None
        return state, buffer[state_rows : state_rows + PAIRS].reshape(PAIRS, 1, LANES)

    def joined(state, carry):
        return jnp.concatenate(
            [
                state.reshape(state_rows, LANES),
                carry.reshape(PAIRS, LANES),
                jnp.zeros((8 - PAIRS, LANES), F32),
            ],
            axis=0,
        )

    def flat(state):
        return state.reshape(state_rows, LANES)

    whole = (1, tokens, width)
    part = (tokens, width // 2)
    buffer = (buffer_rows, LANES)
    rows = (HEAD_TOTAL // 2, LANES)
    blocks_of = [(queries, VMEM), (key_vectors, VMEM), (value_vectors, VMEM)]

    gain_rows = norm_gain.reshape(2 * PAIRS, LANES)

    state_other, tables = call(
        first_state_kernel,
        [
            (key_vectors, HBM),
            (value_vectors, HBM),
            (jnp.swapaxes(log_decay, 1, 2), HBM),
            (restart, HBM),
        ],
        [(buffer, F32, VMEM), ((TABLE_ROWS, LANES), F32, VMEM)],
        [
            pltpu.VMEM(part, BF16),
            pltpu.VMEM(part, BF16),
            pltpu.VMEM((HEAD_TOTAL, tokens), F32),
            pltpu.VMEM((1, tokens), jnp.int32),
            pltpu.SemaphoreType.DMA((4,)),
        ],
        constrain=True,
    )
    swapped = exchange(state_other, 1)
    (state_own,) = call(
        second_state_kernel,
        [(key_vectors, VMEM), (value_vectors, VMEM), (tables, VMEM)],
        [(buffer, F32, VMEM)],
    )
    first_state, first_carry = parts(jnp.where(on_first, state_own, swapped))
    second_state, second_carry = parts(jnp.where(on_first, swapped, state_own))
    total = second_carry * first_state + second_state
    carry = first_carry * second_carry
    prefix = jnp.zeros_like(total)
    prefix_carry = jnp.ones_like(carry)

    def mixture(mine, tables):
        return call(
            functools.partial(mixture_kernel, mine),
            blocks_of + [(upstream, VMEM), (gain_rows, VMEM), (tables, VMEM)],
            [
                (part, F32, VMEM),
                ((width // 2, LANES), BF16, VMEM),
                (part, F32, VMEM),
                (part, F32, VMEM),
            ],
            flops=0,
        )

    mixed = {}
    levels = []
    bit = 2
    while bit < blocks:
        is_upper = (position & bit) != 0
        sent = joined(total, carry)
        mine = not mixed
        if len(mixed) < 2:
            sent, tables = lax.optimization_barrier((sent, tables))
            mixed[mine] = mixture(mine, tables)
        received = exchange(sent, 2 * bit - 2)
        if len(levels) < 2:
            received, mixed[mine] = lax.optimization_barrier((received, mixed[mine]))
        theirs, their_carry = parts(received)
        prefix = jnp.where(is_upper, prefix_carry * theirs + prefix, prefix)
        prefix_carry = jnp.where(is_upper, prefix_carry * their_carry, prefix_carry)
        levels.append((bit, is_upper, carry, their_carry))
        total = jnp.where(is_upper, carry * theirs + total, their_carry * total + theirs)
        carry = carry * their_carry
        bit *= 2
    for mine in (True, False):
        if mine not in mixed:
            mixed[mine] = mixture(mine, tables)
    after_first = first_carry * prefix + first_state
    state_in = {True: flat(jnp.where(on_first, prefix, after_first))}
    state_in[False] = exchange(flat(jnp.where(on_first, after_first, prefix)), 1)

    layer_parts, grad_mixed, query_states = {}, {}, {}
    for mine in (True, False):
        operands = [
            *[(x, VMEM) for x in mixed[mine][:4]],
            (queries, VMEM),
            (upstream, VMEM),
            (gain_rows, VMEM),
            (state_in[mine], VMEM),
        ]
        if mine:
            kernel = lambda *refs: forward_kernel(True, *refs[:8], None, *refs[8:])
        else:
            operands.append((query_states[True], VMEM))
            kernel = functools.partial(forward_kernel, False)
        layer_parts[mine], grad_mixed[mine], query_states[mine] = call(
            kernel, operands, [(part, BF16, VMEM), (part, BF16, VMEM), (buffer, F32, VMEM)]
        )

    outputs = {}

    def backward(mine, state):
        operands = blocks_of + [
            (grad_mixed[mine], VMEM),
            (state, VMEM),
            (mixed[mine][2], VMEM),
            (tables, VMEM),
            (layer_parts[mine], VMEM),
        ]
        aliases = {}
        kernel = functools.partial(backward_kernel, mine)
        if outputs:
            kernel = lambda *refs: backward_kernel(mine, *refs[:8], *refs[10:])
            operands += [(outputs["layer"], HBM), (outputs["query"], HBM)]
            aliases = {8: 0, 9: 1}
        outputs["layer"], outputs["query"], *local_parts = call(
            kernel,
            operands,
            [
                (whole, BF16, HBM),
                (whole, BF16, HBM),
                (part, F32, VMEM),
                (part, F32, VMEM),
                (rows, F32, VMEM),
                (part, F32, VMEM),
            ],
            [pltpu.VMEM(part, BF16), pltpu.SemaphoreType.DMA((1 + PAIRS,))],
            aliases,
            flops=0,
        )
        return local_parts

    swapped = exchange(query_states[False], 1)
    first_query, _ = parts(jnp.where(on_first, query_states[True], swapped))
    second_query, _ = parts(jnp.where(on_first, swapped, query_states[True]))
    total = flat(first_query + first_carry * second_query)
    suffix = jnp.zeros_like(first_query)
    suffix_carry = jnp.ones_like(carry)
    gain = query_states[False][state_rows:] + swapped[state_rows:]
    local_parts = {}
    gains = [gain]
    for bit, is_upper, carry, their_carry in levels:
        partner = 2 * bit - 2
        mine = not local_parts
        beside = len(local_parts) < 2
        gain = sum(gains)
        state = state_in[mine]
        total, gain, state = lax.optimization_barrier((total, gain, state))
        if bit == 2:
            received = exchange(total, partner)
            gains = [gain]
            for k in range(1, min(4, scans)):
                gains.append(exchange(gain, k, "dp"))
            step = 4
            while step < scans:
                gain = sum(gains)
                gains = [gain] + [
                    exchange(gain, k * step, "dp") for k in range(1, min(4, scans // step))
                ]
                step *= 4
            if len(levels) == 1:
                gain = sum(gains)
                gains = [gain, exchange(gain, partner)]
        else:
            received = exchange(jnp.concatenate([total, gain], axis=0), partner)
            gains = [gain]
            if 2 * bit == blocks:
                gains += [exchange(gain, 2), exchange(gain, partner ^ 2)]
        if beside:
            local_parts[mine] = backward(mine, state)
            received, gains, local_parts[mine] = lax.optimization_barrier(
                (received, gains, local_parts[mine])
            )
        if bit > 2:
            gains.append(received[state_rows:])
        theirs, _ = parts(received)
        total = parts(total)[0]
        suffix = jnp.where(is_upper, suffix, suffix_carry * theirs + suffix)
        suffix_carry = jnp.where(is_upper, suffix_carry, suffix_carry * their_carry)
        total = flat(jnp.where(is_upper, theirs + their_carry * total, total + carry * theirs))
    for mine in (True, False):
        if mine not in local_parts:
            local_parts[mine] = backward(mine, state_in[mine])
    before_second = second_query + second_carry * suffix
    state_grad = {True: flat(jnp.where(on_first, before_second, suffix))}
    state_grad[False] = exchange(flat(jnp.where(on_first, suffix, before_second)), 1)

    for mine in (True, False):
        grad_key_part, grad_value_part, later, leave = local_parts[mine]
        operands = [
            (key_vectors, VMEM),
            (value_vectors, VMEM),
            (grad_key_part, VMEM),
            (grad_value_part, VMEM),
            (later, VMEM),
            (leave, VMEM),
            (state_in[mine], VMEM),
            (state_grad[mine], VMEM),
            (tables, VMEM),
        ]
        results = [(whole, BF16, HBM), (whole, BF16, HBM)]
        scratch = [pltpu.VMEM(part, BF16), pltpu.VMEM(part, BF16)]
        if mine:
            kernel = lambda *refs: final_kernel(
                True, *refs[:9], None, [], *refs[9:12], None, None, *refs[12:14], None, None, refs[14]
            )
            aliases = None
            results.append((rows, F32, VMEM))
        else:
            count = len(gains)
            operands.append((decay_rows, VMEM))
            operands += [(x, VMEM) for x in gains]
            operands += [(grad_key, HBM), (grad_value, HBM)]
            kernel = lambda *refs: final_kernel(
                False,
                *refs[:10],
                refs[10 : 10 + count],
                *refs[12 + count : 14 + count],
                None,
                *refs[14 + count :],
            )
            aliases = {10 + count: 0, 11 + count: 1}
            results += [((1, HEAD_TOTAL, tokens), F32, HBM), ((2 * PAIRS, LANES), F32, HBM)]
            scratch += [pltpu.VMEM((HEAD_TOTAL, tokens), F32), pltpu.VMEM((2 * PAIRS, LANES), F32)]
        scratch.append(pltpu.SemaphoreType.DMA((4,)))
        grad_key, grad_value, *rest = call(kernel, operands, results, scratch, aliases)
        if mine:
            (decay_rows,) = rest
        else:
            grad_decay, grad_gain = rest
    grad_decay = jnp.swapaxes(grad_decay, 1, 2)
    return (
        outputs["layer"],
        outputs["query"],
        grad_key,
        grad_value,
        grad_decay,
        grad_gain.reshape(-1),
    )


def solution(mesh):
    rows = P("dp", "seq", None)
    return jax.shard_map(
        local,
        mesh=mesh,
        in_specs=(rows, rows, rows, rows, P("dp", "seq"), P(), rows),
        out_specs=(rows, rows, rows, rows, rows, P()),
        check_vma=False,
    )
```

time: 50.6 us -> 42 us (0.83)
  local copies, waits for them, and re-layouts: 4.18 us -> 0.11 us
  Pallas kernels: 13.6 us -> 11.1 us
  starting transfers between devices: 19.7 us -> 18.1 us
  other arithmetic: 1.07 us -> 0.47 us
    unnamed x18 -> x10, local copies, waits for them, and re-layouts: 4.1 us -> 0.03 us
    pallas_call x10, Pallas kernels: 13.6 us -> 11.1 us  [call(): pl.pallas_call(kernel, in_specs=[pl.BlockSpec(memory_space=memory) for a,...]
    ppermute x13, starting transfers between devices: 19.7 us -> 18.1 us  [exchange(): return lax.ppermute(x, axis, [(i, i ^ bit) for i in range(size)])]
    reshape x1 -> x0, other arithmetic: 0.6 us -> none  [local(): gain.reshape(-1)]
  transfers between devices with their start and end apart: 13 -> 13, of which waited for: 5 -> 9; matrix products, arithmetic and copies ran while one was open for 2% -> 0% of each run, Pallas kernels for 18% -> 18%
where the time goes in v3:
time: 42 us; the launch traced here: 41.8 us
  starting transfers between devices  18.1 us (43%)
  waiting for transfers between devices  11.2 us (27%)
  Pallas kernels  11.1 us (26%)
  between operations  0.87 us (2%)
  other arithmetic  0.47 us (1%)
    ppermute x13, starting transfers between devices, exchange(): return lax.ppermute(x, axis, [(i, i ^ bit) for i in range(size)])  18.1 us
    ppermute x13, waiting for transfers between devices, exchange(): return lax.ppermute(x, axis, [(i, i ^ bit) for i in range(size)])  11.2 us
    pallas_call x10, Pallas kernels, call(): pl.pallas_call(kernel, in_specs=[pl.BlockSpec(memory_space=memory) for a,...  11.1 us
  transfers between devices with their start and end apart: 13, of which 9 were waited for; matrix products, arithmetic and copies ran while one was open for 0% of the time, Pallas kernels for 18%

profile of v3, /device:TPU:0, one launch (start us, length us, event | category | flops | bytes accessed | tf_op | source)
XLA Modules:
  0.0 41.8 jit_solution(16419977027249330230)
XLA Ops:
  0.7 1.7 %shard_map.118 = (f32[264,128]{1,0:T(8,128)S(1)}, f32[288,128]{1,0:T(8,128)S(1)}) custom-call(bf16[1,128,1024]{2,1,0:T(8,128)(2,1)} %refs_0_.5, bf16[1,128,1024]{2,1,0:T(8,128)(2,1)} %refs_1_.5, f32[1,16,128]{2,1,0:T(8,128)} %bitcast.68, s32[1,128]{1,0:T(1,128)} %restart_ref.1), custom_call_target="tpu_custom_call" | custom-call | tf_op jit(solution)/shard_map/pallas_call | solution.py:492
  2.4 0.5 %collective-permute-start = (f32[264,128]{1,0:T(8,128)S(1)}, f32[264,128]{1,0:T(8,128)S(1)}, u32[]{:S(2)}, u32[]{:S(2)}) collective-permute-start(f32[264,128]{1,0:T(8,128)S(1)} %get-tuple-element.79), channel_id=1, source_target_pairs={{0,4},{4,0},{8,12},{12,8},{16,20},{20,16},{24,28},{28,24},{1,5},{5... | collective-permute-start | bytes 405512 | tf_op jit(solution)/shard_map/ppermute | solution.py:520
  2.9 0.5 %shard_map.119 = f32[264,128]{1,0:T(8,128)S(1)} custom-call(bf16[1,128,1024]{2,1,0:T(8,128)(2,1)S(1)} %copy-done, bf16[1,128,1024]{2,1,0:T(8,128)(2,1)S(1)} %copy-done.1, f32[288,128]{1,0:T(8,128)S(1)} %get-tuple-element.88.table_ref.refs_6_.refs_8_), custom_call_target="tpu_custom_call" | custom-call | bytes 671744 | tf_op jit(solution)/shard_map/pallas_call | solution.py:492
  4.1 3.0 %collective-permute-start.1 = (f32[264,128]{1,0:T(8,128)S(1)}, f32[264,128]{1,0:T(8,128)S(1)}, u32[]{:S(2)}, u32[]{:S(2)}) collective-permute-start(f32[264,128]{1,0:T(8,128)S(1)} %maximum_maximum_fusion), channel_id=1, source_target_pairs={{0,8},{4,12},{8,0},{12,4},{16,24},{20,28},{24,16},{28,20},{1,9},{5... | collective-permute-start | bytes 405512 | tf_op jit(solution)/shard_map/ppermute | solution.py:520
  7.1 0.6 %shard_map.120 = (f32[128,512]{1,0:T(8,128)S(1)}, bf16[512,128]{1,0:T(8,128)(2,1)S(1)}, f32[128,512]{1,0:T(8,128)S(1)}, f32[128,512]{1,0:T(8,128)S(1)}) custom-call(bf16[1,128,1024]{2,1,0:T(8,128)(2,1)S(1)} %copy-done.2, bf16[1,128,1024]{2,1,0:T(8,128)(2,1)S(1)} %copy-done, bf16[1,128,1024]{2,1,0:T(8,128)(2,1)S(1)} %copy-done.1, ...), custom_call_target="tpu_custom_call" | custom-call | bytes 1200128 | tf_op jit(solution)/shard_map/pallas_call | solution.py:492
  7.7 3.3 %collective-permute-done.1 = f32[264,128]{1,0:T(8,128)S(1)} collective-permute-done((f32[264,128]{1,0:T(8,128)S(1)}, f32[264,128]{1,0:T(8,128)S(1)}, u32[]{:S(2)}, u32[]{:S(2)}) %collective-permute-start.1) | collective-permute-done | bytes 135200 | tf_op jit(solution)/shard_map/ppermute | solution.py:520
  11.1 3.8 %collective-permute-start.2 = (f32[264,128]{1,0:T(8,128)S(1)}, f32[264,128]{1,0:T(8,128)S(1)}, u32[]{:S(2)}, u32[]{:S(2)}) collective-permute-start(f32[264,128]{1,0:T(8,128)S(1)} %maximum_maximum_fusion.1), channel_id=1, source_target_pairs={{0,24},{4,28},{8,16},{12,20},{16,8},{20,12},{24,0},{28,4},{1,25},{... | collective-permute-start | bytes 405512 | tf_op jit(solution)/shard_map/ppermute | solution.py:520
  14.9 0.6 %shard_map.121 = (f32[128,512]{1,0:T(8,128)S(1)}, bf16[512,128]{1,0:T(8,128)(2,1)S(1)}, f32[128,512]{1,0:T(8,128)S(1)}, f32[128,512]{1,0:T(8,128)S(1)}) custom-call(bf16[1,128,1024]{2,1,0:T(8,128)(2,1)S(1)} %copy-done.2, bf16[1,128,1024]{2,1,0:T(8,128)(2,1)S(1)} %copy-done, bf16[1,128,1024]{2,1,0:T(8,128)(2,1)S(1)} %copy-done.1, ...), custom_call_target="tpu_custom_call" | custom-call | bytes 1200128 | tf_op jit(solution)/shard_map/pallas_call | solution.py:492
  15.5 2.7 %collective-permute-done.2 = f32[264,128]{1,0:T(8,128)S(1)} collective-permute-done((f32[264,128]{1,0:T(8,128)S(1)}, f32[264,128]{1,0:T(8,128)S(1)}, u32[]{:S(2)}, u32[]{:S(2)}) %collective-permute-start.2) | collective-permute-done | bytes 135200 | tf_op jit(solution)/shard_map/ppermute | solution.py:520
  18.3 0.7 %shard_map.122 = (bf16[128,512]{1,0:T(8,128)(2,1)S(1)}, bf16[128,512]{1,0:T(8,128)(2,1)S(1)}, f32[264,128]{1,0:T(8,128)S(1)}) custom-call(f32[128,512]{1,0:T(8,128)S(1)} %get-tuple-element.98.refs_0_, bf16[512,128]{1,0:T(8,128)(2,1)S(1)} %get-tuple-element.99.refs_1_, f32[128,512]{1,0:T(8,128)S(1)} %get-tuple-element.100.refs_2_.entry_ref, ...), custom_call_target="tpu_custom_call" | custom-call | bytes 1576960 | tf_op jit(solution)/shard_map/pallas_call | solution.py:492
  19.1 0.6 %collective-permute-done.3.state_ref.refs_4_.refs_6_ = f32[256,128]{1,0:T(8,128)S(1)} collective-permute-done((f32[256,128]{1,0:T(8,128)S(1)}, f32[256,128]{1,0:T(8,128)S(1)}, u32[]{:S(2)}, u32[]{:S(2)}) %collective-permute-start.3) | collective-permute-done | bytes 131104 | tf_op jit(solution)/shard_map/ppermute | solution.py:520
  19.7 0.7 %shard_map.123 = (bf16[128,512]{1,0:T(8,128)(2,1)S(1)}, bf16[128,512]{1,0:T(8,128)(2,1)S(1)}, f32[264,128]{1,0:T(8,128)S(1)}) custom-call(f32[128,512]{1,0:T(8,128)S(1)} %get-tuple-element.93.mixed_ref, bf16[512,128]{1,0:T(8,128)(2,1)S(1)} %get-tuple-element.94.turned_ref, f32[128,512]{1,0:T(8,128)S(1)} %get-tuple-element.95.entry_ref.refs_5_, ...), custom_call_target="tpu_custom_call" | custom-call | bytes 1712128 | tf_op jit(solution)/shard_map/pallas_call | solution.py:492
  20.6 1.2 %collective-permute-done.4 = f32[264,128]{1,0:T(8,128)S(1)} collective-permute-done((f32[264,128]{1,0:T(8,128)S(1)}, f32[264,128]{1,0:T(8,128)S(1)}, u32[]{:S(2)}, u32[]{:S(2)}) %collective-permute-start.4) | collective-permute-done | bytes 135200 | tf_op jit(solution)/shard_map/ppermute | solution.py:520
  21.9 2.5 %collective-permute-start.5 = (f32[256,128]{1,0:T(8,128)S(1)}, f32[256,128]{1,0:T(8,128)S(1)}, u32[]{:S(2)}, u32[]{:S(2)}) collective-permute-start(f32[256,128]{1,0:T(8,128)S(1)} %fusion.13), channel_id=1, source_target_pairs={{0,8},{4,12},{8,0},{12,4},{16,24},{20,28},{24,16},{28,20},{1,9},{5... | collective-permute-start | bytes 393224 | tf_op jit(solution)/shard_map/ppermute | solution.py:520
  24.4 1.5 %collective-permute-start.6 = (f32[8,128]{1,0:T(8,128)S(1)}, f32[8,128]{1,0:T(8,128)S(1)}, u32[]{:S(2)}, u32[]{:S(2)}) collective-permute-start(f32[8,128]{1,0:T(8,128)S(1)} %slice_add_fusion), channel_id=1, source_target_pairs={{0,1},{1,0},{2,3},{3,2},{4,5},{5,4},{6,7},{7,6},{8,9},{9,8},{10,11... | collective-permute-start | bytes 12296 | tf_op jit(solution)/shard_map/ppermute | solution.py:520
  25.8 1.5 %collective-permute-start.7 = (f32[8,128]{1,0:T(8,128)S(1)}, f32[8,128]{1,0:T(8,128)S(1)}, u32[]{:S(2)}, u32[]{:S(2)}) collective-permute-start(f32[8,128]{1,0:T(8,128)S(1)} %slice_add_fusion), channel_id=1, source_target_pairs={{0,2},{1,3},{2,0},{3,1},{4,6},{5,7},{6,4},{7,5},{8,10},{9,11},{10,... | collective-permute-start | bytes 12296 | tf_op jit(solution)/shard_map/ppermute | solution.py:520
  27.8 2.0 %shard_map.124 = (bf16[1,128,1024]{2,1,0:T(8,128)(2,1)}, bf16[1,128,1024]{2,1,0:T(8,128)(2,1)}, f32[128,512]{1,0:T(8,128)S(1)}, f32[128,512]{1,0:T(8,128)S(1)}, ...) custom-call(bf16[1,128,1024]{2,1,0:T(8,128)(2,1)S(1)} %copy-done.2, bf16[1,128,1024]{2,1,0:T(8,128)(2,1)S(1)} %copy-done, ...), custom_call_target="tpu_custom_call" | custom-call | bytes 1589248 | tf_op jit(solution)/shard_map/pallas_call | solution.py:492
  29.9 2.0 %collective-permute-done.8 = f32[8,128]{1,0:T(8,128)S(1)} collective-permute-done((f32[8,128]{1,0:T(8,128)S(1)}, f32[8,128]{1,0:T(8,128)S(1)}, u32[]{:S(2)}, u32[]{:S(2)}) %collective-permute-start.8) | collective-permute-done | bytes 4128 | tf_op jit(solution)/shard_map/ppermute | solution.py:520
  31.9 2.7 %collective-permute-start.9 = (f32[264,128]{1,0:T(8,128)S(1)}, f32[264,128]{1,0:T(8,128)S(1)}, u32[]{:S(2)}, u32[]{:S(2)}) collective-permute-start(f32[264,128]{1,0:T(8,128)S(1)} %pad_maximum_fusion), channel_id=1, source_target_pairs={{0,24},{4,28},{8,16},{12,20},{16,8},{20,12},{24,0},{28,4},{1,25},{... | collective-permute-start | bytes 405512 | tf_op jit(solution)/shard_map/ppermute | solution.py:520
  34.7 1.7 %collective-permute-start.11 = (f32[8,128]{1,0:T(8,128)S(1)}, f32[8,128]{1,0:T(8,128)S(1)}, u32[]{:S(2)}, u32[]{:S(2)}) collective-permute-start(f32[8,128]{1,0:T(8,128)S(1)} %add_add_fusion.refs_10_), channel_id=1, source_target_pairs={{0,16},{4,20},{8,24},{12,28},{16,0},{20,4},{24,8},{28,12},{1,17},{... | collective-permute-start | bytes 12296 | tf_op jit(solution)/shard_map/ppermute | solution.py:520
  36.4 2.0 %shard_map.125 = (bf16[1,128,1024]{2,1,0:T(8,128)(2,1)}, bf16[1,128,1024]{2,1,0:T(8,128)(2,1)}, f32[128,512]{1,0:T(8,128)S(1)}, f32[128,512]{1,0:T(8,128)S(1)}, ...) custom-call(bf16[1,128,1024]{2,1,0:T(8,128)(2,1)S(1)} %copy-done.2, ...), custom_call_target="tpu_custom_call", output_to_operand_aliasing={{0}: (8, {}), {1}: (9, {})} | custom-call | bytes 1589248 | tf_op jit(solution)/shard_map/pallas_call | solution.py:492
  38.7 0.5 %collective-permute-done.11.refs_12_ = f32[8,128]{1,0:T(8,128)S(1)} collective-permute-done((f32[8,128]{1,0:T(8,128)S(1)}, f32[8,128]{1,0:T(8,128)S(1)}, u32[]{:S(2)}, u32[]{:S(2)}) %collective-permute-start.11) | collective-permute-done | bytes 4128 | tf_op jit(solution)/shard_map/ppermute | solution.py:520
  39.4 1.0 %shard_map.126 = (bf16[1,128,1024]{2,1,0:T(8,128)(2,1)}, bf16[1,128,1024]{2,1,0:T(8,128)(2,1)}, f32[8,128]{1,0:T(8,128)S(1)}) custom-call(bf16[1,128,1024]{2,1,0:T(8,128)(2,1)S(1)} %copy-done, bf16[1,128,1024]{2,1,0:T(8,128)(2,1)S(1)} %copy-done.1, f32[128,512]{1,0:T(8,128)S(1)} %get-tuple-element.136.refs_2_, f32[128,512]{1,0:T(8,128)S(1)} %get-tuple-element.137.refs_3_, ...), custom_call_target="tpu_custom_call" | custom-call | bytes 1724416 | tf_op jit(solution)/shard_map/pallas_call | solution.py:492
  40.7 1.1 %shard_map.127 = (bf16[1,128,1024]{2,1,0:T(8,128)(2,1)}, bf16[1,128,1024]{2,1,0:T(8,128)(2,1)}, f32[1,16,128]{2,1,0:T(8,128)}, f32[8,128]{1,0:T(8,128)}) custom-call(bf16[1,128,1024]{2,1,0:T(8,128)(2,1)S(1)} %copy-done, bf16[1,128,1024]{2,1,0:T(8,128)(2,1)S(1)} %copy-done.1, ...), custom_call_target="tpu_custom_call", output_to_operand_aliasing={{0}: (14, {}), {1}: (15, {})} | custom-call | bytes 1744896 | tf_op jit(solution)/shard_map/pallas_call | solution.py:492
  (39 shorter events, 2.3 us)
Async XLA Ops:
  0.6 2.2 %copy-start = (bf16[1,128,1024]{2,1,0:T(8,128)(2,1)S(1)}, bf16[1,128,1024]{2,1,0:T(8,128)(2,1)}, u32[]{:S(2)}) copy-start(bf16[1,128,1024]{2,1,0:T(8,128)(2,1)} %refs_0_.5) | copy-start | bytes 786436
  0.6 2.2 %copy-start.1 = (bf16[1,128,1024]{2,1,0:T(8,128)(2,1)S(1)}, bf16[1,128,1024]{2,1,0:T(8,128)(2,1)}, u32[]{:S(2)}) copy-start(bf16[1,128,1024]{2,1,0:T(8,128)(2,1)} %refs_1_.5) | copy-start | bytes 786436
  2.4 1.5 %collective-permute-start = (f32[264,128]{1,0:T(8,128)S(1)}, f32[264,128]{1,0:T(8,128)S(1)}, u32[]{:S(2)}, u32[]{:S(2)}) collective-permute-start(f32[264,128]{1,0:T(8,128)S(1)} %get-tuple-element.79), channel_id=1, source_target_pairs={{0,4},{4,0},{8,12},{12,8},{16,20},{20,16},{24,28},{28,24},{1,5},{5... | collective-permute-start | bytes 405512 | tf_op jit(solution)/shard_map/ppermute | solution.py:520
  3.9 3.2 %copy-start.2 = (bf16[1,128,1024]{2,1,0:T(8,128)(2,1)S(1)}, bf16[1,128,1024]{2,1,0:T(8,128)(2,1)}, u32[]{:S(2)}) copy-start(bf16[1,128,1024]{2,1,0:T(8,128)(2,1)} %refs_0_.3) | copy-start | bytes 786436
  3.9 3.2 %copy-start.3 = (bf16[1,128,1024]{2,1,0:T(8,128)(2,1)S(1)}, bf16[1,128,1024]{2,1,0:T(8,128)(2,1)}, u32[]{:S(2)}) copy-start(bf16[1,128,1024]{2,1,0:T(8,128)(2,1)} %upstream_ref.5) | copy-start | bytes 786436
  4.1 3.0 %copy-start.4 = (f32[1024]{0:T(1024)S(1)}, f32[1024]{0:T(1024)}, u32[]{:S(2)}) copy-start(f32[1024]{0:T(1024)} %param.12) | copy-start | bytes 12292
  4.1 6.9 %collective-permute-start.1 = (f32[264,128]{1,0:T(8,128)S(1)}, f32[264,128]{1,0:T(8,128)S(1)}, u32[]{:S(2)}, u32[]{:S(2)}) collective-permute-start(f32[264,128]{1,0:T(8,128)S(1)} %maximum_maximum_fusion), channel_id=1, source_target_pairs={{0,8},{4,12},{8,0},{12,4},{16,24},{20,28},{24,16},{28,20},{1,9},{5... | collective-permute-start | bytes 405512 | tf_op jit(solution)/shard_map/ppermute | solution.py:520
  11.1 7.1 %collective-permute-start.2 = (f32[264,128]{1,0:T(8,128)S(1)}, f32[264,128]{1,0:T(8,128)S(1)}, u32[]{:S(2)}, u32[]{:S(2)}) collective-permute-start(f32[264,128]{1,0:T(8,128)S(1)} %maximum_maximum_fusion.1), channel_id=1, source_target_pairs={{0,24},{4,28},{8,16},{12,20},{16,8},{20,12},{24,0},{28,4},{1,25},{... | collective-permute-start | bytes 405512 | tf_op jit(solution)/shard_map/ppermute | solution.py:520
  18.3 1.4 %collective-permute-start.3 = (f32[256,128]{1,0:T(8,128)S(1)}, f32[256,128]{1,0:T(8,128)S(1)}, u32[]{:S(2)}, u32[]{:S(2)}) collective-permute-start(f32[256,128]{1,0:T(8,128)S(1)} %get-tuple-element.153), channel_id=1, source_target_pairs={{0,4},{4,0},{8,12},{12,8},{16,20},{20,16},{24,28},{28,24},{1,5},{5... | collective-permute-start | bytes 393224 | tf_op jit(solution)/shard_map/ppermute | solution.py:520
  20.4 1.4 %collective-permute-start.4 = (f32[264,128]{1,0:T(8,128)S(1)}, f32[264,128]{1,0:T(8,128)S(1)}, u32[]{:S(2)}, u32[]{:S(2)}) collective-permute-start(f32[264,128]{1,0:T(8,128)S(1)} %get-tuple-element.104), channel_id=1, source_target_pairs={{0,4},{4,0},{8,12},{12,8},{16,20},{20,16},{24,28},{28,24},{1,5},{5... | collective-permute-start | bytes 405512 | tf_op jit(solution)/shard_map/ppermute | solution.py:520
  21.9 10.0 %collective-permute-start.5 = (f32[256,128]{1,0:T(8,128)S(1)}, f32[256,128]{1,0:T(8,128)S(1)}, u32[]{:S(2)}, u32[]{:S(2)}) collective-permute-start(f32[256,128]{1,0:T(8,128)S(1)} %fusion.13), channel_id=1, source_target_pairs={{0,8},{4,12},{8,0},{12,4},{16,24},{20,28},{24,16},{28,20},{1,9},{5... | collective-permute-start | bytes 393224 | tf_op jit(solution)/shard_map/ppermute | solution.py:520
  24.4 5.5 %collective-permute-start.6 = (f32[8,128]{1,0:T(8,128)S(1)}, f32[8,128]{1,0:T(8,128)S(1)}, u32[]{:S(2)}, u32[]{:S(2)}) collective-permute-start(f32[8,128]{1,0:T(8,128)S(1)} %slice_add_fusion), channel_id=1, source_target_pairs={{0,1},{1,0},{2,3},{3,2},{4,5},{5,4},{6,7},{7,6},{8,9},{9,8},{10,11... | collective-permute-start | bytes 12296 | tf_op jit(solution)/shard_map/ppermute | solution.py:520
  25.8 4.1 %collective-permute-start.7 = (f32[8,128]{1,0:T(8,128)S(1)}, f32[8,128]{1,0:T(8,128)S(1)}, u32[]{:S(2)}, u32[]{:S(2)}) collective-permute-start(f32[8,128]{1,0:T(8,128)S(1)} %slice_add_fusion), channel_id=1, source_target_pairs={{0,2},{1,3},{2,0},{3,1},{4,6},{5,7},{6,4},{7,5},{8,10},{9,11},{10,... | collective-permute-start | bytes 12296 | tf_op jit(solution)/shard_map/ppermute | solution.py:520
  27.4 4.5 %collective-permute-start.8 = (f32[8,128]{1,0:T(8,128)S(1)}, f32[8,128]{1,0:T(8,128)S(1)}, u32[]{:S(2)}, u32[]{:S(2)}) collective-permute-start(f32[8,128]{1,0:T(8,128)S(1)} %slice_add_fusion), channel_id=1, source_target_pairs={{0,3},{1,2},{2,1},{3,0},{4,7},{5,6},{6,5},{7,4},{8,11},{9,10},{10,... | collective-permute-start | bytes 12296 | tf_op jit(solution)/shard_map/ppermute | solution.py:520
  31.9 7.3 %collective-permute-start.9 = (f32[264,128]{1,0:T(8,128)S(1)}, f32[264,128]{1,0:T(8,128)S(1)}, u32[]{:S(2)}, u32[]{:S(2)}) collective-permute-start(f32[264,128]{1,0:T(8,128)S(1)} %pad_maximum_fusion), channel_id=1, source_target_pairs={{0,24},{4,28},{8,16},{12,20},{16,8},{20,12},{24,0},{28,4},{1,25},{... | collective-permute-start | bytes 405512 | tf_op jit(solution)/shard_map/ppermute | solution.py:520
  34.7 4.0 %collective-permute-start.10 = (f32[8,128]{1,0:T(8,128)S(1)}, f32[8,128]{1,0:T(8,128)S(1)}, u32[]{:S(2)}, u32[]{:S(2)}) collective-permute-start(f32[8,128]{1,0:T(8,128)S(1)} %add_add_fusion.refs_10_), channel_id=1, source_target_pairs={{0,8},{4,12},{8,0},{12,4},{16,24},{20,28},{24,16},{28,20},{1,9},{5... | collective-permute-start | bytes 12296 | tf_op jit(solution)/shard_map/ppermute | solution.py:520
  34.7 4.5 %collective-permute-start.11 = (f32[8,128]{1,0:T(8,128)S(1)}, f32[8,128]{1,0:T(8,128)S(1)}, u32[]{:S(2)}, u32[]{:S(2)}) collective-permute-start(f32[8,128]{1,0:T(8,128)S(1)} %add_add_fusion.refs_10_), channel_id=1, source_target_pairs={{0,16},{4,20},{8,24},{12,28},{16,0},{20,4},{24,8},{28,12},{1,17},{... | collective-permute-start | bytes 12296 | tf_op jit(solution)/shard_map/ppermute | solution.py:520
  39.3 1.4 %collective-permute-start.12 = (f32[256,128]{1,0:T(8,128)S(1)}, f32[256,128]{1,0:T(8,128)S(1)}, u32[]{:S(2)}, u32[]{:S(2)}) collective-permute-start(f32[256,128]{1,0:T(8,128)S(1)} %get-tuple-element.151), channel_id=1, source_target_pairs={{0,4},{4,0},{8,12},{12,8},{16,20},{20,16},{24,28},{28,24},{1,5},{5... | collective-permute-start | bytes 393224 | tf_op jit(solution)/shard_map/ppermute | solution.py:520

commit v4 on v3

--- a/solution.py
+++ b/solution.py
@@ -189,12 +189,12 @@
     for head in (2 * pair, 2 * pair + 1):
         column = jnp.broadcast_to(table[:, head : head + 1], (tokens, tokens))
         parts.append(jnp.exp(column - cum_rows[head : head + 1] + mask))
-    return jnp.concatenate(parts, axis=0)
-
-
-def side_by_side(x):
-    rows = x.shape[0] // 2
-    return jnp.concatenate([x[:rows], x[rows:]], axis=1)
+    return jnp.concatenate(parts, axis=1)
+
+
+def one_above_other(x):
+    columns = x.shape[1] // 2
+    return jnp.concatenate([x[:, :columns], x[:, columns:]], axis=0)
 
 
 def pick_gains(gain_ref, half):
@@ -224,11 +224,11 @@
         lanes = pair_lanes(half, width, pair)
         query = query_ref[0, :, lanes]
         decay = pair_decays(table, cum_rows, mask, pair, tokens)
-        scores = dot(by_head(query, 0), key_ref[0, :, lanes], 1, 1) * decay
+        scores = dot(query, by_head(key_ref[0, :, lanes], 0), 1, 1) * decay
         weights = scores.astype(BF16)
         here = pl.ds(pair * LANES, LANES)
         grad_ref[:, here] = upstream_ref[0, :, lanes].astype(F32) * gains[pair : pair + 1]
-        out_ref[:, here] = dot(side_by_side(weights), by_head(value_ref[0, :, lanes], 0))
+        out_ref[:, here] = dot(weights, by_head(value_ref[0, :, lanes], 0))
         turned_ref[here, :] = jnp.transpose(query)
         entry_ref[:, here] = pair_columns(table, HEAD_TOTAL + 2 * pair, tokens)
 
@@ -247,6 +247,7 @@
     layer_ref,
     grad_mixed_ref,
     out_ref,
+    gain_part_ref,
 ):
     tokens, width = query_ref.shape[1:]
     half = own_half(mine)
@@ -299,8 +300,8 @@
         jnp.concatenate([blank, part], axis=0),
     )
     if before_ref is not None:
-        part = part + before_ref[pl.ds(PAIRS * 64, 8), :]
-    out_ref[pl.ds(PAIRS * 64, 8), :] = part
+        part = part + before_ref[...]
+    gain_part_ref[...] = part
 
 
 def backward_kernel(
@@ -312,69 +313,85 @@
     state_ref,
     entry_ref,
     table_ref,
-    layer_part_ref,
-    layer_ref,
     grad_query_ref,
     grad_key_ref,
     grad_value_ref,
     later_ref,
     leave_ref,
-    grad_query_part,
-    sent,
 ):
     tokens, width = query_ref.shape[1:]
     half = own_half(mine)
-    copies = [
-        pltpu.make_async_copy(
-            layer_part_ref, layer_ref.at[0, :, half_lanes(half, width)], sent.at[0]
-        )
-    ]
-    copies[0].start()
     table = pick_columns(table_ref[pl.ds(COLUMNS, 128), :], half)
     cum_rows = pick_rows(table_ref[pl.ds(CUM_ROWS, 16), :], half)
     mask = table_ref[pl.ds(MASK, 128), :]
     earlier = twice(triangle(tokens, lambda s, t: s < t).astype(F32).astype(BF16), 0)
     reached = triangle(tokens, lambda u, t: u >= t)
     chooser = twice(head_chooser(), 1)
-    balance_rows = []
-    entry_rows = []
-    for pair in range(PAIRS):
-        lanes = pair_lanes(half, width, pair)
-        here = pl.ds(pair * LANES, LANES)
-        query = query_ref[0, :, lanes]
-        key = key_ref[0, :, lanes]
-        value = value_ref[0, :, lanes]
-        grad_mixed = grad_mixed_ref[:, here]
-        query_rows = by_head(query, 0)
-        mixed_rows = by_head(grad_mixed, 0)
+    places = [pl.ds(pair * LANES, LANES) for pair in range(PAIRS)]
+    lanes = [pair_lanes(half, width, pair) for pair in range(PAIRS)]
+    balance_rows, entry_rows, carried = [], [], []
+    for pair in range(PAIRS):
+        state = by_head(state_ref[pl.ds(pair * 64, 64), :], 0)
+        grad_mixed = grad_mixed_ref[:, places[pair]]
+        carried.append(
+            entry_ref[:, places[pair]] * dot(twice(grad_mixed, 1), stacked(state, 1), 1, 1)
+        )
+        leave_ref[:, places[pair]] = pair_columns(table, 2 * HEAD_TOTAL + 2 * pair, tokens)
+    for pair in range(PAIRS):
+        query = query_ref[0, :, lanes[pair]]
+        grad_mixed = grad_mixed_ref[:, places[pair]]
+        key_rows = by_head(key_ref[0, :, lanes[pair]], 0)
         decay = pair_decays(table, cum_rows, mask, pair, tokens)
-        decayed_scores = dot(query_rows, key, 1, 1) * decay
-        grad_pairs = dot(mixed_rows, value, 1, 1)
+        decayed_scores = dot(query, key_rows, 1, 1) * decay
+        grad_pairs = dot(grad_mixed, by_head(value_ref[0, :, lanes[pair]], 0), 1, 1)
         weights = decayed_scores.astype(BF16)
         grad_weights = (grad_pairs * decay).astype(BF16)
-        state = by_head(state_ref[pl.ds(pair * 64, 64), :], 0)
-        carried = entry_ref[:, here] * dot(twice(grad_mixed, 1), stacked(state, 1), 1, 1)
-        grad_query_part[:, here] = (
-            dot(side_by_side(grad_weights), by_head(key, 0)) + carried
-        ).astype(BF16)
-        copies.append(
-            pltpu.make_async_copy(
-                grad_query_part.at[:, here], grad_query_ref.at[0, :, lanes], sent.at[1 + pair]
-            )
-        )
-        copies[-1].start()
-        grad_key_ref[:, here] = dot(grad_weights, query_rows, 0, 0)
-        grad_value_ref[:, here] = dot(weights, mixed_rows, 0, 0)
-        leave_ref[:, here] = pair_columns(table, 2 * HEAD_TOTAL + 2 * pair, tokens)
-        before = dot(stacked(decayed_scores * grad_pairs, 1), earlier)
+        grad_query_ref[:, places[pair]] = (dot(grad_weights, key_rows) + carried[pair]).astype(
+            BF16
+        )
+        grad_key_ref[:, places[pair]] = dot(
+            one_above_other(grad_weights), by_head(query, 0), 0, 0
+        )
+        grad_value_ref[:, places[pair]] = dot(
+            one_above_other(weights), by_head(grad_mixed, 0), 0, 0
+        )
+        terms = one_above_other(decayed_scores * grad_pairs)
+        before = dot(stacked(terms, 1), earlier)
         for head in range(2):
             part = before[head * tokens : (head + 1) * tokens]
             balance_rows.append(jnp.sum(jnp.where(reached, part, 0.0), axis=0, keepdims=True))
-        terms = dot(chooser, stacked(query.astype(F32) * carried, 1), 1, 1)
-        entry_rows.append(terms[:2])
+        entry_rows.append(dot(chooser, stacked(query.astype(F32) * carried[pair], 1), 1, 1)[:2])
     later_ref[...] = jnp.concatenate(balance_rows, axis=0) + row_sums(
         jnp.concatenate(entry_rows, axis=0), reached
     )
+
+
+def other_backward_kernel(*refs):
+    inputs, (layer_own, layer_other, query_own) = refs[:7], refs[7:10]
+    layer_ref, grad_query_ref = refs[10:12]
+    *outs, query_part, sent = refs[12:]
+    width = layer_ref.shape[2]
+    half = own_half(False)
+    own_lanes, lanes = half_lanes(own_half(True), width), half_lanes(half, width)
+    copies = [
+        pltpu.make_async_copy(source, target, sent.at[i])
+        for i, (source, target) in enumerate(
+            [
+                (layer_own, layer_ref.at[0, :, own_lanes]),
+                (layer_other, layer_ref.at[0, :, lanes]),
+                (query_own, grad_query_ref.at[0, :, own_lanes]),
+                (query_part, grad_query_ref.at[0, :, lanes]),
+            ]
+        )
+    ]
+
+    @pl.when(half >= 0)
+    def _():
+        for copy in copies[:3]:
+            copy.start()
+
+    backward_kernel(False, *inputs, query_part, *outs)
+    copies[3].start()
     for copy in copies:
         copy.wait()
 
@@ -396,7 +413,7 @@
     )
 
 
-def final_kernel(
+def final_parts(
     mine,
     key_ref,
     value_ref,
@@ -407,30 +424,11 @@
     state_ref,
     grad_ref,
     table_ref,
-    other_ref,
-    gain_refs,
-    grad_key_ref,
-    grad_value_ref,
-    rows_ref,
-    decay_ref,
-    gain_ref,
     key_out,
     value_out,
-    decay_out,
-    gain_out,
-    sent,
 ):
     tokens, width = key_ref.shape[1:]
     half = own_half(mine)
-    copies = []
-
-    def send(source, target):
-        copies.append(pltpu.make_async_copy(source, target, sent.at[len(copies)]))
-        copies[-1].start()
-
-    if gain_refs:
-        gain_out[...] = sum(ref[...] for ref in gain_refs[1:]) + gain_refs[0][...]
-        send(gain_out, gain_ref)
     carry = pick_rows(table_ref[pl.ds(CARRY_ROWS, 16), :], half)
     chooser = twice(head_chooser(), 1)
     left = left_lanes((1, LANES))
@@ -448,38 +446,68 @@
             grad_value_part_ref[:, places[pair]] + carried[pair]
         ).astype(BF16)
         terms.append(stacked(carried[pair] * value_ref[0, :, lanes[pair]].astype(F32), 1))
-    send(value_out, grad_value_ref.at[0, :, half_lanes(half, width)])
+    earlier = [dot(chooser, terms[pair], 1, 1)[:2] for pair in range(PAIRS)]
     key_parts = [
         dot(twice(value_ref[0, :, lanes[pair]], 1), jnp.concatenate(grads[pair], axis=1), 1, 1)
         for pair in range(PAIRS)
     ]
-    earlier = [dot(chooser, terms[pair], 1, 1)[:2] for pair in range(PAIRS)]
-    for pair in range(PAIRS):
-        key_out[:, places[pair]] = (
-            grad_key_part_ref[:, places[pair]] + leave_ref[:, places[pair]] * key_parts[pair]
-        ).astype(BF16)
-    send(key_out, grad_key_ref.at[0, :, half_lanes(half, width)])
     through_rows = []
     for pair in range(PAIRS):
         block = pl.ds(pair * 64, 64)
         product = jnp.sum(grad_ref[block, :] * state_ref[block, :], axis=0, keepdims=True)
         for side in (left, ~left):
             through_rows.append(jnp.sum(jnp.where(side, product, 0.0), axis=1, keepdims=True))
-    rows = (
+    for pair in range(PAIRS):
+        key_out[:, places[pair]] = (
+            grad_key_part_ref[:, places[pair]] + leave_ref[:, places[pair]] * key_parts[pair]
+        ).astype(BF16)
+    return (
         later_ref[...]
         + row_sums(jnp.concatenate(earlier, axis=0), triangle(tokens, lambda u, t: u < t))
         + carry * jnp.concatenate(through_rows, axis=0)
     )
-    if rows_ref is not None:
-        rows_ref[...] = rows
-    else:
-        other = other_ref[...]
-        decay_out[...] = jnp.where(
-            half == 0,
-            jnp.concatenate([rows, other], axis=0),
-            jnp.concatenate([other, rows], axis=0),
-        )
-        send(decay_out, decay_ref.at[0])
+
+
+def own_final_kernel(*refs):
+    *refs, rows_ref = refs
+    rows_ref[...] = final_parts(True, *refs)
+
+
+def other_final_kernel(*refs):
+    inputs, (key_own, value_own, other_ref, gain_part_ref) = refs[:9], refs[9:13]
+    grad_key_ref, grad_value_ref, decay_ref, gain_ref = refs[13:17]
+    *parts, decay_out, gain_out, sent = refs[17:]
+    width = grad_key_ref.shape[2]
+    half = own_half(False)
+    own_lanes, lanes = half_lanes(own_half(True), width), half_lanes(half, width)
+    pairs = [
+        (key_own, grad_key_ref.at[0, :, own_lanes]),
+        (value_own, grad_value_ref.at[0, :, own_lanes]),
+        (gain_out, gain_ref),
+        (parts[0], grad_key_ref.at[0, :, lanes]),
+        (parts[1], grad_value_ref.at[0, :, lanes]),
+        (decay_out, decay_ref.at[0]),
+    ]
+    copies = [
+        pltpu.make_async_copy(source, target, sent.at[i])
+        for i, (source, target) in enumerate(pairs)
+    ]
+    gain_out[...] = gain_part_ref[...] + inputs[7][pl.ds(PAIRS * 64, 2 * PAIRS), :]
+
+    @pl.when(half >= 0)
+    def _():
+        for copy in copies[:3]:
+            copy.start()
+
+    rows = final_parts(False, *inputs, *parts)
+    other = other_ref[...]
+    decay_out[...] = jnp.where(
+        half == 0,
+        jnp.concatenate([rows, other], axis=0),
+        jnp.concatenate([other, rows], axis=0),
+    )
+    for copy in copies[3:]:
+        copy.start()
     for copy in copies:
         copy.wait()
 
@@ -629,13 +657,18 @@
         if mine:
             kernel = lambda *refs: forward_kernel(True, *refs[:8], None, *refs[8:])
         else:
-            operands.append((query_states[True], VMEM))
+            operands.append((gain, VMEM))
             kernel = functools.partial(forward_kernel, False)
-        layer_parts[mine], grad_mixed[mine], query_states[mine] = call(
-            kernel, operands, [(part, BF16, VMEM), (part, BF16, VMEM), (buffer, F32, VMEM)]
-        )
-
-    outputs = {}
+        layer_parts[mine], grad_mixed[mine], query_states[mine], gain = call(
+            kernel,
+            operands,
+            [
+                (part, BF16, VMEM),
+                (part, BF16, VMEM),
+                ((state_rows, LANES), F32, VMEM),
+                ((2 * PAIRS, LANES), F32, VMEM),
+            ],
+        )
 
     def backward(mine, state):
         operands = blocks_of + [
@@ -643,63 +676,53 @@
             (state, VMEM),
             (mixed[mine][2], VMEM),
             (tables, VMEM),
-            (layer_parts[mine], VMEM),
         ]
-        aliases = {}
-        kernel = functools.partial(backward_kernel, mine)
-        if outputs:
-            kernel = lambda *refs: backward_kernel(mine, *refs[:8], *refs[10:])
-            operands += [(outputs["layer"], HBM), (outputs["query"], HBM)]
-            aliases = {8: 0, 9: 1}
-        outputs["layer"], outputs["query"], *local_parts = call(
-            kernel,
-            operands,
-            [
-                (whole, BF16, HBM),
-                (whole, BF16, HBM),
-                (part, F32, VMEM),
-                (part, F32, VMEM),
-                (rows, F32, VMEM),
-                (part, F32, VMEM),
-            ],
-            [pltpu.VMEM(part, BF16), pltpu.SemaphoreType.DMA((1 + PAIRS,))],
-            aliases,
-            flops=0,
-        )
-        return local_parts
-
+        results = [(part, F32, VMEM), (part, F32, VMEM), (rows, F32, VMEM), (part, F32, VMEM)]
+        if mine:
+            return call(
+                functools.partial(backward_kernel, True),
+                operands,
+                [(part, BF16, VMEM)] + results,
+            )
+        finished = (layer_parts[True], layer_parts[False], local_parts[True][0])
+        return call(
+            other_backward_kernel,
+            operands + [(x, VMEM) for x in finished],
+            [(whole, BF16, HBM), (whole, BF16, HBM)] + results,
+            [pltpu.VMEM(part, BF16), pltpu.SemaphoreType.DMA((4,))],
+        )
+
+    steps = []
+    step = scans // 2
+    while step:
+        steps.append(step)
+        step //= 2
     swapped = exchange(query_states[False], 1)
+    gains = [gain]
+    for step in steps[:1]:
+        larger = jnp.concatenate([gain, query_states[False][:24]], axis=0)
+        gains.append(exchange(larger, step, "dp")[: 2 * PAIRS])
     first_query, _ = parts(jnp.where(on_first, query_states[True], swapped))
     second_query, _ = parts(jnp.where(on_first, swapped, query_states[True]))
     total = flat(first_query + first_carry * second_query)
     suffix = jnp.zeros_like(first_query)
     suffix_carry = jnp.ones_like(carry)
-    gain = query_states[False][state_rows:] + swapped[state_rows:]
     local_parts = {}
-    gains = [gain]
     for bit, is_upper, carry, their_carry in levels:
         partner = 2 * bit - 2
         mine = not local_parts
         beside = len(local_parts) < 2
-        gain = sum(gains)
-        state = state_in[mine]
-        total, gain, state = lax.optimization_barrier((total, gain, state))
         if bit == 2:
+            total, state = lax.optimization_barrier((total, state_in[mine]))
             received = exchange(total, partner)
-            gains = [gain]
-            for k in range(1, min(4, scans)):
-                gains.append(exchange(gain, k, "dp"))
-            step = 4
-            while step < scans:
+            gain = sum(gains)
+            for step in steps[1:]:
+                gains = [gain, exchange(gain, step, "dp")]
                 gain = sum(gains)
-                gains = [gain] + [
-                    exchange(gain, k * step, "dp") for k in range(1, min(4, scans // step))
-                ]
-                step *= 4
             if len(levels) == 1:
-                gain = sum(gains)
                 gains = [gain, exchange(gain, partner)]
         else:
+            total, gain, state = lax.optimization_barrier((total, sum(gains), state_in[mine]))
             received = exchange(jnp.concatenate([total, gain], axis=0), partner)
             gains = [gain]
             if 2 * bit == blocks:
@@ -719,60 +742,66 @@
     for mine in (True, False):
         if mine not in local_parts:
             local_parts[mine] = backward(mine, state_in[mine])
+    if not levels:
+        gain = sum(gains)
+        for step in steps[1:]:
+            gain = gain + exchange(gain, step, "dp")
+        gains = [gain]
     before_second = second_query + second_carry * suffix
     state_grad = {True: flat(jnp.where(on_first, before_second, suffix))}
-    state_grad[False] = exchange(flat(jnp.where(on_first, suffix, before_second)), 1)
-
-    for mine in (True, False):
-        grad_key_part, grad_value_part, later, leave = local_parts[mine]
-        operands = [
-            (key_vectors, VMEM),
-            (value_vectors, VMEM),
-            (grad_key_part, VMEM),
-            (grad_value_part, VMEM),
-            (later, VMEM),
-            (leave, VMEM),
-            (state_in[mine], VMEM),
-            (state_grad[mine], VMEM),
-            (tables, VMEM),
+    gain = sum(gains)
+    swapped = exchange(
+        jnp.concatenate([flat(jnp.where(on_first, suffix, before_second)), gain], axis=0), 1
+    )
+    state_grad[False] = swapped
+
+    def final_operands(mine):
+        grad_key_part, grad_value_part, later, leave = local_parts[mine][-4:]
+        return [
+            (x, VMEM)
+            for x in (
+                key_vectors,
+                value_vectors,
+                grad_key_part,
+                grad_value_part,
+                later,
+                leave,
+                state_in[mine],
+                state_grad[mine],
+                tables,
+            )
         ]
-        results = [(whole, BF16, HBM), (whole, BF16, HBM)]
-        scratch = [pltpu.VMEM(part, BF16), pltpu.VMEM(part, BF16)]
-        if mine:
-            kernel = lambda *refs: final_kernel(
-                True, *refs[:9], None, [], *refs[9:12], None, None, *refs[12:14], None, None, refs[14]
-            )
-            aliases = None
-            results.append((rows, F32, VMEM))
-        else:
-            count = len(gains)
-            operands.append((decay_rows, VMEM))
-            operands += [(x, VMEM) for x in gains]
-            operands += [(grad_key, HBM), (grad_value, HBM)]
-            kernel = lambda *refs: final_kernel(
-                False,
-                *refs[:10],
-                refs[10 : 10 + count],
-                *refs[12 + count : 14 + count],
-                None,
-                *refs[14 + count :],
-            )
-            aliases = {10 + count: 0, 11 + count: 1}
-            results += [((1, HEAD_TOTAL, tokens), F32, HBM), ((2 * PAIRS, LANES), F32, HBM)]
-            scratch += [pltpu.VMEM((HEAD_TOTAL, tokens), F32), pltpu.VMEM((2 * PAIRS, LANES), F32)]
-        scratch.append(pltpu.SemaphoreType.DMA((4,)))
-        grad_key, grad_value, *rest = call(kernel, operands, results, scratch, aliases)
-        if mine:
-            (decay_rows,) = rest
-        else:
-            grad_decay, grad_gain = rest
-    grad_decay = jnp.swapaxes(grad_decay, 1, 2)
+
+    grad_key, grad_value, decay_rows = call(
+        own_final_kernel,
+        final_operands(True),
+        [(part, BF16, VMEM), (part, BF16, VMEM), (rows, F32, VMEM)],
+    )
+    finished = (grad_key, grad_value, decay_rows, gain)
+    grad_key, grad_value, grad_decay, grad_gain = call(
+        other_final_kernel,
+        final_operands(False) + [(x, VMEM) for x in finished],
+        [
+            (whole, BF16, HBM),
+            (whole, BF16, HBM),
+            ((1, HEAD_TOTAL, tokens), F32, HBM),
+            ((2 * PAIRS, LANES), F32, HBM),
+        ],
+        [
+            pltpu.VMEM(part, BF16),
+            pltpu.VMEM(part, BF16),
+            pltpu.VMEM((HEAD_TOTAL, tokens), F32),
+            pltpu.VMEM((2 * PAIRS, LANES), F32),
+            pltpu.SemaphoreType.DMA((6,)),
+        ],
+    )
+    layer_out, grad_query = local_parts[False][:2]
     return (
-        outputs["layer"],
-        outputs["query"],
+        layer_out,
+        grad_query,
         grad_key,
         grad_value,
-        grad_decay,
+        jnp.swapaxes(grad_decay, 1, 2),
         grad_gain.reshape(-1),
     )
 

time: 42 us -> 40.5 us (0.964)
  Pallas kernels: 11.1 us -> 10.3 us
    pallas_call x10, Pallas kernels: 11.1 us -> 10.3 us  [call(): pl.pallas_call(kernel, in_specs=[pl.BlockSpec(memory_space=memory) for a,...]
    ppermute x13 -> x12, starting transfers between devices: 18.1 us -> 17.7 us  [exchange(): return lax.ppermute(x, axis, [(i, i ^ bit) for i in range(size)])]
    ppermute x13 -> x12, waiting for transfers between devices: 11.2 us -> 10.9 us  [exchange(): return lax.ppermute(x, axis, [(i, i ^ bit) for i in range(size)])]
  transfers between devices with their start and end apart: 13 -> 12, of which waited for: 9 -> 8; matrix products, arithmetic and copies ran while one was open for 0% -> 0% of each run, Pallas kernels for 18% -> 16%
where the time goes in v4:
time: 40.5 us; the launch traced here: 40.3 us
  starting transfers between devices  17.7 us (44%)
  waiting for transfers between devices  10.9 us (27%)
  Pallas kernels  10.3 us (25%)
  between operations  0.84 us (2%)
  other arithmetic  0.47 us (1%)
    ppermute x12, starting transfers between devices, exchange(): return lax.ppermute(x, axis, [(i, i ^ bit) for i in range(size)])  17.7 us
    ppermute x12, waiting for transfers between devices, exchange(): return lax.ppermute(x, axis, [(i, i ^ bit) for i in range(size)])  10.9 us
    pallas_call x10, Pallas kernels, call(): pl.pallas_call(kernel, in_specs=[pl.BlockSpec(memory_space=memory) for a,...  10.3 us
  transfers between devices with their start and end apart: 12, of which 8 were waited for; matrix products, arithmetic and copies ran while one was open for 0% of the time, Pallas kernels for 16%

profile of v4, /device:TPU:0, one launch (start us, length us, event | category | flops | bytes accessed | tf_op | source)
XLA Modules:
  0.0 40.3 jit_solution(11143408402969082820)
XLA Ops:
  0.7 1.7 %shard_map.118 = (f32[264,128]{1,0:T(8,128)S(1)}, f32[288,128]{1,0:T(8,128)S(1)}) custom-call(bf16[1,128,1024]{2,1,0:T(8,128)(2,1)} %refs_0_.5, bf16[1,128,1024]{2,1,0:T(8,128)(2,1)} %refs_1_.5, f32[1,16,128]{2,1,0:T(8,128)} %bitcast.68, s32[1,128]{1,0:T(1,128)} %restart_ref.1), custom_call_target="tpu_custom_call" | custom-call | tf_op jit(solution)/shard_map/pallas_call | solution.py:520
  2.4 0.5 %collective-permute-start = (f32[264,128]{1,0:T(8,128)S(1)}, f32[264,128]{1,0:T(8,128)S(1)}, u32[]{:S(2)}, u32[]{:S(2)}) collective-permute-start(f32[264,128]{1,0:T(8,128)S(1)} %get-tuple-element.79), channel_id=1, source_target_pairs={{0,4},{4,0},{8,12},{12,8},{16,20},{20,16},{24,28},{28,24},{1,5},{5... | collective-permute-start | bytes 405512 | tf_op jit(solution)/shard_map/ppermute | solution.py:548
  2.9 0.5 %shard_map.119 = f32[264,128]{1,0:T(8,128)S(1)} custom-call(bf16[1,128,1024]{2,1,0:T(8,128)(2,1)S(1)} %copy-done, bf16[1,128,1024]{2,1,0:T(8,128)(2,1)S(1)} %copy-done.1, f32[288,128]{1,0:T(8,128)S(1)} %get-tuple-element.93.table_ref.refs_6_.refs_8_), custom_call_target="tpu_custom_call" | custom-call | bytes 671744 | tf_op jit(solution)/shard_map/pallas_call | solution.py:520
  4.1 3.0 %collective-permute-start.1 = (f32[264,128]{1,0:T(8,128)S(1)}, f32[264,128]{1,0:T(8,128)S(1)}, u32[]{:S(2)}, u32[]{:S(2)}) collective-permute-start(f32[264,128]{1,0:T(8,128)S(1)} %maximum_maximum_fusion), channel_id=1, source_target_pairs={{0,8},{4,12},{8,0},{12,4},{16,24},{20,28},{24,16},{28,20},{1,9},{5... | collective-permute-start | bytes 405512 | tf_op jit(solution)/shard_map/ppermute | solution.py:548
  7.1 0.6 %shard_map.120 = (f32[128,512]{1,0:T(8,128)S(1)}, bf16[512,128]{1,0:T(8,128)(2,1)S(1)}, f32[128,512]{1,0:T(8,128)S(1)}, f32[128,512]{1,0:T(8,128)S(1)}) custom-call(bf16[1,128,1024]{2,1,0:T(8,128)(2,1)S(1)} %copy-done.2, bf16[1,128,1024]{2,1,0:T(8,128)(2,1)S(1)} %copy-done, bf16[1,128,1024]{2,1,0:T(8,128)(2,1)S(1)} %copy-done.1, ...), custom_call_target="tpu_custom_call" | custom-call | bytes 1200128 | tf_op jit(solution)/shard_map/pallas_call | solution.py:520
  7.6 3.3 %collective-permute-done.1 = f32[264,128]{1,0:T(8,128)S(1)} collective-permute-done((f32[264,128]{1,0:T(8,128)S(1)}, f32[264,128]{1,0:T(8,128)S(1)}, u32[]{:S(2)}, u32[]{:S(2)}) %collective-permute-start.1) | collective-permute-done | bytes 135200 | tf_op jit(solution)/shard_map/ppermute | solution.py:548
  11.1 3.8 %collective-permute-start.2 = (f32[264,128]{1,0:T(8,128)S(1)}, f32[264,128]{1,0:T(8,128)S(1)}, u32[]{:S(2)}, u32[]{:S(2)}) collective-permute-start(f32[264,128]{1,0:T(8,128)S(1)} %maximum_maximum_fusion.1), channel_id=1, source_target_pairs={{0,24},{4,28},{8,16},{12,20},{16,8},{20,12},{24,0},{28,4},{1,25},{... | collective-permute-start | bytes 405512 | tf_op jit(solution)/shard_map/ppermute | solution.py:548
  14.9 0.6 %shard_map.121 = (f32[128,512]{1,0:T(8,128)S(1)}, bf16[512,128]{1,0:T(8,128)(2,1)S(1)}, f32[128,512]{1,0:T(8,128)S(1)}, f32[128,512]{1,0:T(8,128)S(1)}) custom-call(bf16[1,128,1024]{2,1,0:T(8,128)(2,1)S(1)} %copy-done.2, bf16[1,128,1024]{2,1,0:T(8,128)(2,1)S(1)} %copy-done, bf16[1,128,1024]{2,1,0:T(8,128)(2,1)S(1)} %copy-done.1, ...), custom_call_target="tpu_custom_call" | custom-call | bytes 1200128 | tf_op jit(solution)/shard_map/pallas_call | solution.py:520
  15.5 2.7 %collective-permute-done.2 = f32[264,128]{1,0:T(8,128)S(1)} collective-permute-done((f32[264,128]{1,0:T(8,128)S(1)}, f32[264,128]{1,0:T(8,128)S(1)}, u32[]{:S(2)}, u32[]{:S(2)}) %collective-permute-start.2) | collective-permute-done | bytes 135200 | tf_op jit(solution)/shard_map/ppermute | solution.py:548
  18.3 0.7 %shard_map.122 = (bf16[128,512]{1,0:T(8,128)(2,1)S(1)}, bf16[128,512]{1,0:T(8,128)(2,1)S(1)}, f32[256,128]{1,0:T(8,128)S(1)}, f32[8,128]{1,0:T(8,128)S(1)}) custom-call(f32[128,512]{1,0:T(8,128)S(1)} %get-tuple-element.87.refs_0_, bf16[512,128]{1,0:T(8,128)(2,1)S(1)} %get-tuple-element.88.refs_1_, f32[128,512]{1,0:T(8,128)S(1)} %get-tuple-element.89.refs_2_.entry_ref, ...), custom_call_target="tpu_custom_call" | custom-call | bytes 1576960 | tf_op jit(solution)/shard_map/pallas_call | solution.py:520
  19.1 0.6 %collective-permute-done.3.state_ref.refs_4_.refs_6_ = f32[256,128]{1,0:T(8,128)S(1)} collective-permute-done((f32[256,128]{1,0:T(8,128)S(1)}, f32[256,128]{1,0:T(8,128)S(1)}, u32[]{:S(2)}, u32[]{:S(2)}) %collective-permute-start.3) | collective-permute-done | bytes 131104 | tf_op jit(solution)/shard_map/ppermute | solution.py:548
  19.7 0.7 %shard_map.123 = (bf16[128,512]{1,0:T(8,128)(2,1)S(1)}, bf16[128,512]{1,0:T(8,128)(2,1)S(1)}, f32[256,128]{1,0:T(8,128)S(1)}, f32[8,128]{1,0:T(8,128)S(1)}) custom-call(f32[128,512]{1,0:T(8,128)S(1)} %get-tuple-element.100.mixed_ref, bf16[512,128]{1,0:T(8,128)(2,1)S(1)} %get-tuple-element.101.turned_ref, ...), custom_call_target="tpu_custom_call" | custom-call | bytes 1581056 | tf_op jit(solution)/shard_map/pallas_call | solution.py:520
  20.6 1.5 %collective-permute-start.6 = (f32[32,128]{1,0:T(8,128)S(1)}, f32[32,128]{1,0:T(8,128)S(1)}, u32[]{:S(2)}, u32[]{:S(2)}) collective-permute-start(f32[32,128]{1,0:T(8,128)S(1)} %pad_maximum_fusion.2), channel_id=1, source_target_pairs={{0,2},{1,3},{2,0},{3,1},{4,6},{5,7},{6,4},{7,5},{8,10},{9,11},{10,... | collective-permute-start | bytes 49160 | tf_op jit(solution)/shard_map/ppermute | solution.py:548
  22.2 2.5 %collective-permute-start.5 = (f32[256,128]{1,0:T(8,128)S(1)}, f32[256,128]{1,0:T(8,128)S(1)}, u32[]{:S(2)}, u32[]{:S(2)}) collective-permute-start(f32[256,128]{1,0:T(8,128)S(1)} %fusion.13), channel_id=1, source_target_pairs={{0,8},{4,12},{8,0},{12,4},{16,24},{20,28},{24,16},{28,20},{1,9},{5... | collective-permute-start | bytes 393224 | tf_op jit(solution)/shard_map/ppermute | solution.py:548
  24.7 1.5 %collective-permute-start.7 = (f32[8,128]{1,0:T(8,128)S(1)}, f32[8,128]{1,0:T(8,128)S(1)}, u32[]{:S(2)}, u32[]{:S(2)}) collective-permute-start(f32[8,128]{1,0:T(8,128)S(1)} %slice_add_fusion), channel_id=1, source_target_pairs={{0,1},{1,0},{2,3},{3,2},{4,5},{5,4},{6,7},{7,6},{8,9},{9,8},{10,11... | collective-permute-start | bytes 12296 | tf_op jit(solution)/shard_map/ppermute | solution.py:548
  26.2 1.5 %shard_map.124 = (bf16[128,512]{1,0:T(8,128)(2,1)S(1)}, f32[128,512]{1,0:T(8,128)S(1)}, f32[128,512]{1,0:T(8,128)S(1)}, f32[8,128]{1,0:T(8,128)S(1)}, f32[128,512]{1,0:T(8,128)S(1)}) custom-call(bf16[1,128,1024]{2,1,0:T(8,128)(2,1)S(1)} %copy-done.2, bf16[1,128,1024]{2,1,0:T(8,128)(2,1)S(1)} %copy-done, bf16[1,128,1024]{2,1,0:T(8,128)(2,1)S(1)} %copy-done.1, ...), custom_call_target="tpu_custom_call" | custom-call | bytes 1458176 | tf_op jit(solution)/shard_map/pallas_call | solution.py:520
  27.7 0.6 %collective-permute-done.7 = f32[8,128]{1,0:T(8,128)S(1)} collective-permute-done((f32[8,128]{1,0:T(8,128)S(1)}, f32[8,128]{1,0:T(8,128)S(1)}, u32[]{:S(2)}, u32[]{:S(2)}) %collective-permute-start.7) | collective-permute-done | bytes 4128 | tf_op jit(solution)/shard_map/ppermute | solution.py:548
  28.5 3.3 %collective-permute-start.8 = (f32[264,128]{1,0:T(8,128)S(1)}, f32[264,128]{1,0:T(8,128)S(1)}, u32[]{:S(2)}, u32[]{:S(2)}) collective-permute-start(f32[264,128]{1,0:T(8,128)S(1)} %pad_maximum_fusion), channel_id=1, source_target_pairs={{0,24},{4,28},{8,16},{12,20},{16,8},{20,12},{24,0},{28,4},{1,25},{... | collective-permute-start | bytes 405512 | tf_op jit(solution)/shard_map/ppermute | solution.py:548
  32.0 0.9 %collective-permute-start.9 = (f32[8,128]{1,0:T(8,128)S(1)}, f32[8,128]{1,0:T(8,128)S(1)}, u32[]{:S(2)}, u32[]{:S(2)}) collective-permute-start(f32[8,128]{1,0:T(8,128)S(1)} %add.69), channel_id=1, source_target_pairs={{0,8},{4,12},{8,0},{12,4},{16,24},{20,28},{24,16},{28,20},{1,9},{5... | collective-permute-start | bytes 12296 | tf_op jit(solution)/shard_map/ppermute | solution.py:548
  32.9 2.3 %shard_map.125 = (bf16[1,128,1024]{2,1,0:T(8,128)(2,1)}, bf16[1,128,1024]{2,1,0:T(8,128)(2,1)}, f32[128,512]{1,0:T(8,128)S(1)}, f32[128,512]{1,0:T(8,128)S(1)}, ...) custom-call(bf16[1,128,1024]{2,1,0:T(8,128)(2,1)S(1)} %copy-done.2, bf16[1,128,1024]{2,1,0:T(8,128)(2,1)S(1)} %copy-done, ...), custom_call_target="tpu_custom_call" | custom-call | bytes 1851392 | tf_op jit(solution)/shard_map/pallas_call | solution.py:520
  35.2 2.4 %collective-permute-done.10 = f32[8,128]{1,0:T(8,128)S(1)} collective-permute-done((f32[8,128]{1,0:T(8,128)S(1)}, f32[8,128]{1,0:T(8,128)S(1)}, u32[]{:S(2)}, u32[]{:S(2)}) %collective-permute-start.10) | collective-permute-done | bytes 4128 | tf_op jit(solution)/shard_map/ppermute | solution.py:548
  37.7 0.5 %shard_map.126 = (bf16[128,512]{1,0:T(8,128)(2,1)S(1)}, bf16[128,512]{1,0:T(8,128)(2,1)S(1)}, f32[8,128]{1,0:T(8,128)S(1)}) custom-call(bf16[1,128,1024]{2,1,0:T(8,128)(2,1)S(1)} %copy-done, bf16[1,128,1024]{2,1,0:T(8,128)(2,1)S(1)} %copy-done.1, f32[128,512]{1,0:T(8,128)S(1)} %get-tuple-element.141.refs_2_, f32[128,512]{1,0:T(8,128)S(1)} %get-tuple-element.142.refs_3_, ...), custom_call_target="tpu_custom_call" | custom-call | bytes 1724416 | tf_op jit(solution)/shard_map/pallas_call | solution.py:520
  38.2 0.8 %collective-permute-done.11.refs_7_ = f32[264,128]{1,0:T(8,128)S(1)} collective-permute-done((f32[264,128]{1,0:T(8,128)S(1)}, f32[264,128]{1,0:T(8,128)S(1)}, u32[]{:S(2)}, u32[]{:S(2)}) %collective-permute-start.11) | collective-permute-done | bytes 135200 | tf_op jit(solution)/shard_map/ppermute | solution.py:548
  39.1 1.3 %shard_map.127 = (bf16[1,128,1024]{2,1,0:T(8,128)(2,1)}, bf16[1,128,1024]{2,1,0:T(8,128)(2,1)}, f32[1,16,128]{2,1,0:T(8,128)}, f32[8,128]{1,0:T(8,128)}) custom-call(bf16[1,128,1024]{2,1,0:T(8,128)(2,1)S(1)} %copy-done, bf16[1,128,1024]{2,1,0:T(8,128)(2,1)S(1)} %copy-done.1, f32[128,512]{1,0:T(8,128)S(1)} %get-tuple-element.133.refs_2_, ...), custom_call_target="tpu_custom_call" | custom-call | bytes 1998848 | tf_op jit(solution)/shard_map/pallas_call | solution.py:520
  (40 shorter events, 1.7 us)
Async XLA Ops:
  0.6 2.2 %copy-start = (bf16[1,128,1024]{2,1,0:T(8,128)(2,1)S(1)}, bf16[1,128,1024]{2,1,0:T(8,128)(2,1)}, u32[]{:S(2)}) copy-start(bf16[1,128,1024]{2,1,0:T(8,128)(2,1)} %refs_0_.5) | copy-start | bytes 786436
  0.6 2.2 %copy-start.1 = (bf16[1,128,1024]{2,1,0:T(8,128)(2,1)S(1)}, bf16[1,128,1024]{2,1,0:T(8,128)(2,1)}, u32[]{:S(2)}) copy-start(bf16[1,128,1024]{2,1,0:T(8,128)(2,1)} %refs_1_.5) | copy-start | bytes 786436
  2.4 1.5 %collective-permute-start = (f32[264,128]{1,0:T(8,128)S(1)}, f32[264,128]{1,0:T(8,128)S(1)}, u32[]{:S(2)}, u32[]{:S(2)}) collective-permute-start(f32[264,128]{1,0:T(8,128)S(1)} %get-tuple-element.79), channel_id=1, source_target_pairs={{0,4},{4,0},{8,12},{12,8},{16,20},{20,16},{24,28},{28,24},{1,5},{5... | collective-permute-start | bytes 405512 | tf_op jit(solution)/shard_map/ppermute | solution.py:548
  3.9 3.2 %copy-start.2 = (bf16[1,128,1024]{2,1,0:T(8,128)(2,1)S(1)}, bf16[1,128,1024]{2,1,0:T(8,128)(2,1)}, u32[]{:S(2)}) copy-start(bf16[1,128,1024]{2,1,0:T(8,128)(2,1)} %refs_0_.3) | copy-start | bytes 786436
  3.9 3.2 %copy-start.3 = (bf16[1,128,1024]{2,1,0:T(8,128)(2,1)S(1)}, bf16[1,128,1024]{2,1,0:T(8,128)(2,1)}, u32[]{:S(2)}) copy-start(bf16[1,128,1024]{2,1,0:T(8,128)(2,1)} %upstream_ref.5) | copy-start | bytes 786436
  4.1 3.0 %copy-start.4 = (f32[1024]{0:T(1024)S(1)}, f32[1024]{0:T(1024)}, u32[]{:S(2)}) copy-start(f32[1024]{0:T(1024)} %param.12) | copy-start | bytes 12292
  4.1 6.9 %collective-permute-start.1 = (f32[264,128]{1,0:T(8,128)S(1)}, f32[264,128]{1,0:T(8,128)S(1)}, u32[]{:S(2)}, u32[]{:S(2)}) collective-permute-start(f32[264,128]{1,0:T(8,128)S(1)} %maximum_maximum_fusion), channel_id=1, source_target_pairs={{0,8},{4,12},{8,0},{12,4},{16,24},{20,28},{24,16},{28,20},{1,9},{5... | collective-permute-start | bytes 405512 | tf_op jit(solution)/shard_map/ppermute | solution.py:548
  11.1 7.1 %collective-permute-start.2 = (f32[264,128]{1,0:T(8,128)S(1)}, f32[264,128]{1,0:T(8,128)S(1)}, u32[]{:S(2)}, u32[]{:S(2)}) collective-permute-start(f32[264,128]{1,0:T(8,128)S(1)} %maximum_maximum_fusion.1), channel_id=1, source_target_pairs={{0,24},{4,28},{8,16},{12,20},{16,8},{20,12},{24,0},{28,4},{1,25},{... | collective-permute-start | bytes 405512 | tf_op jit(solution)/shard_map/ppermute | solution.py:548
  18.3 1.4 %collective-permute-start.3 = (f32[256,128]{1,0:T(8,128)S(1)}, f32[256,128]{1,0:T(8,128)S(1)}, u32[]{:S(2)}, u32[]{:S(2)}) collective-permute-start(f32[256,128]{1,0:T(8,128)S(1)} %get-tuple-element.154), channel_id=1, source_target_pairs={{0,4},{4,0},{8,12},{12,8},{16,20},{20,16},{24,28},{28,24},{1,5},{5... | collective-permute-start | bytes 393224 | tf_op jit(solution)/shard_map/ppermute | solution.py:548
  20.4 1.7 %collective-permute-start.4 = (f32[256,128]{1,0:T(8,128)S(1)}, f32[256,128]{1,0:T(8,128)S(1)}, u32[]{:S(2)}, u32[]{:S(2)}) collective-permute-start(f32[256,128]{1,0:T(8,128)S(1)} %get-tuple-element.105), channel_id=1, source_target_pairs={{0,4},{4,0},{8,12},{12,8},{16,20},{20,16},{24,28},{28,24},{1,5},{5... | collective-permute-start | bytes 393224 | tf_op jit(solution)/shard_map/ppermute | solution.py:548
  20.6 4.0 %collective-permute-start.6 = (f32[32,128]{1,0:T(8,128)S(1)}, f32[32,128]{1,0:T(8,128)S(1)}, u32[]{:S(2)}, u32[]{:S(2)}) collective-permute-start(f32[32,128]{1,0:T(8,128)S(1)} %pad_maximum_fusion.2), channel_id=1, source_target_pairs={{0,2},{1,3},{2,0},{3,1},{4,6},{5,7},{6,4},{7,5},{8,10},{9,11},{10,... | collective-permute-start | bytes 49160 | tf_op jit(solution)/shard_map/ppermute | solution.py:548
  22.2 6.2 %collective-permute-start.5 = (f32[256,128]{1,0:T(8,128)S(1)}, f32[256,128]{1,0:T(8,128)S(1)}, u32[]{:S(2)}, u32[]{:S(2)}) collective-permute-start(f32[256,128]{1,0:T(8,128)S(1)} %fusion.13), channel_id=1, source_target_pairs={{0,8},{4,12},{8,0},{12,4},{16,24},{20,28},{24,16},{28,20},{1,9},{5... | collective-permute-start | bytes 393224 | tf_op jit(solution)/shard_map/ppermute | solution.py:548
  24.7 3.6 %collective-permute-start.7 = (f32[8,128]{1,0:T(8,128)S(1)}, f32[8,128]{1,0:T(8,128)S(1)}, u32[]{:S(2)}, u32[]{:S(2)}) collective-permute-start(f32[8,128]{1,0:T(8,128)S(1)} %slice_add_fusion), channel_id=1, source_target_pairs={{0,1},{1,0},{2,3},{3,2},{4,5},{5,4},{6,7},{7,6},{8,9},{9,8},{10,11... | collective-permute-start | bytes 12296 | tf_op jit(solution)/shard_map/ppermute | solution.py:548
  28.5 9.1 %collective-permute-start.8 = (f32[264,128]{1,0:T(8,128)S(1)}, f32[264,128]{1,0:T(8,128)S(1)}, u32[]{:S(2)}, u32[]{:S(2)}) collective-permute-start(f32[264,128]{1,0:T(8,128)S(1)} %pad_maximum_fusion), channel_id=1, source_target_pairs={{0,24},{4,28},{8,16},{12,20},{16,8},{20,12},{24,0},{28,4},{1,25},{... | collective-permute-start | bytes 405512 | tf_op jit(solution)/shard_map/ppermute | solution.py:548
  31.7 5.8 %collective-permute-start.10 = (f32[8,128]{1,0:T(8,128)S(1)}, f32[8,128]{1,0:T(8,128)S(1)}, u32[]{:S(2)}, u32[]{:S(2)}) collective-permute-start(f32[8,128]{1,0:T(8,128)S(1)} %add.69), channel_id=1, source_target_pairs={{0,16},{4,20},{8,24},{12,28},{16,0},{20,4},{24,8},{28,12},{1,17},{... | collective-permute-start | bytes 12296 | tf_op jit(solution)/shard_map/ppermute | solution.py:548
  32.0 5.6 %collective-permute-start.9 = (f32[8,128]{1,0:T(8,128)S(1)}, f32[8,128]{1,0:T(8,128)S(1)}, u32[]{:S(2)}, u32[]{:S(2)}) collective-permute-start(f32[8,128]{1,0:T(8,128)S(1)} %add.69), channel_id=1, source_target_pairs={{0,8},{4,12},{8,0},{12,4},{16,24},{20,28},{24,16},{28,20},{1,9},{5... | collective-permute-start | bytes 12296 | tf_op jit(solution)/shard_map/ppermute | solution.py:548
  37.6 1.4 %collective-permute-start.11 = (f32[264,128]{1,0:T(8,128)S(1)}, f32[264,128]{1,0:T(8,128)S(1)}, u32[]{:S(2)}, u32[]{:S(2)}) collective-permute-start(f32[264,128]{1,0:T(8,128)S(1)} %pad_maximum_fusion.1), channel_id=1, source_target_pairs={{0,4},{4,0},{8,12},{12,8},{16,20},{20,16},{24,28},{28,24},{1,5},{5... | collective-permute-start | bytes 405512 | tf_op jit(solution)/shard_map/ppermute | solution.py:548

commit v5 on v4

--- a/solution.py
+++ b/solution.py
@@ -14,7 +14,7 @@
 VMEM_BYTES = 12 * 1024 * 1024
 F32 = jnp.float32
 BF16 = jnp.bfloat16
-COLUMNS, MASK, CUM_ROWS, CARRY_ROWS, TABLE_ROWS = 0, 128, 256, 272, 288
+COLUMNS, CUM_ROWS, CARRY_ROWS, RESET_ROWS, TABLE_ROWS = 0, 128, 144, 160, 168
 
 
 def dot(a, b, contract_a=1, contract_b=0):
@@ -67,29 +67,26 @@
 
 def make_tables(decay_rows, restart):
     heads, tokens = decay_rows.shape
-    lower = triangle(tokens, lambda t, s: s <= t).astype(F32).astype(BF16)
-    upper = triangle(tokens, lambda t, s: t <= s).astype(F32).astype(BF16)
-    marks = jnp.broadcast_to(restart.astype(F32), (tokens, tokens)).astype(BF16)
-    resets_column = dot(lower, marks, 1, 1)
-    resets_row = dot(marks, upper)
-    cum_rows = row_sums(decay_rows, triangle(tokens, lambda s, t: s <= t))
-    cum = jnp.transpose(
-        jnp.concatenate([cum_rows, jnp.zeros((LANES - heads, tokens), F32)], axis=0)
-    )
-    last = cum[tokens - 1 :, :]
-    last_reset = resets_column[tokens - 1 :, :]
-    entry = jnp.where(resets_column == 0.0, jnp.exp(cum), 0.0)
-    leave = jnp.where(resets_column == last_reset, jnp.exp(last - cum), 0.0)
-    lane = lax.broadcasted_iota(jnp.int32, (tokens, LANES), 1)
-    columns = jnp.where(
-        lane < heads,
-        cum,
-        jnp.where(lane < 2 * heads, pltpu.roll(entry, heads, 1), pltpu.roll(leave, 2 * heads, 1)),
-    )
-    allowed = triangle(tokens, lambda t, s: t >= s) & (resets_column == resets_row)
-    mask = jnp.where(allowed, 0.0, -1e30)
-    carry = jnp.where(last_reset[:, :1] == 0.0, jnp.exp(cum_rows[:, tokens - 1 :]), 0.0)
-    return columns, mask, cum_rows, jnp.broadcast_to(carry, (heads, LANES))
+    marks = jnp.broadcast_to(restart.astype(F32), (8, tokens))
+    sums = row_sums(
+        jnp.concatenate([decay_rows, marks], axis=0), triangle(tokens, lambda s, t: s <= t)
+    )
+    cum, resets = sums[:heads], sums[heads:]
+    last, last_reset = cum[:, tokens - 1 :], resets[:1, tokens - 1 :]
+    entry = jnp.where(resets[:1] == 0.0, jnp.exp(cum), 0.0)
+    leave = jnp.where(resets[:1] == last_reset, jnp.exp(last - cum), 0.0)
+    carry = jnp.where(last_reset == 0.0, jnp.exp(last), 0.0)
+    rows = [cum, entry, leave, resets]
+    rows.append(jnp.zeros((LANES - sum(x.shape[0] for x in rows), tokens), F32))
+    columns = jnp.transpose(jnp.concatenate(rows, axis=0))
+    return columns, cum, jnp.broadcast_to(carry, (heads, LANES)), resets
+
+
+def make_mask(columns, resets):
+    tokens = columns.shape[0]
+    column = jnp.broadcast_to(columns[:, 3 * HEAD_TOTAL : 3 * HEAD_TOTAL + 1], (tokens, tokens))
+    allowed = triangle(tokens, lambda t, s: t >= s) & (column == resets[:1])
+    return jnp.where(allowed, 0.0, -1e30)
 
 
 def pick_columns(columns, half):
@@ -112,6 +109,14 @@
 
 def pair_lanes(half, width, pair):
     return pl.ds(pl.multiple_of(half * (width // 2) + pair * LANES, LANES), LANES)
+
+
+def once(half, work):
+    def step(i, carry):
+        work()
+        return carry
+
+    lax.fori_loop(0, 1 + (half >> 1), step, 0)
 
 
 def write_states(half, columns, carry_rows, keys, values, out_ref):
@@ -143,35 +148,45 @@
     restart_ref,
     out_ref,
     table_ref,
-    keys,
-    values,
+    keys_ref,
+    values_ref,
     decays,
     restarts,
     arrived,
 ):
     half = own_half(False)
-    lanes = half_lanes(half, key_ref.shape[2])
-    decay_copy = pltpu.make_async_copy(decay_ref.at[0], decays, arrived.at[2])
-    restart_copy = pltpu.make_async_copy(restart_ref, restarts, arrived.at[3])
-    value_copy = pltpu.make_async_copy(value_ref.at[0, :, lanes], values, arrived.at[1])
-    key_copy = pltpu.make_async_copy(key_ref.at[0, :, lanes], keys, arrived.at[0])
+    width = key_ref.shape[2]
+    lanes, later_lanes = half_lanes(half, width), half_lanes(own_half(True), width)
+    decay_copy = pltpu.make_async_copy(decay_ref.at[0], decays, arrived.at[4])
+    restart_copy = pltpu.make_async_copy(restart_ref, restarts, arrived.at[5])
+    copies = [
+        pltpu.make_async_copy(
+            source.at[0, :, place], target.at[0, :, place], arrived.at[2 * first + i]
+        )
+        for first, place in enumerate((lanes, later_lanes))
+        for i, (source, target) in enumerate(((value_ref, values_ref), (key_ref, keys_ref)))
+    ]
     decay_copy.start()
     restart_copy.start()
-    value_copy.start()
-    key_copy.start()
+    for copy in copies:
+        copy.start()
     decay_copy.wait()
     restart_copy.wait()
-    columns, mask, cum_rows, carry_rows = make_tables(decays[...], restarts[...])
+    columns, cum_rows, carry_rows, reset_rows = make_tables(decays[...], restarts[...])
     table_ref[pl.ds(COLUMNS, 128), :] = columns
-    table_ref[pl.ds(MASK, 128), :] = mask
     table_ref[pl.ds(CUM_ROWS, 16), :] = cum_rows
     table_ref[pl.ds(CARRY_ROWS, 16), :] = carry_rows
-    value_copy.wait()
-    key_copy.wait()
-    write_states(half, columns, carry_rows, keys[...], values[...], out_ref)
-
-
-def second_state_kernel(key_ref, value_ref, table_ref, out_ref):
+    table_ref[pl.ds(RESET_ROWS, 8), :] = reset_rows
+    for copy in copies[:2]:
+        copy.wait()
+    write_states(
+        half, columns, carry_rows, keys_ref[0, :, lanes], values_ref[0, :, lanes], out_ref
+    )
+    for copy in copies[2:]:
+        copy.wait()
+
+
+def second_state_kernel(key_ref, value_ref, table_ref, out_ref, mask_ref):
     half = own_half(True)
     lanes = half_lanes(half, key_ref.shape[2])
     write_states(
@@ -182,6 +197,9 @@
         value_ref[0, :, lanes],
         out_ref,
     )
+    mask_ref[...] = make_mask(
+        table_ref[pl.ds(COLUMNS, 128), :], table_ref[pl.ds(RESET_ROWS, 8), :]
+    )
 
 
 def pair_decays(table, cum_rows, mask, pair, tokens):
@@ -209,6 +227,7 @@
     upstream_ref,
     gain_ref,
     table_ref,
+    mask_ref,
     out_ref,
     turned_ref,
     entry_ref,
@@ -218,7 +237,7 @@
     half = own_half(mine)
     table = pick_columns(table_ref[pl.ds(COLUMNS, 128), :], half)
     cum_rows = pick_rows(table_ref[pl.ds(CUM_ROWS, 16), :], half)
-    mask = table_ref[pl.ds(MASK, 128), :]
+    mask = mask_ref[...]
     gains = pick_gains(gain_ref, half)
     for pair in range(PAIRS):
         lanes = pair_lanes(half, width, pair)
@@ -247,7 +266,6 @@
     layer_ref,
     grad_mixed_ref,
     out_ref,
-    gain_part_ref,
 ):
     tokens, width = query_ref.shape[1:]
     half = own_half(mine)
@@ -300,8 +318,8 @@
         jnp.concatenate([blank, part], axis=0),
     )
     if before_ref is not None:
-        part = part + before_ref[...]
-    gain_part_ref[...] = part
+        part = part + before_ref[pl.ds(PAIRS * 64, 2 * PAIRS), :]
+    out_ref[pl.ds(PAIRS * 64, 2 * PAIRS), :] = part
 
 
 def backward_kernel(
@@ -313,6 +331,7 @@
     state_ref,
     entry_ref,
     table_ref,
+    mask_ref,
     grad_query_ref,
     grad_key_ref,
     grad_value_ref,
@@ -323,7 +342,7 @@
     half = own_half(mine)
     table = pick_columns(table_ref[pl.ds(COLUMNS, 128), :], half)
     cum_rows = pick_rows(table_ref[pl.ds(CUM_ROWS, 16), :], half)
-    mask = table_ref[pl.ds(MASK, 128), :]
+    mask = mask_ref[...]
     earlier = twice(triangle(tokens, lambda s, t: s < t).astype(F32).astype(BF16), 0)
     reached = triangle(tokens, lambda u, t: u >= t)
     chooser = twice(head_chooser(), 1)
@@ -367,9 +386,8 @@
 
 
 def other_backward_kernel(*refs):
-    inputs, (layer_own, layer_other, query_own) = refs[:7], refs[7:10]
-    layer_ref, grad_query_ref = refs[10:12]
-    *outs, query_part, sent = refs[12:]
+    inputs, (layer_own, layer_other), layer_ref = refs[:8], refs[8:10], refs[10]
+    *outs, sent = refs[11:]
     width = layer_ref.shape[2]
     half = own_half(False)
     own_lanes, lanes = half_lanes(own_half(True), width), half_lanes(half, width)
@@ -379,19 +397,13 @@
             [
                 (layer_own, layer_ref.at[0, :, own_lanes]),
                 (layer_other, layer_ref.at[0, :, lanes]),
-                (query_own, grad_query_ref.at[0, :, own_lanes]),
-                (query_part, grad_query_ref.at[0, :, lanes]),
             ]
         )
     ]
 
-    @pl.when(half >= 0)
-    def _():
-        for copy in copies[:3]:
-            copy.start()
-
-    backward_kernel(False, *inputs, query_part, *outs)
-    copies[3].start()
+    for copy in copies:
+        copy.start()
+    once(half, lambda: backward_kernel(False, *inputs, *outs))
     for copy in copies:
         copy.wait()
 
@@ -474,15 +486,17 @@
 
 
 def other_final_kernel(*refs):
-    inputs, (key_own, value_own, other_ref, gain_part_ref) = refs[:9], refs[9:13]
-    grad_key_ref, grad_value_ref, decay_ref, gain_ref = refs[13:17]
-    *parts, decay_out, gain_out, sent = refs[17:]
+    inputs, done, (other_ref, gain_part_ref) = refs[:9], refs[9:13], refs[13:15]
+    grad_query_ref, grad_key_ref, grad_value_ref, decay_ref, gain_ref = refs[15:20]
+    *parts, decay_out, gain_out, sent = refs[20:]
     width = grad_key_ref.shape[2]
     half = own_half(False)
     own_lanes, lanes = half_lanes(own_half(True), width), half_lanes(half, width)
     pairs = [
-        (key_own, grad_key_ref.at[0, :, own_lanes]),
-        (value_own, grad_value_ref.at[0, :, own_lanes]),
+        (done[0], grad_query_ref.at[0, :, own_lanes]),
+        (done[1], grad_query_ref.at[0, :, lanes]),
+        (done[2], grad_key_ref.at[0, :, own_lanes]),
+        (done[3], grad_value_ref.at[0, :, own_lanes]),
         (gain_out, gain_ref),
         (parts[0], grad_key_ref.at[0, :, lanes]),
         (parts[1], grad_value_ref.at[0, :, lanes]),
@@ -494,19 +508,20 @@
     ]
     gain_out[...] = gain_part_ref[...] + inputs[7][pl.ds(PAIRS * 64, 2 * PAIRS), :]
 
-    @pl.when(half >= 0)
-    def _():
-        for copy in copies[:3]:
-            copy.start()
-
-    rows = final_parts(False, *inputs, *parts)
-    other = other_ref[...]
-    decay_out[...] = jnp.where(
-        half == 0,
-        jnp.concatenate([rows, other], axis=0),
-        jnp.concatenate([other, rows], axis=0),
-    )
-    for copy in copies[3:]:
+    for copy in copies[:5]:
+        copy.start()
+
+    def work():
+        rows = final_parts(False, *inputs, *parts)
+        other = other_ref[...]
+        decay_out[...] = jnp.where(
+            half == 0,
+            jnp.concatenate([rows, other], axis=0),
+            jnp.concatenate([other, rows], axis=0),
+        )
+
+    once(half, work)
+    for copy in copies[5:]:
         copy.start()
     for copy in copies:
         copy.wait()
@@ -547,6 +562,14 @@
         size = blocks if axis == "seq" else scans
         return lax.ppermute(x, axis, [(i, i ^ bit) for i in range(size)])
 
+    def exchange_mixed(x, *bits):
+        pairs = [
+            (i * scans + j, (i ^ bits[i & 1][0]) * scans + (j ^ bits[i & 1][1]))
+            for i in range(blocks)
+            for j in range(scans)
+        ]
+        return lax.ppermute(x, ("seq", "dp"), pairs)
+
     def parts(buffer):
         state = buffer[:state_rows].reshape(PAIRS, 64, LANES)
         if buffer.shape[0] == state_rows:
@@ -570,11 +593,10 @@
     part = (tokens, width // 2)
     buffer = (buffer_rows, LANES)
     rows = (HEAD_TOTAL // 2, LANES)
-    blocks_of = [(queries, VMEM), (key_vectors, VMEM), (value_vectors, VMEM)]
 
     gain_rows = norm_gain.reshape(2 * PAIRS, LANES)
 
-    state_other, tables = call(
+    state_other, tables, key_vectors, value_vectors = call(
         first_state_kernel,
         [
             (key_vectors, HBM),
@@ -582,21 +604,25 @@
             (jnp.swapaxes(log_decay, 1, 2), HBM),
             (restart, HBM),
         ],
-        [(buffer, F32, VMEM), ((TABLE_ROWS, LANES), F32, VMEM)],
         [
-            pltpu.VMEM(part, BF16),
-            pltpu.VMEM(part, BF16),
+            (buffer, F32, VMEM),
+            ((TABLE_ROWS, LANES), F32, VMEM),
+            (whole, BF16, VMEM),
+            (whole, BF16, VMEM),
+        ],
+        [
             pltpu.VMEM((HEAD_TOTAL, tokens), F32),
             pltpu.VMEM((1, tokens), jnp.int32),
-            pltpu.SemaphoreType.DMA((4,)),
+            pltpu.SemaphoreType.DMA((6,)),
         ],
         constrain=True,
     )
+    blocks_of = [(queries, VMEM), (key_vectors, VMEM), (value_vectors, VMEM)]
     swapped = exchange(state_other, 1)
-    (state_own,) = call(
+    state_own, mask = call(
         second_state_kernel,
         [(key_vectors, VMEM), (value_vectors, VMEM), (tables, VMEM)],
-        [(buffer, F32, VMEM)],
+        [(buffer, F32, VMEM), ((tokens, tokens), F32, VMEM)],
     )
     first_state, first_carry = parts(jnp.where(on_first, state_own, swapped))
     second_state, second_carry = parts(jnp.where(on_first, swapped, state_own))
@@ -608,7 +634,7 @@
     def mixture(mine, tables):
         return call(
             functools.partial(mixture_kernel, mine),
-            blocks_of + [(upstream, VMEM), (gain_rows, VMEM), (tables, VMEM)],
+            blocks_of + [(upstream, VMEM), (gain_rows, VMEM), (tables, VMEM), (mask, VMEM)],
             [
                 (part, F32, VMEM),
                 ((width // 2, LANES), BF16, VMEM),
@@ -657,17 +683,10 @@
         if mine:
             kernel = lambda *refs: forward_kernel(True, *refs[:8], None, *refs[8:])
         else:
-            operands.append((gain, VMEM))
+            operands.append((query_states[True], VMEM))
             kernel = functools.partial(forward_kernel, False)
-        layer_parts[mine], grad_mixed[mine], query_states[mine], gain = call(
-            kernel,
-            operands,
-            [
-                (part, BF16, VMEM),
-                (part, BF16, VMEM),
-                ((state_rows, LANES), F32, VMEM),
-                ((2 * PAIRS, LANES), F32, VMEM),
-            ],
+        layer_parts[mine], grad_mixed[mine], query_states[mine] = call(
+            kernel, operands, [(part, BF16, VMEM), (part, BF16, VMEM), (buffer, F32, VMEM)]
         )
 
     def backward(mine, state):
@@ -676,20 +695,22 @@
             (state, VMEM),
             (mixed[mine][2], VMEM),
             (tables, VMEM),
+            (mask, VMEM),
         ]
-        results = [(part, F32, VMEM), (part, F32, VMEM), (rows, F32, VMEM), (part, F32, VMEM)]
+        results = [
+            (part, BF16, VMEM),
+            (part, F32, VMEM),
+            (part, F32, VMEM),
+            (rows, F32, VMEM),
+            (part, F32, VMEM),
+        ]
         if mine:
-            return call(
-                functools.partial(backward_kernel, True),
-                operands,
-                [(part, BF16, VMEM)] + results,
-            )
-        finished = (layer_parts[True], layer_parts[False], local_parts[True][0])
+            return call(functools.partial(backward_kernel, True), operands, results)
         return call(
             other_backward_kernel,
-            operands + [(x, VMEM) for x in finished],
-            [(whole, BF16, HBM), (whole, BF16, HBM)] + results,
-            [pltpu.VMEM(part, BF16), pltpu.SemaphoreType.DMA((4,))],
+            operands + [(layer_parts[x], VMEM) for x in (True, False)],
+            [(whole, BF16, HBM)] + results,
+            [pltpu.SemaphoreType.DMA((2,))],
         )
 
     steps = []
@@ -698,16 +719,38 @@
         steps.append(step)
         step //= 2
     swapped = exchange(query_states[False], 1)
-    gains = [gain]
-    for step in steps[:1]:
-        larger = jnp.concatenate([gain, query_states[False][:24]], axis=0)
-        gains.append(exchange(larger, step, "dp")[: 2 * PAIRS])
+    chip_gain = query_states[False][state_rows:] + swapped[state_rows:]
+    gains = [jnp.where(on_first, chip_gain, 0.0)]
     first_query, _ = parts(jnp.where(on_first, query_states[True], swapped))
     second_query, _ = parts(jnp.where(on_first, swapped, query_states[True]))
     total = flat(first_query + first_carry * second_query)
     suffix = jnp.zeros_like(first_query)
     suffix_carry = jnp.ones_like(carry)
     local_parts = {}
+    if len(levels) == 2 and scans == 4:
+        total, chip_gain = lax.optimization_barrier((total, chip_gain))
+        received = exchange(jnp.concatenate([total, chip_gain], axis=0), 2)
+        fetched = [exchange_mixed(chip_gain, *bits) for bits in (((0, 1), (0, 3)), ((0, 2), (2, 1)), ((2, 3), (2, 2)))]
+        bit, is_upper, carry, their_carry = levels[0]
+        near = parts(received)[0]
+        own_query = parts(total)[0]
+        total = flat(jnp.where(is_upper, near + their_carry * own_query, own_query + carry * near))
+        gain = jnp.where(on_first, chip_gain + received[state_rows:], 0.0) + sum(fetched)
+        total, state = lax.optimization_barrier((total, state_in[False]))
+        received = exchange(total, 6)
+        others = exchange(gain, 6)
+        local_parts[True] = backward(True, state_in[True])
+        local_parts[False] = backward(False, state)
+        received, others, local_parts = lax.optimization_barrier((received, others, local_parts))
+        gains = [gain, others]
+        first_level, (bit, is_last, carry, their_carry) = levels
+        far = parts(received)[0]
+        suffix = jnp.where(
+            is_last,
+            jnp.where(is_upper, 0.0, near),
+            jnp.where(is_upper, far, near + first_level[3] * far),
+        )
+        levels = []
     for bit, is_upper, carry, their_carry in levels:
         partner = 2 * bit - 2
         mine = not local_parts
@@ -716,7 +759,7 @@
             total, state = lax.optimization_barrier((total, state_in[mine]))
             received = exchange(total, partner)
             gain = sum(gains)
-            for step in steps[1:]:
+            for step in steps:
                 gains = [gain, exchange(gain, step, "dp")]
                 gain = sum(gains)
             if len(levels) == 1:
@@ -742,9 +785,9 @@
     for mine in (True, False):
         if mine not in local_parts:
             local_parts[mine] = backward(mine, state_in[mine])
-    if not levels:
+    if blocks == 2:
         gain = sum(gains)
-        for step in steps[1:]:
+        for step in steps:
             gain = gain + exchange(gain, step, "dp")
         gains = [gain]
     before_second = second_query + second_carry * suffix
@@ -777,11 +820,13 @@
         final_operands(True),
         [(part, BF16, VMEM), (part, BF16, VMEM), (rows, F32, VMEM)],
     )
-    finished = (grad_key, grad_value, decay_rows, gain)
-    grad_key, grad_value, grad_decay, grad_gain = call(
+    finished = [local_parts[mine][-5] for mine in (True, False)]
+    finished += [grad_key, grad_value, decay_rows, gain]
+    grad_query, grad_key, grad_value, grad_decay, grad_gain = call(
         other_final_kernel,
         final_operands(False) + [(x, VMEM) for x in finished],
         [
+            (whole, BF16, HBM),
             (whole, BF16, HBM),
             (whole, BF16, HBM),
             ((1, HEAD_TOTAL, tokens), F32, HBM),
@@ -792,12 +837,11 @@
             pltpu.VMEM(part, BF16),
             pltpu.VMEM((HEAD_TOTAL, tokens), F32),
             pltpu.VMEM((2 * PAIRS, LANES), F32),
-            pltpu.SemaphoreType.DMA((6,)),
+            pltpu.SemaphoreType.DMA((8,)),
         ],
     )
-    layer_out, grad_query = local_parts[False][:2]
     return (
-        layer_out,
+        local_parts[False][0],
         grad_query,
         grad_key,
         grad_value,

time: 40.5 us -> 39.8 us (0.983)
  Pallas kernels: 10.3 us -> 9.54 us
  starting transfers between devices: 17.7 us -> 18.4 us
  waiting for transfers between devices: 10.9 us -> 10.3 us
    ppermute x0 -> x3, starting transfers between devices: none -> 3.01 us  [exchange_mixed(): return lax.ppermute(x, ('seq', 'dp'), pairs)]
    ppermute x12 -> x9, starting transfers between devices: 17.7 us -> 15.4 us  [exchange(): return lax.ppermute(x, axis, [(i, i ^ bit) for i in range(size)])]
    pallas_call x10, Pallas kernels: 10.3 us -> 9.54 us  [call(): pl.pallas_call(kernel, in_specs=[pl.BlockSpec(memory_space=memory) for a,...]
    ppermute x12 -> x9, waiting for transfers between devices: 10.9 us -> 10.3 us  [exchange(): return lax.ppermute(x, axis, [(i, i ^ bit) for i in range(size)])]
  transfers between devices with their start and end apart: 12 -> 12, of which waited for: 8 -> 8; matrix products, arithmetic and copies ran while one was open for 0% -> 0% of each run, Pallas kernels for 16% -> 15%
where the time goes in v5:
time: 39.8 us; the launch traced here: 39.6 us
  starting transfers between devices  18.4 us (46%)
  waiting for transfers between devices  10.3 us (26%)
  Pallas kernels  9.54 us (24%)
  between operations  0.81 us (2%)
  other arithmetic  0.47 us (1%)
    ppermute x9, starting transfers between devices, exchange(): return lax.ppermute(x, axis, [(i, i ^ bit) for i in range(size)])  15.4 us
    ppermute x9, waiting for transfers between devices, exchange(): return lax.ppermute(x, axis, [(i, i ^ bit) for i in range(size)])  10.3 us
    pallas_call x10, Pallas kernels, call(): pl.pallas_call(kernel, in_specs=[pl.BlockSpec(memory_space=memory) for a,...  9.54 us
    ppermute x3, starting transfers between devices, exchange_mixed(): return lax.ppermute(x, ('seq', 'dp'), pairs)  3.01 us
  transfers between devices with their start and end apart: 12, of which 8 were waited for; matrix products, arithmetic and copies ran while one was open for 0% of the time, Pallas kernels for 15%

profile of v5, /device:TPU:0, one launch (start us, length us, event | category | flops | bytes accessed | tf_op | source)
XLA Modules:
  0.0 39.6 jit_solution(18332558585438436580)
XLA Ops:
  0.6 1.6 %shard_map.118 = (f32[264,128]{1,0:T(8,128)S(1)}, f32[168,128]{1,0:T(8,128)S(1)}, bf16[1,128,1024]{2,1,0:T(8,128)(2,1)S(1)}, bf16[1,128,1024]{2,1,0:T(8,128)(2,1)S(1)}) custom-call(bf16[1,128,1024]{2,1,0:T(8,128)(2,1)} %key_ref.1, bf16[1,128,1024]{2,1,0:T(8,128)(2,1)} %value_ref.1, f32[1,16,128]{2,1,0:T(8,128)} %bitcast.71, s32[1,128]{1,0:T(1,128)} %restart_ref.1), custom_call_target="tpu_custom_call" | custom-call | tf_op jit(solution)/shard_map/pallas_call | solution.py:535
  2.2 0.5 %collective-permute-start = (f32[264,128]{1,0:T(8,128)S(1)}, f32[264,128]{1,0:T(8,128)S(1)}, u32[]{:S(2)}, u32[]{:S(2)}) collective-permute-start(f32[264,128]{1,0:T(8,128)S(1)} %get-tuple-element.76), channel_id=1, source_target_pairs={{0,4},{4,0},{8,12},{12,8},{16,20},{20,16},{24,28},{28,24},{1,5},{5... | collective-permute-start | bytes 405512 | tf_op jit(solution)/shard_map/ppermute | solution.py:563
  2.8 0.5 %shard_map.119 = (f32[264,128]{1,0:T(8,128)S(1)}, f32[128,128]{1,0:T(8,128)S(1)}) custom-call(bf16[1,128,1024]{2,1,0:T(8,128)(2,1)S(1)} %get-tuple-element.77.key_ref.refs_1_.refs_0_, bf16[1,128,1024]{2,1,0:T(8,128)(2,1)S(1)} %get-tuple-element.78.value_ref.refs_2_.refs_1_, f32[168,128]{1,0:T(8,128)S(1)} %get-tuple-element.94.table_ref.refs_6_.refs_8_), custom_call_target="tpu_custom_call" | custom-call | bytes 610304 | tf_op jit(solution)/shard_map/pallas_call | solution.py:535
  3.9 3.0 %collective-permute-start.1 = (f32[264,128]{1,0:T(8,128)S(1)}, f32[264,128]{1,0:T(8,128)S(1)}, u32[]{:S(2)}, u32[]{:S(2)}) collective-permute-start(f32[264,128]{1,0:T(8,128)S(1)} %maximum_maximum_fusion), channel_id=1, source_target_pairs={{0,8},{4,12},{8,0},{12,4},{16,24},{20,28},{24,16},{28,20},{1,9},{5... | collective-permute-start | bytes 405512 | tf_op jit(solution)/shard_map/ppermute | solution.py:563
  6.9 0.6 %shard_map.120 = (f32[128,512]{1,0:T(8,128)S(1)}, bf16[512,128]{1,0:T(8,128)(2,1)S(1)}, f32[128,512]{1,0:T(8,128)S(1)}, f32[128,512]{1,0:T(8,128)S(1)}) custom-call(bf16[1,128,1024]{2,1,0:T(8,128)(2,1)S(1)} %copy-done, bf16[1,128,1024]{2,1,0:T(8,128)(2,1)S(1)} %get-tuple-element.77.key_ref.refs_1_.refs_0_, ...), custom_call_target="tpu_custom_call" | custom-call | bytes 1204224 | tf_op jit(solution)/shard_map/pallas_call | solution.py:535
  7.5 3.3 %collective-permute-done.1 = f32[264,128]{1,0:T(8,128)S(1)} collective-permute-done((f32[264,128]{1,0:T(8,128)S(1)}, f32[264,128]{1,0:T(8,128)S(1)}, u32[]{:S(2)}, u32[]{:S(2)}) %collective-permute-start.1) | collective-permute-done | bytes 135200 | tf_op jit(solution)/shard_map/ppermute | solution.py:563
  11.0 3.8 %collective-permute-start.2 = (f32[264,128]{1,0:T(8,128)S(1)}, f32[264,128]{1,0:T(8,128)S(1)}, u32[]{:S(2)}, u32[]{:S(2)}) collective-permute-start(f32[264,128]{1,0:T(8,128)S(1)} %maximum_maximum_fusion.1), channel_id=1, source_target_pairs={{0,24},{4,28},{8,16},{12,20},{16,8},{20,12},{24,0},{28,4},{1,25},{... | collective-permute-start | bytes 405512 | tf_op jit(solution)/shard_map/ppermute | solution.py:563
  14.8 0.6 %shard_map.121 = (f32[128,512]{1,0:T(8,128)S(1)}, bf16[512,128]{1,0:T(8,128)(2,1)S(1)}, f32[128,512]{1,0:T(8,128)S(1)}, f32[128,512]{1,0:T(8,128)S(1)}) custom-call(bf16[1,128,1024]{2,1,0:T(8,128)(2,1)S(1)} %copy-done, bf16[1,128,1024]{2,1,0:T(8,128)(2,1)S(1)} %get-tuple-element.77.key_ref.refs_1_.refs_0_, ...), custom_call_target="tpu_custom_call" | custom-call | bytes 1204224 | tf_op jit(solution)/shard_map/pallas_call | solution.py:535
  15.4 2.7 %collective-permute-done.2 = f32[264,128]{1,0:T(8,128)S(1)} collective-permute-done((f32[264,128]{1,0:T(8,128)S(1)}, f32[264,128]{1,0:T(8,128)S(1)}, u32[]{:S(2)}, u32[]{:S(2)}) %collective-permute-start.2) | collective-permute-done | bytes 135200 | tf_op jit(solution)/shard_map/ppermute | solution.py:563
  18.2 0.7 %shard_map.122 = (bf16[128,512]{1,0:T(8,128)(2,1)S(1)}, bf16[128,512]{1,0:T(8,128)(2,1)S(1)}, f32[264,128]{1,0:T(8,128)S(1)}) custom-call(f32[128,512]{1,0:T(8,128)S(1)} %get-tuple-element.88.refs_0_, bf16[512,128]{1,0:T(8,128)(2,1)S(1)} %get-tuple-element.89.refs_1_, f32[128,512]{1,0:T(8,128)S(1)} %get-tuple-element.90.refs_2_.entry_ref, ...), custom_call_target="tpu_custom_call" | custom-call | bytes 1576960 | tf_op jit(solution)/shard_map/pallas_call | solution.py:535
  18.9 0.6 %collective-permute-done.3.state_ref.refs_4_.refs_6_ = f32[256,128]{1,0:T(8,128)S(1)} collective-permute-done((f32[256,128]{1,0:T(8,128)S(1)}, f32[256,128]{1,0:T(8,128)S(1)}, u32[]{:S(2)}, u32[]{:S(2)}) %collective-permute-start.3) | collective-permute-done | bytes 131104 | tf_op jit(solution)/shard_map/ppermute | solution.py:563
  19.5 0.7 %shard_map.123 = (bf16[128,512]{1,0:T(8,128)(2,1)S(1)}, bf16[128,512]{1,0:T(8,128)(2,1)S(1)}, f32[264,128]{1,0:T(8,128)S(1)}) custom-call(f32[128,512]{1,0:T(8,128)S(1)} %get-tuple-element.101.mixed_ref, bf16[512,128]{1,0:T(8,128)(2,1)S(1)} %get-tuple-element.102.turned_ref, f32[128,512]{1,0:T(8,128)S(1)} %get-tuple-element.103.entry_ref.refs_5_, ...), custom_call_target="tpu_custom_call" | custom-call | bytes 1712128 | tf_op jit(solution)/shard_map/pallas_call | solution.py:535
  20.5 1.2 %collective-permute-done.4 = f32[264,128]{1,0:T(8,128)S(1)} collective-permute-done((f32[264,128]{1,0:T(8,128)S(1)}, f32[264,128]{1,0:T(8,128)S(1)}, u32[]{:S(2)}, u32[]{:S(2)}) %collective-permute-start.4) | collective-permute-done | bytes 135200 | tf_op jit(solution)/shard_map/ppermute | solution.py:563
  21.7 2.5 %collective-permute-start.5 = (f32[264,128]{1,0:T(8,128)S(1)}, f32[264,128]{1,0:T(8,128)S(1)}, u32[]{:S(2)}, u32[]{:S(2)}) collective-permute-start(f32[264,128]{1,0:T(8,128)S(1)} %pad_maximum_fusion), channel_id=1, source_target_pairs={{0,8},{4,12},{8,0},{12,4},{16,24},{20,28},{24,16},{28,20},{1,9},{5... | collective-permute-start | bytes 405512 | tf_op jit(solution)/shard_map/ppermute | solution.py:563
  24.2 2.0 %collective-permute-start.9 = (f32[8,128]{1,0:T(8,128)S(1)}, f32[8,128]{1,0:T(8,128)S(1)}, u32[]{:S(2)}, u32[]{:S(2)}) collective-permute-start(f32[8,128]{1,0:T(8,128)S(1)} %slice_add_fusion.1), channel_id=1, source_target_pairs={{0,11},{1,10},{2,9},{3,8},{4,14},{5,15},{6,12},{7,13},{8,3},{9,2},... | collective-permute-start | bytes 12296 | tf_op jit(solution)/shard_map/ppermute | solution.py:571
  26.2 0.5 %collective-permute-start.8 = (f32[8,128]{1,0:T(8,128)S(1)}, f32[8,128]{1,0:T(8,128)S(1)}, u32[]{:S(2)}, u32[]{:S(2)}) collective-permute-start(f32[8,128]{1,0:T(8,128)S(1)} %slice_add_fusion.1), channel_id=1, source_target_pairs={{0,2},{1,3},{2,0},{3,1},{4,13},{5,12},{6,15},{7,14},{8,10},{9,11},... | collective-permute-start | bytes 12296 | tf_op jit(solution)/shard_map/ppermute | solution.py:571
  26.7 0.5 %collective-permute-start.7 = (f32[8,128]{1,0:T(8,128)S(1)}, f32[8,128]{1,0:T(8,128)S(1)}, u32[]{:S(2)}, u32[]{:S(2)}) collective-permute-start(f32[8,128]{1,0:T(8,128)S(1)} %slice_add_fusion.1), channel_id=1, source_target_pairs={{0,1},{1,0},{2,3},{3,2},{4,7},{5,6},{6,5},{7,4},{8,9},{9,8},{10,11... | collective-permute-start | bytes 12296 | tf_op jit(solution)/shard_map/ppermute | solution.py:571
  27.2 0.9 %collective-permute-done.5 = f32[264,128]{1,0:T(8,128)S(1)} collective-permute-done((f32[264,128]{1,0:T(8,128)S(1)}, f32[264,128]{1,0:T(8,128)S(1)}, u32[]{:S(2)}, u32[]{:S(2)}) %collective-permute-start.5) | collective-permute-done | bytes 135200 | tf_op jit(solution)/shard_map/ppermute | solution.py:563
  28.2 3.0 %collective-permute-start.6 = (f32[256,128]{1,0:T(8,128)S(1)}, f32[256,128]{1,0:T(8,128)S(1)}, u32[]{:S(2)}, u32[]{:S(2)}) collective-permute-start(f32[256,128]{1,0:T(8,128)S(1)} %fusion.7), channel_id=1, source_target_pairs={{0,24},{4,28},{8,16},{12,20},{16,8},{20,12},{24,0},{28,4},{1,25},{... | collective-permute-start | bytes 393224 | tf_op jit(solution)/shard_map/ppermute | solution.py:563
  31.2 2.2 %collective-permute-start.10 = (f32[8,128]{1,0:T(8,128)S(1)}, f32[8,128]{1,0:T(8,128)S(1)}, u32[]{:S(2)}, u32[]{:S(2)}) collective-permute-start(f32[8,128]{1,0:T(8,128)S(1)} %fusion.18), channel_id=1, source_target_pairs={{0,24},{4,28},{8,16},{12,20},{16,8},{20,12},{24,0},{28,4},{1,25},{... | collective-permute-start | bytes 12296 | tf_op jit(solution)/shard_map/ppermute | solution.py:563
  33.4 1.5 %shard_map.125 = (bf16[128,512]{1,0:T(8,128)(2,1)S(1)}, f32[128,512]{1,0:T(8,128)S(1)}, f32[128,512]{1,0:T(8,128)S(1)}, f32[8,128]{1,0:T(8,128)S(1)}, f32[128,512]{1,0:T(8,128)S(1)}) custom-call(bf16[1,128,1024]{2,1,0:T(8,128)(2,1)S(1)} %copy-done, bf16[1,128,1024]{2,1,0:T(8,128)(2,1)S(1)} %get-tuple-element.77.key_ref.refs_1_.refs_0_, ...), custom_call_target="tpu_custom_call" | custom-call | bytes 1462272 | tf_op jit(solution)/shard_map/pallas_call | solution.py:535
  35.0 1.6 %shard_map.124 = (bf16[1,128,1024]{2,1,0:T(8,128)(2,1)}, bf16[128,512]{1,0:T(8,128)(2,1)S(1)}, f32[128,512]{1,0:T(8,128)S(1)}, f32[128,512]{1,0:T(8,128)S(1)}, f...) custom-call(bf16[1,128,1024]{2,1,0:T(8,128)(2,1)S(1)} %copy-done, ...), custom_call_target="tpu_custom_call" | custom-call | bytes 1724416 | tf_op jit(solution)/shard_map/pallas_call | solution.py:535
  37.5 0.8 %collective-permute-done.11.refs_7_ = f32[264,128]{1,0:T(8,128)S(1)} collective-permute-done((f32[264,128]{1,0:T(8,128)S(1)}, f32[264,128]{1,0:T(8,128)S(1)}, u32[]{:S(2)}, u32[]{:S(2)}) %collective-permute-start.11) | collective-permute-done | bytes 135200 | tf_op jit(solution)/shard_map/ppermute | solution.py:563
  38.3 1.3 %shard_map.127 = (bf16[1,128,1024]{2,1,0:T(8,128)(2,1)}, bf16[1,128,1024]{2,1,0:T(8,128)(2,1)}, bf16[1,128,1024]{2,1,0:T(8,128)(2,1)}, f32[1,16,128]{2,1,0:T(8,128)}, f32[8,128]{1,0:T(8,128)}) custom-call(bf16[1,128,1024]{2,1,0:T(8,128)(2,1)S(1)} %get-tuple-element.77.key_ref.refs_1_.refs_0_, ...), custom_call_target="tpu_custom_call" | custom-call | bytes 2199552 | tf_op jit(solution)/shard_map/pallas_call | solution.py:535
  (34 shorter events, 2.1 us)
Async XLA Ops:
  2.2 1.5 %collective-permute-start = (f32[264,128]{1,0:T(8,128)S(1)}, f32[264,128]{1,0:T(8,128)S(1)}, u32[]{:S(2)}, u32[]{:S(2)}) collective-permute-start(f32[264,128]{1,0:T(8,128)S(1)} %get-tuple-element.76), channel_id=1, source_target_pairs={{0,4},{4,0},{8,12},{12,8},{16,20},{20,16},{24,28},{28,24},{1,5},{5... | collective-permute-start | bytes 405512 | tf_op jit(solution)/shard_map/ppermute | solution.py:563
  3.8 3.2 %copy-start = (bf16[1,128,1024]{2,1,0:T(8,128)(2,1)S(1)}, bf16[1,128,1024]{2,1,0:T(8,128)(2,1)}, u32[]{:S(2)}) copy-start(bf16[1,128,1024]{2,1,0:T(8,128)(2,1)} %query_ref.7) | copy-start | bytes 786436
  3.8 3.2 %copy-start.1 = (bf16[1,128,1024]{2,1,0:T(8,128)(2,1)S(1)}, bf16[1,128,1024]{2,1,0:T(8,128)(2,1)}, u32[]{:S(2)}) copy-start(bf16[1,128,1024]{2,1,0:T(8,128)(2,1)} %upstream_ref.5) | copy-start | bytes 786436
  3.9 3.0 %copy-start.2 = (f32[1024]{0:T(1024)S(1)}, f32[1024]{0:T(1024)}, u32[]{:S(2)}) copy-start(f32[1024]{0:T(1024)} %param.12) | copy-start | bytes 12292
  3.9 6.9 %collective-permute-start.1 = (f32[264,128]{1,0:T(8,128)S(1)}, f32[264,128]{1,0:T(8,128)S(1)}, u32[]{:S(2)}, u32[]{:S(2)}) collective-permute-start(f32[264,128]{1,0:T(8,128)S(1)} %maximum_maximum_fusion), channel_id=1, source_target_pairs={{0,8},{4,12},{8,0},{12,4},{16,24},{20,28},{24,16},{28,20},{1,9},{5... | collective-permute-start | bytes 405512 | tf_op jit(solution)/shard_map/ppermute | solution.py:563
  11.0 7.1 %collective-permute-start.2 = (f32[264,128]{1,0:T(8,128)S(1)}, f32[264,128]{1,0:T(8,128)S(1)}, u32[]{:S(2)}, u32[]{:S(2)}) collective-permute-start(f32[264,128]{1,0:T(8,128)S(1)} %maximum_maximum_fusion.1), channel_id=1, source_target_pairs={{0,24},{4,28},{8,16},{12,20},{16,8},{20,12},{24,0},{28,4},{1,25},{... | collective-permute-start | bytes 405512 | tf_op jit(solution)/shard_map/ppermute | solution.py:563
  18.1 1.4 %collective-permute-start.3 = (f32[256,128]{1,0:T(8,128)S(1)}, f32[256,128]{1,0:T(8,128)S(1)}, u32[]{:S(2)}, u32[]{:S(2)}) collective-permute-start(f32[256,128]{1,0:T(8,128)S(1)} %get-tuple-element.149), channel_id=1, source_target_pairs={{0,4},{4,0},{8,12},{12,8},{16,20},{20,16},{24,28},{28,24},{1,5},{5... | collective-permute-start | bytes 393224 | tf_op jit(solution)/shard_map/ppermute | solution.py:563
  20.3 1.4 %collective-permute-start.4 = (f32[264,128]{1,0:T(8,128)S(1)}, f32[264,128]{1,0:T(8,128)S(1)}, u32[]{:S(2)}, u32[]{:S(2)}) collective-permute-start(f32[264,128]{1,0:T(8,128)S(1)} %get-tuple-element.105), channel_id=1, source_target_pairs={{0,4},{4,0},{8,12},{12,8},{16,20},{20,16},{24,28},{28,24},{1,5},{5... | collective-permute-start | bytes 405512 | tf_op jit(solution)/shard_map/ppermute | solution.py:563
  21.7 6.4 %collective-permute-start.5 = (f32[264,128]{1,0:T(8,128)S(1)}, f32[264,128]{1,0:T(8,128)S(1)}, u32[]{:S(2)}, u32[]{:S(2)}) collective-permute-start(f32[264,128]{1,0:T(8,128)S(1)} %pad_maximum_fusion), channel_id=1, source_target_pairs={{0,8},{4,12},{8,0},{12,4},{16,24},{20,28},{24,16},{28,20},{1,9},{5... | collective-permute-start | bytes 405512 | tf_op jit(solution)/shard_map/ppermute | solution.py:563
  24.2 7.0 %collective-permute-start.9 = (f32[8,128]{1,0:T(8,128)S(1)}, f32[8,128]{1,0:T(8,128)S(1)}, u32[]{:S(2)}, u32[]{:S(2)}) collective-permute-start(f32[8,128]{1,0:T(8,128)S(1)} %slice_add_fusion.1), channel_id=1, source_target_pairs={{0,11},{1,10},{2,9},{3,8},{4,14},{5,15},{6,12},{7,13},{8,3},{9,2},... | collective-permute-start | bytes 12296 | tf_op jit(solution)/shard_map/ppermute | solution.py:571
  26.2 5.0 %collective-permute-start.8 = (f32[8,128]{1,0:T(8,128)S(1)}, f32[8,128]{1,0:T(8,128)S(1)}, u32[]{:S(2)}, u32[]{:S(2)}) collective-permute-start(f32[8,128]{1,0:T(8,128)S(1)} %slice_add_fusion.1), channel_id=1, source_target_pairs={{0,2},{1,3},{2,0},{3,1},{4,13},{5,12},{6,15},{7,14},{8,10},{9,11},... | collective-permute-start | bytes 12296 | tf_op jit(solution)/shard_map/ppermute | solution.py:571
  26.7 4.5 %collective-permute-start.7 = (f32[8,128]{1,0:T(8,128)S(1)}, f32[8,128]{1,0:T(8,128)S(1)}, u32[]{:S(2)}, u32[]{:S(2)}) collective-permute-start(f32[8,128]{1,0:T(8,128)S(1)} %slice_add_fusion.1), channel_id=1, source_target_pairs={{0,1},{1,0},{2,3},{3,2},{4,7},{5,6},{6,5},{7,4},{8,9},{9,8},{10,11... | collective-permute-start | bytes 12296 | tf_op jit(solution)/shard_map/ppermute | solution.py:571
  28.2 8.6 %collective-permute-start.6 = (f32[256,128]{1,0:T(8,128)S(1)}, f32[256,128]{1,0:T(8,128)S(1)}, u32[]{:S(2)}, u32[]{:S(2)}) collective-permute-start(f32[256,128]{1,0:T(8,128)S(1)} %fusion.7), channel_id=1, source_target_pairs={{0,24},{4,28},{8,16},{12,20},{16,8},{20,12},{24,0},{28,4},{1,25},{... | collective-permute-start | bytes 393224 | tf_op jit(solution)/shard_map/ppermute | solution.py:563
  31.2 5.6 %collective-permute-start.10 = (f32[8,128]{1,0:T(8,128)S(1)}, f32[8,128]{1,0:T(8,128)S(1)}, u32[]{:S(2)}, u32[]{:S(2)}) collective-permute-start(f32[8,128]{1,0:T(8,128)S(1)} %fusion.18), channel_id=1, source_target_pairs={{0,24},{4,28},{8,16},{12,20},{16,8},{20,12},{24,0},{28,4},{1,25},{... | collective-permute-start | bytes 12296 | tf_op jit(solution)/shard_map/ppermute | solution.py:563
  36.9 1.4 %collective-permute-start.11 = (f32[264,128]{1,0:T(8,128)S(1)}, f32[264,128]{1,0:T(8,128)S(1)}, u32[]{:S(2)}, u32[]{:S(2)}) collective-permute-start(f32[264,128]{1,0:T(8,128)S(1)} %pad_maximum_fusion.1), channel_id=1, source_target_pairs={{0,4},{4,0},{8,12},{12,8},{16,20},{20,16},{24,28},{28,24},{1,5},{5... | collective-permute-start | bytes 405512 | tf_op jit(solution)/shard_map/ppermute | solution.py:563

commit v6 on v5

--- a/solution.py
+++ b/solution.py
@@ -649,7 +649,7 @@
     bit = 2
     while bit < blocks:
         is_upper = (position & bit) != 0
-        sent = joined(total, carry)
+        sent = flat(total) if 2 * bit == blocks else joined(total, carry)
         mine = not mixed
         if len(mixed) < 2:
             sent, tables = lax.optimization_barrier((sent, tables))
@@ -659,8 +659,10 @@
             received, mixed[mine] = lax.optimization_barrier((received, mixed[mine]))
         theirs, their_carry = parts(received)
         prefix = jnp.where(is_upper, prefix_carry * theirs + prefix, prefix)
+        levels.append((bit, is_upper, carry, their_carry))
+        if their_carry is None:
+            break
         prefix_carry = jnp.where(is_upper, prefix_carry * their_carry, prefix_carry)
-        levels.append((bit, is_upper, carry, their_carry))
         total = jnp.where(is_upper, carry * theirs + total, their_carry * total + theirs)
         carry = carry * their_carry
         bit *= 2
@@ -730,7 +732,10 @@
     if len(levels) == 2 and scans == 4:
         total, chip_gain = lax.optimization_barrier((total, chip_gain))
         received = exchange(jnp.concatenate([total, chip_gain], axis=0), 2)
-        fetched = [exchange_mixed(chip_gain, *bits) for bits in (((0, 1), (0, 3)), ((0, 2), (2, 1)), ((2, 3), (2, 2)))]
+        fetched = [
+            exchange_mixed(chip_gain, *bits)
+            for bits in (((0, 1), (0, 3)), ((0, 2), (2, 2)), ((2, 3), (2, 1)))
+        ]
         bit, is_upper, carry, their_carry = levels[0]
         near = parts(received)[0]
         own_query = parts(total)[0]
@@ -780,6 +785,8 @@
         theirs, _ = parts(received)
         total = parts(total)[0]
         suffix = jnp.where(is_upper, suffix, suffix_carry * theirs + suffix)
+        if their_carry is None:
+            break
         suffix_carry = jnp.where(is_upper, suffix_carry, suffix_carry * their_carry)
         total = flat(jnp.where(is_upper, theirs + their_carry * total, total + carry * theirs))
     for mine in (True, False):

time: 39.8 us -> 39.6 us (level)
  no operation moved by 1% of the time
where the time goes in v6:
time: 39.6 us; the launch traced here: 39.4 us
  starting transfers between devices  18.4 us (46%)
  waiting for transfers between devices  10.2 us (26%)
  Pallas kernels  9.53 us (24%)
  between operations  0.8 us (2%)
    ppermute x9, starting transfers between devices, exchange(): return lax.ppermute(x, axis, [(i, i ^ bit) for i in range(size)])  15.4 us
    ppermute x9, waiting for transfers between devices, exchange(): return lax.ppermute(x, axis, [(i, i ^ bit) for i in range(size)])  10.2 us
    pallas_call x10, Pallas kernels, call(): pl.pallas_call(kernel, in_specs=[pl.BlockSpec(memory_space=memory) for a,...  9.53 us
    ppermute x3, starting transfers between devices, exchange_mixed(): return lax.ppermute(x, ('seq', 'dp'), pairs)  3.01 us
  transfers between devices with their start and end apart: 12, of which 8 were waited for; matrix products, arithmetic and copies ran while one was open for 0% of the time, Pallas kernels for 15%

profile of v6, /device:TPU:0, one launch (start us, length us, event | category | flops | bytes accessed | tf_op | source)
XLA Modules:
  0.0 39.4 jit_solution(13265935250215828288)
XLA Ops:
  0.6 1.6 %shard_map.118 = (f32[264,128]{1,0:T(8,128)S(1)}, f32[168,128]{1,0:T(8,128)S(1)}, bf16[1,128,1024]{2,1,0:T(8,128)(2,1)S(1)}, bf16[1,128,1024]{2,1,0:T(8,128)(2,1)S(1)}) custom-call(bf16[1,128,1024]{2,1,0:T(8,128)(2,1)} %key_ref.1, bf16[1,128,1024]{2,1,0:T(8,128)(2,1)} %value_ref.1, f32[1,16,128]{2,1,0:T(8,128)} %bitcast.71, s32[1,128]{1,0:T(1,128)} %restart_ref.1), custom_call_target="tpu_custom_call" | custom-call | tf_op jit(solution)/shard_map/pallas_call | solution.py:535
  2.2 0.5 %collective-permute-start = (f32[264,128]{1,0:T(8,128)S(1)}, f32[264,128]{1,0:T(8,128)S(1)}, u32[]{:S(2)}, u32[]{:S(2)}) collective-permute-start(f32[264,128]{1,0:T(8,128)S(1)} %get-tuple-element.76), channel_id=1, source_target_pairs={{0,4},{4,0},{8,12},{12,8},{16,20},{20,16},{24,28},{28,24},{1,5},{5... | collective-permute-start | bytes 405512 | tf_op jit(solution)/shard_map/ppermute | solution.py:563
  2.8 0.5 %shard_map.119 = (f32[264,128]{1,0:T(8,128)S(1)}, f32[128,128]{1,0:T(8,128)S(1)}) custom-call(bf16[1,128,1024]{2,1,0:T(8,128)(2,1)S(1)} %get-tuple-element.77.key_ref.refs_1_.refs_0_, bf16[1,128,1024]{2,1,0:T(8,128)(2,1)S(1)} %get-tuple-element.78.value_ref.refs_2_.refs_1_, f32[168,128]{1,0:T(8,128)S(1)} %get-tuple-element.94.table_ref.refs_6_.refs_8_), custom_call_target="tpu_custom_call" | custom-call | bytes 610304 | tf_op jit(solution)/shard_map/pallas_call | solution.py:535
  3.9 3.0 %collective-permute-start.1 = (f32[264,128]{1,0:T(8,128)S(1)}, f32[264,128]{1,0:T(8,128)S(1)}, u32[]{:S(2)}, u32[]{:S(2)}) collective-permute-start(f32[264,128]{1,0:T(8,128)S(1)} %maximum_maximum_fusion), channel_id=1, source_target_pairs={{0,8},{4,12},{8,0},{12,4},{16,24},{20,28},{24,16},{28,20},{1,9},{5... | collective-permute-start | bytes 405512 | tf_op jit(solution)/shard_map/ppermute | solution.py:563
  6.9 0.6 %shard_map.120 = (f32[128,512]{1,0:T(8,128)S(1)}, bf16[512,128]{1,0:T(8,128)(2,1)S(1)}, f32[128,512]{1,0:T(8,128)S(1)}, f32[128,512]{1,0:T(8,128)S(1)}) custom-call(bf16[1,128,1024]{2,1,0:T(8,128)(2,1)S(1)} %copy-done, bf16[1,128,1024]{2,1,0:T(8,128)(2,1)S(1)} %get-tuple-element.77.key_ref.refs_1_.refs_0_, ...), custom_call_target="tpu_custom_call" | custom-call | bytes 1204224 | tf_op jit(solution)/shard_map/pallas_call | solution.py:535
  7.5 3.3 %collective-permute-done.1 = f32[264,128]{1,0:T(8,128)S(1)} collective-permute-done((f32[264,128]{1,0:T(8,128)S(1)}, f32[264,128]{1,0:T(8,128)S(1)}, u32[]{:S(2)}, u32[]{:S(2)}) %collective-permute-start.1) | collective-permute-done | bytes 135200 | tf_op jit(solution)/shard_map/ppermute | solution.py:563
  10.9 3.8 %collective-permute-start.2 = (f32[256,128]{1,0:T(8,128)S(1)}, f32[256,128]{1,0:T(8,128)S(1)}, u32[]{:S(2)}, u32[]{:S(2)}) collective-permute-start(f32[256,128]{1,0:T(8,128)S(1)} %fusion.5), channel_id=1, source_target_pairs={{0,24},{4,28},{8,16},{12,20},{16,8},{20,12},{24,0},{28,4},{1,25},{... | collective-permute-start | bytes 393224 | tf_op jit(solution)/shard_map/ppermute | solution.py:563
  14.7 0.6 %shard_map.121 = (f32[128,512]{1,0:T(8,128)S(1)}, bf16[512,128]{1,0:T(8,128)(2,1)S(1)}, f32[128,512]{1,0:T(8,128)S(1)}, f32[128,512]{1,0:T(8,128)S(1)}) custom-call(bf16[1,128,1024]{2,1,0:T(8,128)(2,1)S(1)} %copy-done, bf16[1,128,1024]{2,1,0:T(8,128)(2,1)S(1)} %get-tuple-element.77.key_ref.refs_1_.refs_0_, ...), custom_call_target="tpu_custom_call" | custom-call | bytes 1204224 | tf_op jit(solution)/shard_map/pallas_call | solution.py:535
  15.3 2.6 %collective-permute-done.2 = f32[256,128]{1,0:T(8,128)S(1)} collective-permute-done((f32[256,128]{1,0:T(8,128)S(1)}, f32[256,128]{1,0:T(8,128)S(1)}, u32[]{:S(2)}, u32[]{:S(2)}) %collective-permute-start.2) | collective-permute-done | bytes 131104 | tf_op jit(solution)/shard_map/ppermute | solution.py:563
  18.0 0.7 %shard_map.122 = (bf16[128,512]{1,0:T(8,128)(2,1)S(1)}, bf16[128,512]{1,0:T(8,128)(2,1)S(1)}, f32[264,128]{1,0:T(8,128)S(1)}) custom-call(f32[128,512]{1,0:T(8,128)S(1)} %get-tuple-element.88.refs_0_, bf16[512,128]{1,0:T(8,128)(2,1)S(1)} %get-tuple-element.89.refs_1_, f32[128,512]{1,0:T(8,128)S(1)} %get-tuple-element.90.refs_2_.entry_ref, ...), custom_call_target="tpu_custom_call" | custom-call | bytes 1576960 | tf_op jit(solution)/shard_map/pallas_call | solution.py:535
  18.7 0.6 %collective-permute-done.3.state_ref.refs_4_.refs_6_ = f32[256,128]{1,0:T(8,128)S(1)} collective-permute-done((f32[256,128]{1,0:T(8,128)S(1)}, f32[256,128]{1,0:T(8,128)S(1)}, u32[]{:S(2)}, u32[]{:S(2)}) %collective-permute-start.3) | collective-permute-done | bytes 131104 | tf_op jit(solution)/shard_map/ppermute | solution.py:563
  19.3 0.7 %shard_map.123 = (bf16[128,512]{1,0:T(8,128)(2,1)S(1)}, bf16[128,512]{1,0:T(8,128)(2,1)S(1)}, f32[264,128]{1,0:T(8,128)S(1)}) custom-call(f32[128,512]{1,0:T(8,128)S(1)} %get-tuple-element.101.mixed_ref, bf16[512,128]{1,0:T(8,128)(2,1)S(1)} %get-tuple-element.102.turned_ref, f32[128,512]{1,0:T(8,128)S(1)} %get-tuple-element.103.entry_ref.refs_5_, ...), custom_call_target="tpu_custom_call" | custom-call | bytes 1712128 | tf_op jit(solution)/shard_map/pallas_call | solution.py:535
  20.3 1.2 %collective-permute-done.4 = f32[264,128]{1,0:T(8,128)S(1)} collective-permute-done((f32[264,128]{1,0:T(8,128)S(1)}, f32[264,128]{1,0:T(8,128)S(1)}, u32[]{:S(2)}, u32[]{:S(2)}) %collective-permute-start.4) | collective-permute-done | bytes 135200 | tf_op jit(solution)/shard_map/ppermute | solution.py:563
  21.6 2.4 %collective-permute-start.5 = (f32[264,128]{1,0:T(8,128)S(1)}, f32[264,128]{1,0:T(8,128)S(1)}, u32[]{:S(2)}, u32[]{:S(2)}) collective-permute-start(f32[264,128]{1,0:T(8,128)S(1)} %pad_maximum_fusion), channel_id=1, source_target_pairs={{0,8},{4,12},{8,0},{12,4},{16,24},{20,28},{24,16},{28,20},{1,9},{5... | collective-permute-start | bytes 405512 | tf_op jit(solution)/shard_map/ppermute | solution.py:563
  24.0 2.0 %collective-permute-start.9 = (f32[8,128]{1,0:T(8,128)S(1)}, f32[8,128]{1,0:T(8,128)S(1)}, u32[]{:S(2)}, u32[]{:S(2)}) collective-permute-start(f32[8,128]{1,0:T(8,128)S(1)} %slice_add_fusion.1), channel_id=1, source_target_pairs={{0,11},{1,10},{2,9},{3,8},{4,13},{5,12},{6,15},{7,14},{8,3},{9,2},... | collective-permute-start | bytes 12296 | tf_op jit(solution)/shard_map/ppermute | solution.py:571
  25.9 0.5 %collective-permute-start.8 = (f32[8,128]{1,0:T(8,128)S(1)}, f32[8,128]{1,0:T(8,128)S(1)}, u32[]{:S(2)}, u32[]{:S(2)}) collective-permute-start(f32[8,128]{1,0:T(8,128)S(1)} %slice_add_fusion.1), channel_id=1, source_target_pairs={{0,2},{1,3},{2,0},{3,1},{4,14},{5,15},{6,12},{7,13},{8,10},{9,11},... | collective-permute-start | bytes 12296 | tf_op jit(solution)/shard_map/ppermute | solution.py:571
  26.4 0.5 %collective-permute-start.7 = (f32[8,128]{1,0:T(8,128)S(1)}, f32[8,128]{1,0:T(8,128)S(1)}, u32[]{:S(2)}, u32[]{:S(2)}) collective-permute-start(f32[8,128]{1,0:T(8,128)S(1)} %slice_add_fusion.1), channel_id=1, source_target_pairs={{0,1},{1,0},{2,3},{3,2},{4,7},{5,6},{6,5},{7,4},{8,9},{9,8},{10,11... | collective-permute-start | bytes 12296 | tf_op jit(solution)/shard_map/ppermute | solution.py:571
  27.0 0.9 %collective-permute-done.5 = f32[264,128]{1,0:T(8,128)S(1)} collective-permute-done((f32[264,128]{1,0:T(8,128)S(1)}, f32[264,128]{1,0:T(8,128)S(1)}, u32[]{:S(2)}, u32[]{:S(2)}) %collective-permute-start.5) | collective-permute-done | bytes 135200 | tf_op jit(solution)/shard_map/ppermute | solution.py:563
  27.9 3.1 %collective-permute-start.6 = (f32[256,128]{1,0:T(8,128)S(1)}, f32[256,128]{1,0:T(8,128)S(1)}, u32[]{:S(2)}, u32[]{:S(2)}) collective-permute-start(f32[256,128]{1,0:T(8,128)S(1)} %fusion.7), channel_id=1, source_target_pairs={{0,24},{4,28},{8,16},{12,20},{16,8},{20,12},{24,0},{28,4},{1,25},{... | collective-permute-start | bytes 393224 | tf_op jit(solution)/shard_map/ppermute | solution.py:563
  31.1 2.2 %collective-permute-start.10 = (f32[8,128]{1,0:T(8,128)S(1)}, f32[8,128]{1,0:T(8,128)S(1)}, u32[]{:S(2)}, u32[]{:S(2)}) collective-permute-start(f32[8,128]{1,0:T(8,128)S(1)} %fusion.18), channel_id=1, source_target_pairs={{0,24},{4,28},{8,16},{12,20},{16,8},{20,12},{24,0},{28,4},{1,25},{... | collective-permute-start | bytes 12296 | tf_op jit(solution)/shard_map/ppermute | solution.py:563
  33.3 1.5 %shard_map.125 = (bf16[128,512]{1,0:T(8,128)(2,1)S(1)}, f32[128,512]{1,0:T(8,128)S(1)}, f32[128,512]{1,0:T(8,128)S(1)}, f32[8,128]{1,0:T(8,128)S(1)}, f32[128,512]{1,0:T(8,128)S(1)}) custom-call(bf16[1,128,1024]{2,1,0:T(8,128)(2,1)S(1)} %copy-done, bf16[1,128,1024]{2,1,0:T(8,128)(2,1)S(1)} %get-tuple-element.77.key_ref.refs_1_.refs_0_, ...), custom_call_target="tpu_custom_call" | custom-call | bytes 1462272 | tf_op jit(solution)/shard_map/pallas_call | solution.py:535
  34.8 1.6 %shard_map.124 = (bf16[1,128,1024]{2,1,0:T(8,128)(2,1)}, bf16[128,512]{1,0:T(8,128)(2,1)S(1)}, f32[128,512]{1,0:T(8,128)S(1)}, f32[128,512]{1,0:T(8,128)S(1)}, f...) custom-call(bf16[1,128,1024]{2,1,0:T(8,128)(2,1)S(1)} %copy-done, ...), custom_call_target="tpu_custom_call" | custom-call | bytes 1724416 | tf_op jit(solution)/shard_map/pallas_call | solution.py:535
  37.3 0.8 %collective-permute-done.11.refs_7_ = f32[264,128]{1,0:T(8,128)S(1)} collective-permute-done((f32[264,128]{1,0:T(8,128)S(1)}, f32[264,128]{1,0:T(8,128)S(1)}, u32[]{:S(2)}, u32[]{:S(2)}) %collective-permute-start.11) | collective-permute-done | bytes 135200 | tf_op jit(solution)/shard_map/ppermute | solution.py:563
  38.2 1.3 %shard_map.127 = (bf16[1,128,1024]{2,1,0:T(8,128)(2,1)}, bf16[1,128,1024]{2,1,0:T(8,128)(2,1)}, bf16[1,128,1024]{2,1,0:T(8,128)(2,1)}, f32[1,16,128]{2,1,0:T(8,128)}, f32[8,128]{1,0:T(8,128)}) custom-call(bf16[1,128,1024]{2,1,0:T(8,128)(2,1)S(1)} %get-tuple-element.77.key_ref.refs_1_.refs_0_, ...), custom_call_target="tpu_custom_call" | custom-call | bytes 2199552 | tf_op jit(solution)/shard_map/pallas_call | solution.py:535
  (33 shorter events, 2.0 us)
Async XLA Ops:
  2.2 1.5 %collective-permute-start = (f32[264,128]{1,0:T(8,128)S(1)}, f32[264,128]{1,0:T(8,128)S(1)}, u32[]{:S(2)}, u32[]{:S(2)}) collective-permute-start(f32[264,128]{1,0:T(8,128)S(1)} %get-tuple-element.76), channel_id=1, source_target_pairs={{0,4},{4,0},{8,12},{12,8},{16,20},{20,16},{24,28},{28,24},{1,5},{5... | collective-permute-start | bytes 405512 | tf_op jit(solution)/shard_map/ppermute | solution.py:563
  3.8 3.2 %copy-start = (bf16[1,128,1024]{2,1,0:T(8,128)(2,1)S(1)}, bf16[1,128,1024]{2,1,0:T(8,128)(2,1)}, u32[]{:S(2)}) copy-start(bf16[1,128,1024]{2,1,0:T(8,128)(2,1)} %query_ref.7) | copy-start | bytes 786436
  3.8 3.2 %copy-start.1 = (bf16[1,128,1024]{2,1,0:T(8,128)(2,1)S(1)}, bf16[1,128,1024]{2,1,0:T(8,128)(2,1)}, u32[]{:S(2)}) copy-start(bf16[1,128,1024]{2,1,0:T(8,128)(2,1)} %upstream_ref.5) | copy-start | bytes 786436
  3.9 3.0 %copy-start.2 = (f32[1024]{0:T(1024)S(1)}, f32[1024]{0:T(1024)}, u32[]{:S(2)}) copy-start(f32[1024]{0:T(1024)} %param.12) | copy-start | bytes 12292
  3.9 6.9 %collective-permute-start.1 = (f32[264,128]{1,0:T(8,128)S(1)}, f32[264,128]{1,0:T(8,128)S(1)}, u32[]{:S(2)}, u32[]{:S(2)}) collective-permute-start(f32[264,128]{1,0:T(8,128)S(1)} %maximum_maximum_fusion), channel_id=1, source_target_pairs={{0,8},{4,12},{8,0},{12,4},{16,24},{20,28},{24,16},{28,20},{1,9},{5... | collective-permute-start | bytes 405512 | tf_op jit(solution)/shard_map/ppermute | solution.py:563
  10.9 7.0 %collective-permute-start.2 = (f32[256,128]{1,0:T(8,128)S(1)}, f32[256,128]{1,0:T(8,128)S(1)}, u32[]{:S(2)}, u32[]{:S(2)}) collective-permute-start(f32[256,128]{1,0:T(8,128)S(1)} %fusion.5), channel_id=1, source_target_pairs={{0,24},{4,28},{8,16},{12,20},{16,8},{20,12},{24,0},{28,4},{1,25},{... | collective-permute-start | bytes 393224 | tf_op jit(solution)/shard_map/ppermute | solution.py:563
  17.9 1.4 %collective-permute-start.3 = (f32[256,128]{1,0:T(8,128)S(1)}, f32[256,128]{1,0:T(8,128)S(1)}, u32[]{:S(2)}, u32[]{:S(2)}) collective-permute-start(f32[256,128]{1,0:T(8,128)S(1)} %get-tuple-element.149), channel_id=1, source_target_pairs={{0,4},{4,0},{8,12},{12,8},{16,20},{20,16},{24,28},{28,24},{1,5},{5... | collective-permute-start | bytes 393224 | tf_op jit(solution)/shard_map/ppermute | solution.py:563
  20.1 1.4 %collective-permute-start.4 = (f32[264,128]{1,0:T(8,128)S(1)}, f32[264,128]{1,0:T(8,128)S(1)}, u32[]{:S(2)}, u32[]{:S(2)}) collective-permute-start(f32[264,128]{1,0:T(8,128)S(1)} %get-tuple-element.105), channel_id=1, source_target_pairs={{0,4},{4,0},{8,12},{12,8},{16,20},{20,16},{24,28},{28,24},{1,5},{5... | collective-permute-start | bytes 405512 | tf_op jit(solution)/shard_map/ppermute | solution.py:563
  21.6 6.3 %collective-permute-start.5 = (f32[264,128]{1,0:T(8,128)S(1)}, f32[264,128]{1,0:T(8,128)S(1)}, u32[]{:S(2)}, u32[]{:S(2)}) collective-permute-start(f32[264,128]{1,0:T(8,128)S(1)} %pad_maximum_fusion), channel_id=1, source_target_pairs={{0,8},{4,12},{8,0},{12,4},{16,24},{20,28},{24,16},{28,20},{1,9},{5... | collective-permute-start | bytes 405512 | tf_op jit(solution)/shard_map/ppermute | solution.py:563
  24.0 7.1 %collective-permute-start.9 = (f32[8,128]{1,0:T(8,128)S(1)}, f32[8,128]{1,0:T(8,128)S(1)}, u32[]{:S(2)}, u32[]{:S(2)}) collective-permute-start(f32[8,128]{1,0:T(8,128)S(1)} %slice_add_fusion.1), channel_id=1, source_target_pairs={{0,11},{1,10},{2,9},{3,8},{4,13},{5,12},{6,15},{7,14},{8,3},{9,2},... | collective-permute-start | bytes 12296 | tf_op jit(solution)/shard_map/ppermute | solution.py:571
  25.9 5.1 %collective-permute-start.8 = (f32[8,128]{1,0:T(8,128)S(1)}, f32[8,128]{1,0:T(8,128)S(1)}, u32[]{:S(2)}, u32[]{:S(2)}) collective-permute-start(f32[8,128]{1,0:T(8,128)S(1)} %slice_add_fusion.1), channel_id=1, source_target_pairs={{0,2},{1,3},{2,0},{3,1},{4,14},{5,15},{6,12},{7,13},{8,10},{9,11},... | collective-permute-start | bytes 12296 | tf_op jit(solution)/shard_map/ppermute | solution.py:571
  26.4 4.6 %collective-permute-start.7 = (f32[8,128]{1,0:T(8,128)S(1)}, f32[8,128]{1,0:T(8,128)S(1)}, u32[]{:S(2)}, u32[]{:S(2)}) collective-permute-start(f32[8,128]{1,0:T(8,128)S(1)} %slice_add_fusion.1), channel_id=1, source_target_pairs={{0,1},{1,0},{2,3},{3,2},{4,7},{5,6},{6,5},{7,4},{8,9},{9,8},{10,11... | collective-permute-start | bytes 12296 | tf_op jit(solution)/shard_map/ppermute | solution.py:571
  27.9 8.7 %collective-permute-start.6 = (f32[256,128]{1,0:T(8,128)S(1)}, f32[256,128]{1,0:T(8,128)S(1)}, u32[]{:S(2)}, u32[]{:S(2)}) collective-permute-start(f32[256,128]{1,0:T(8,128)S(1)} %fusion.7), channel_id=1, source_target_pairs={{0,24},{4,28},{8,16},{12,20},{16,8},{20,12},{24,0},{28,4},{1,25},{... | collective-permute-start | bytes 393224 | tf_op jit(solution)/shard_map/ppermute | solution.py:563
  31.1 5.6 %collective-permute-start.10 = (f32[8,128]{1,0:T(8,128)S(1)}, f32[8,128]{1,0:T(8,128)S(1)}, u32[]{:S(2)}, u32[]{:S(2)}) collective-permute-start(f32[8,128]{1,0:T(8,128)S(1)} %fusion.18), channel_id=1, source_target_pairs={{0,24},{4,28},{8,16},{12,20},{16,8},{20,12},{24,0},{28,4},{1,25},{... | collective-permute-start | bytes 12296 | tf_op jit(solution)/shard_map/ppermute | solution.py:563
  36.7 1.4 %collective-permute-start.11 = (f32[264,128]{1,0:T(8,128)S(1)}, f32[264,128]{1,0:T(8,128)S(1)}, u32[]{:S(2)}, u32[]{:S(2)}) collective-permute-start(f32[264,128]{1,0:T(8,128)S(1)} %pad_maximum_fusion.1), channel_id=1, source_target_pairs={{0,4},{4,0},{8,12},{12,8},{16,20},{20,16},{24,28},{28,24},{1,5},{5... | collective-permute-start | bytes 405512 | tf_op jit(solution)/shard_map/ppermute | solution.py:563

commit v7 on v6

--- a/solution.py
+++ b/solution.py
@@ -570,6 +570,21 @@
         ]
         return lax.ppermute(x, ("seq", "dp"), pairs)
 
+    def exchange_by_core(x, first, second):
+        bits = (first, second)
+        return lax.ppermute(x, "seq", [(i, i ^ bits[i & 1]) for i in range(blocks)])
+
+    def by_chip(*cases):
+        return jnp.where(
+            is_last,
+            jnp.where(is_odd, cases[3], cases[2]),
+            jnp.where(is_odd, cases[1], cases[0]),
+        )
+
+    four_chips = blocks == 8 and scans == 4
+    is_last = (position & 4) != 0
+    is_odd = (position & 2) != 0
+
     def parts(buffer):
         state = buffer[:state_rows].reshape(PAIRS, 64, LANES)
         if buffer.shape[0] == state_rows:
@@ -646,8 +661,34 @@
 
     mixed = {}
     levels = []
+    if four_chips:
+        sent = joined(total, carry)
+        sent, tables = lax.optimization_barrier((sent, tables))
+        mixed[True] = mixture(True, tables)
+        received = exchange_by_core(sent, 6, 2)
+        received, mixed[True] = lax.optimization_barrier((received, mixed[True]))
+        near, near_carry = parts(received)
+        own_first = near_carry * total + near
+        own_last = carry * near + total
+        sent = jnp.where(
+            on_first,
+            by_chip(total, own_first, own_last, near),
+            jnp.where(is_odd, own_last, own_first),
+        )
+        sent = joined(sent, carry * near_carry)
+        sent, tables = lax.optimization_barrier((sent, tables))
+        mixed[False] = mixture(False, tables)
+        received = exchange_by_core(sent, 2, 6)
+        received, mixed[False] = lax.optimization_barrier((received, mixed[False]))
+        far, far_carry = parts(received)
+        near_last = near_carry * far + near
+        prefix = jnp.where(
+            on_first,
+            by_chip(0.0, far, near_last, far_carry * near + far),
+            by_chip(0.0, near, far, near_last),
+        )
     bit = 2
-    while bit < blocks:
+    while bit < blocks and not four_chips:
         is_upper = (position & bit) != 0
         sent = flat(total) if 2 * bit == blocks else joined(total, carry)
         mine = not mixed
@@ -729,33 +770,38 @@
     suffix = jnp.zeros_like(first_query)
     suffix_carry = jnp.ones_like(carry)
     local_parts = {}
-    if len(levels) == 2 and scans == 4:
+    if four_chips:
         total, chip_gain = lax.optimization_barrier((total, chip_gain))
-        received = exchange(jnp.concatenate([total, chip_gain], axis=0), 2)
+        received = exchange_by_core(jnp.concatenate([total, chip_gain], axis=0), 6, 2)
         fetched = [
             exchange_mixed(chip_gain, *bits)
             for bits in (((0, 1), (0, 3)), ((0, 2), (2, 2)), ((2, 3), (2, 1)))
         ]
-        bit, is_upper, carry, their_carry = levels[0]
         near = parts(received)[0]
         own_query = parts(total)[0]
-        total = flat(jnp.where(is_upper, near + their_carry * own_query, own_query + carry * near))
-        gain = jnp.where(on_first, chip_gain + received[state_rows:], 0.0) + sum(fetched)
+        own_first = own_query + carry * near
+        total = flat(
+            jnp.where(
+                on_first,
+                by_chip(near, own_first, own_query, own_query),
+                jnp.where(is_odd, near + near_carry * own_query, own_first),
+            )
+        )
+        gain = jnp.where(on_first, 0.0, chip_gain + received[state_rows:]) + sum(fetched)
         total, state = lax.optimization_barrier((total, state_in[False]))
-        received = exchange(total, 6)
-        others = exchange(gain, 6)
+        received = exchange_by_core(total, 2, 6)
+        others = exchange(gain, 4)
         local_parts[True] = backward(True, state_in[True])
         local_parts[False] = backward(False, state)
         received, others, local_parts = lax.optimization_barrier((received, others, local_parts))
         gains = [gain, others]
-        first_level, (bit, is_last, carry, their_carry) = levels
         far = parts(received)[0]
+        near_first = near + near_carry * far
         suffix = jnp.where(
-            is_last,
-            jnp.where(is_upper, 0.0, near),
-            jnp.where(is_upper, far, near + first_level[3] * far),
-        )
-        levels = []
+            on_first,
+            by_chip(far + far_carry * near, near_first, far, 0.0),
+            by_chip(near_first, far, near, 0.0),
+        )
     for bit, is_upper, carry, their_carry in levels:
         partner = 2 * bit - 2
         mine = not local_parts

time: 39.6 us -> 38.6 us (0.975)
  starting transfers between devices: 18.4 us -> 14.6 us
  waiting for transfers between devices: 10.2 us -> 12.1 us
  local copies, waits for them, and re-layouts: 0.1 us -> 0.77 us
    ppermute x9 -> x5, starting transfers between devices: 15.4 us -> 2.74 us  [exchange(): return lax.ppermute(x, axis, [(i, i ^ bit) for i in range(size)])]
    ppermute x0 -> x4, starting transfers between devices: none -> 8.83 us  [exchange_by_core(): return lax.ppermute(x, 'seq', [(i, i ^ bits[i & 1]) for i in range(blocks)])]
    ppermute x0 -> x4, waiting for transfers between devices: none -> 8.33 us  [exchange_by_core(): return lax.ppermute(x, 'seq', [(i, i ^ bits[i & 1]) for i in range(blocks)])]
    ppermute x9 -> x5, waiting for transfers between devices: 10.2 us -> 3.05 us  [exchange(): return lax.ppermute(x, axis, [(i, i ^ bit) for i in range(size)])]
    ppermute x3, waiting for transfers between devices: 0.01 us -> 0.75 us  [exchange_mixed(): return lax.ppermute(x, ('seq', 'dp'), pairs)]
    unnamed x6, local copies, waits for them, and re-layouts: 0.02 us -> 0.69 us
  transfers between devices with their start and end apart: 12 -> 12, of which waited for: 8 -> 8; matrix products, arithmetic and copies ran while one was open for 0% -> 0% of each run, Pallas kernels for 15% -> 16%
where the time goes in v7:
time: 38.6 us; the launch traced here: 38.4 us
  starting transfers between devices  14.6 us (38%)
  waiting for transfers between devices  12.1 us (31%)
  Pallas kernels  9.55 us (25%)
  between operations  0.82 us (2%)
  local copies, waits for them, and re-layouts  0.77 us (2%)
  other arithmetic  0.57 us (1%)
    pallas_call x10, Pallas kernels, call(): pl.pallas_call(kernel, in_specs=[pl.BlockSpec(memory_space=memory) for a,...  9.55 us
    ppermute x4, starting transfers between devices, exchange_by_core(): return lax.ppermute(x, 'seq', [(i, i ^ bits[i & 1]) for i in range(blocks)])  8.83 us
    ppermute x4, waiting for transfers between devices, exchange_by_core(): return lax.ppermute(x, 'seq', [(i, i ^ bits[i & 1]) for i in range(blocks)])  8.33 us
    ppermute x5, waiting for transfers between devices, exchange(): return lax.ppermute(x, axis, [(i, i ^ bit) for i in range(size)])  3.05 us
    ppermute x3, starting transfers between devices, exchange_mixed(): return lax.ppermute(x, ('seq', 'dp'), pairs)  3.01 us
    ppermute x5, starting transfers between devices, exchange(): return lax.ppermute(x, axis, [(i, i ^ bit) for i in range(size)])  2.74 us
  transfers between devices with their start and end apart: 12, of which 8 were waited for; matrix products, arithmetic and copies ran while one was open for 0% of the time, Pallas kernels for 16%

profile of v7, /device:TPU:0, one launch (start us, length us, event | category | flops | bytes accessed | tf_op | source)
XLA Modules:
  0.0 38.4 jit_solution(17522861375823000973)
XLA Ops:
  0.6 1.6 %shard_map.118 = (f32[264,128]{1,0:T(8,128)S(1)}, f32[168,128]{1,0:T(8,128)S(1)}, bf16[1,128,1024]{2,1,0:T(8,128)(2,1)S(1)}, bf16[1,128,1024]{2,1,0:T(8,128)(2,1)S(1)}) custom-call(bf16[1,128,1024]{2,1,0:T(8,128)(2,1)} %key_ref.1, bf16[1,128,1024]{2,1,0:T(8,128)(2,1)} %value_ref.1, f32[1,16,128]{2,1,0:T(8,128)} %bitcast.111, s32[1,128]{1,0:T(1,128)} %restart_ref.1), custom_call_target="tpu_custom_call" | custom-call | tf_op jit(solution)/shard_map/pallas_call | solution.py:535
  2.2 0.5 %collective-permute-start = (f32[264,128]{1,0:T(8,128)S(1)}, f32[264,128]{1,0:T(8,128)S(1)}, u32[]{:S(2)}, u32[]{:S(2)}) collective-permute-start(f32[264,128]{1,0:T(8,128)S(1)} %get-tuple-element.76), channel_id=1, source_target_pairs={{0,4},{4,0},{8,12},{12,8},{16,20},{20,16},{24,28},{28,24},{1,5},{5... | collective-permute-start | bytes 405512 | tf_op jit(solution)/shard_map/ppermute | solution.py:563
  3.9 5.0 %collective-permute-start.1 = (f32[264,128]{1,0:T(8,128)S(1)}, f32[264,128]{1,0:T(8,128)S(1)}, u32[]{:S(2)}, u32[]{:S(2)}) collective-permute-start(f32[264,128]{1,0:T(8,128)S(1)} %maximum_maximum_fusion), channel_id=1, source_target_pairs={{0,24},{4,12},{8,16},{12,4},{16,8},{20,28},{24,0},{28,20},{1,25},{... | collective-permute-start | bytes 405512 | tf_op jit(solution)/shard_map/ppermute | solution.py:575
  9.0 0.7 %copy-done.2 = f32[1024]{0:T(1024)S(1)} copy-done((f32[1024]{0:T(1024)S(1)}, f32[1024]{0:T(1024)}, u32[]{:S(2)}) %copy-start.2) | copy-done | bytes 4120
  9.6 0.6 %shard_map.120 = (f32[128,512]{1,0:T(8,128)S(1)}, bf16[512,128]{1,0:T(8,128)(2,1)S(1)}, f32[128,512]{1,0:T(8,128)S(1)}, f32[128,512]{1,0:T(8,128)S(1)}) custom-call(bf16[1,128,1024]{2,1,0:T(8,128)(2,1)S(1)} %copy-done, bf16[1,128,1024]{2,1,0:T(8,128)(2,1)S(1)} %get-tuple-element.77.key_ref.refs_1_.refs_0_, ...), custom_call_target="tpu_custom_call" | custom-call | bytes 1204224 | tf_op jit(solution)/shard_map/pallas_call | solution.py:535
  10.2 2.8 %collective-permute-done.1 = f32[264,128]{1,0:T(8,128)S(1)} collective-permute-done((f32[264,128]{1,0:T(8,128)S(1)}, f32[264,128]{1,0:T(8,128)S(1)}, u32[]{:S(2)}, u32[]{:S(2)}) %collective-permute-start.1) | collective-permute-done | bytes 135200 | tf_op jit(solution)/shard_map/ppermute | solution.py:575
  13.2 0.6 %shard_map.121 = (f32[128,512]{1,0:T(8,128)S(1)}, bf16[512,128]{1,0:T(8,128)(2,1)S(1)}, f32[128,512]{1,0:T(8,128)S(1)}, f32[128,512]{1,0:T(8,128)S(1)}) custom-call(bf16[1,128,1024]{2,1,0:T(8,128)(2,1)S(1)} %copy-done, bf16[1,128,1024]{2,1,0:T(8,128)(2,1)S(1)} %get-tuple-element.77.key_ref.refs_1_.refs_0_, ...), custom_call_target="tpu_custom_call" | custom-call | bytes 1204224 | tf_op jit(solution)/shard_map/pallas_call | solution.py:535
  13.8 4.4 %collective-permute-done.2 = f32[264,128]{1,0:T(8,128)S(1)} collective-permute-done((f32[264,128]{1,0:T(8,128)S(1)}, f32[264,128]{1,0:T(8,128)S(1)}, u32[]{:S(2)}, u32[]{:S(2)}) %collective-permute-start.2) | collective-permute-done | bytes 135200 | tf_op jit(solution)/shard_map/ppermute | solution.py:575
  18.4 0.7 %shard_map.122 = (bf16[128,512]{1,0:T(8,128)(2,1)S(1)}, bf16[128,512]{1,0:T(8,128)(2,1)S(1)}, f32[264,128]{1,0:T(8,128)S(1)}) custom-call(f32[128,512]{1,0:T(8,128)S(1)} %get-tuple-element.88.refs_0_, bf16[512,128]{1,0:T(8,128)(2,1)S(1)} %get-tuple-element.89.refs_1_, f32[128,512]{1,0:T(8,128)S(1)} %get-tuple-element.90.refs_2_.entry_ref, ...), custom_call_target="tpu_custom_call" | custom-call | bytes 1576960 | tf_op jit(solution)/shard_map/pallas_call | solution.py:535
  19.1 0.6 %collective-permute-done.3.state_ref.refs_4_.refs_6_ = f32[256,128]{1,0:T(8,128)S(1)} collective-permute-done((f32[256,128]{1,0:T(8,128)S(1)}, f32[256,128]{1,0:T(8,128)S(1)}, u32[]{:S(2)}, u32[]{:S(2)}) %collective-permute-start.3) | collective-permute-done | bytes 131104 | tf_op jit(solution)/shard_map/ppermute | solution.py:563
  19.7 0.7 %shard_map.123 = (bf16[128,512]{1,0:T(8,128)(2,1)S(1)}, bf16[128,512]{1,0:T(8,128)(2,1)S(1)}, f32[264,128]{1,0:T(8,128)S(1)}) custom-call(f32[128,512]{1,0:T(8,128)S(1)} %get-tuple-element.101.mixed_ref, bf16[512,128]{1,0:T(8,128)(2,1)S(1)} %get-tuple-element.102.turned_ref, f32[128,512]{1,0:T(8,128)S(1)} %get-tuple-element.103.entry_ref.refs_5_, ...), custom_call_target="tpu_custom_call" | custom-call | bytes 1712128 | tf_op jit(solution)/shard_map/pallas_call | solution.py:535
  20.7 1.2 %collective-permute-done.4 = f32[264,128]{1,0:T(8,128)S(1)} collective-permute-done((f32[264,128]{1,0:T(8,128)S(1)}, f32[264,128]{1,0:T(8,128)S(1)}, u32[]{:S(2)}, u32[]{:S(2)}) %collective-permute-start.4) | collective-permute-done | bytes 135200 | tf_op jit(solution)/shard_map/ppermute | solution.py:563
  22.0 2.8 %collective-permute-start.5 = (f32[264,128]{1,0:T(8,128)S(1)}, f32[264,128]{1,0:T(8,128)S(1)}, u32[]{:S(2)}, u32[]{:S(2)}) collective-permute-start(f32[264,128]{1,0:T(8,128)S(1)} %pad_maximum_fusion), channel_id=1, source_target_pairs={{0,24},{4,12},{8,16},{12,4},{16,8},{20,28},{24,0},{28,20},{1,25},{... | collective-permute-start | bytes 405512 | tf_op jit(solution)/shard_map/ppermute | solution.py:575
  24.8 1.0 %collective-permute-start.9 = (f32[8,128]{1,0:T(8,128)S(1)}, f32[8,128]{1,0:T(8,128)S(1)}, u32[]{:S(2)}, u32[]{:S(2)}) collective-permute-start(f32[8,128]{1,0:T(8,128)S(1)} %slice_add_fusion.1), channel_id=1, source_target_pairs={{0,11},{1,10},{2,9},{3,8},{4,13},{5,12},{6,15},{7,14},{8,3},{9,2},... | collective-permute-start | bytes 12296 | tf_op jit(solution)/shard_map/ppermute | solution.py:571
  25.8 0.5 %collective-permute-start.8 = (f32[8,128]{1,0:T(8,128)S(1)}, f32[8,128]{1,0:T(8,128)S(1)}, u32[]{:S(2)}, u32[]{:S(2)}) collective-permute-start(f32[8,128]{1,0:T(8,128)S(1)} %slice_add_fusion.1), channel_id=1, source_target_pairs={{0,2},{1,3},{2,0},{3,1},{4,14},{5,15},{6,12},{7,13},{8,10},{9,11},... | collective-permute-start | bytes 12296 | tf_op jit(solution)/shard_map/ppermute | solution.py:571
  26.3 1.5 %collective-permute-start.7 = (f32[8,128]{1,0:T(8,128)S(1)}, f32[8,128]{1,0:T(8,128)S(1)}, u32[]{:S(2)}, u32[]{:S(2)}) collective-permute-start(f32[8,128]{1,0:T(8,128)S(1)} %slice_add_fusion.1), channel_id=1, source_target_pairs={{0,1},{1,0},{2,3},{3,2},{4,7},{5,6},{6,5},{7,4},{8,9},{9,8},{10,11... | collective-permute-start | bytes 12296 | tf_op jit(solution)/shard_map/ppermute | solution.py:571
  27.8 1.1 %collective-permute-done.5 = f32[264,128]{1,0:T(8,128)S(1)} collective-permute-done((f32[264,128]{1,0:T(8,128)S(1)}, f32[264,128]{1,0:T(8,128)S(1)}, u32[]{:S(2)}, u32[]{:S(2)}) %collective-permute-start.5) | collective-permute-done | bytes 135200 | tf_op jit(solution)/shard_map/ppermute | solution.py:575
  28.9 0.9 %collective-permute-start.6 = (f32[256,128]{1,0:T(8,128)S(1)}, f32[256,128]{1,0:T(8,128)S(1)}, u32[]{:S(2)}, u32[]{:S(2)}) collective-permute-start(f32[256,128]{1,0:T(8,128)S(1)} %fusion.24), channel_id=1, source_target_pairs={{0,8},{4,28},{8,0},{12,20},{16,24},{20,12},{24,16},{28,4},{1,9},{5... | collective-permute-start | bytes 393224 | tf_op jit(solution)/shard_map/ppermute | solution.py:575
  29.8 0.7 %collective-permute-done.9 = f32[8,128]{1,0:T(8,128)S(1)} collective-permute-done((f32[8,128]{1,0:T(8,128)S(1)}, f32[8,128]{1,0:T(8,128)S(1)}, u32[]{:S(2)}, u32[]{:S(2)}) %collective-permute-start.9) | collective-permute-done | bytes 4128 | tf_op jit(solution)/shard_map/ppermute | solution.py:571
  30.6 1.9 %collective-permute-start.10 = (f32[8,128]{1,0:T(8,128)S(1)}, f32[8,128]{1,0:T(8,128)S(1)}, u32[]{:S(2)}, u32[]{:S(2)}) collective-permute-start(f32[8,128]{1,0:T(8,128)S(1)} %fusion.29), channel_id=1, source_target_pairs={{0,16},{4,20},{8,24},{12,28},{16,0},{20,4},{24,8},{28,12},{1,17},{... | collective-permute-start | bytes 12296 | tf_op jit(solution)/shard_map/ppermute | solution.py:563
  32.5 1.5 %shard_map.125 = (bf16[128,512]{1,0:T(8,128)(2,1)S(1)}, f32[128,512]{1,0:T(8,128)S(1)}, f32[128,512]{1,0:T(8,128)S(1)}, f32[8,128]{1,0:T(8,128)S(1)}, f32[128,512]{1,0:T(8,128)S(1)}) custom-call(bf16[1,128,1024]{2,1,0:T(8,128)(2,1)S(1)} %copy-done, bf16[1,128,1024]{2,1,0:T(8,128)(2,1)S(1)} %get-tuple-element.77.key_ref.refs_1_.refs_0_, ...), custom_call_target="tpu_custom_call" | custom-call | bytes 1462272 | tf_op jit(solution)/shard_map/pallas_call | solution.py:535
  34.0 1.6 %shard_map.124 = (bf16[1,128,1024]{2,1,0:T(8,128)(2,1)}, bf16[128,512]{1,0:T(8,128)(2,1)S(1)}, f32[128,512]{1,0:T(8,128)S(1)}, f32[128,512]{1,0:T(8,128)S(1)}, f...) custom-call(bf16[1,128,1024]{2,1,0:T(8,128)(2,1)S(1)} %copy-done, ...), custom_call_target="tpu_custom_call" | custom-call | bytes 1724416 | tf_op jit(solution)/shard_map/pallas_call | solution.py:535
  36.3 0.8 %collective-permute-done.11.refs_7_ = f32[264,128]{1,0:T(8,128)S(1)} collective-permute-done((f32[264,128]{1,0:T(8,128)S(1)}, f32[264,128]{1,0:T(8,128)S(1)}, u32[]{:S(2)}, u32[]{:S(2)}) %collective-permute-start.11) | collective-permute-done | bytes 135200 | tf_op jit(solution)/shard_map/ppermute | solution.py:563
  37.1 1.3 %shard_map.127 = (bf16[1,128,1024]{2,1,0:T(8,128)(2,1)}, bf16[1,128,1024]{2,1,0:T(8,128)(2,1)}, bf16[1,128,1024]{2,1,0:T(8,128)(2,1)}, f32[1,16,128]{2,1,0:T(8,128)}, f32[8,128]{1,0:T(8,128)}) custom-call(bf16[1,128,1024]{2,1,0:T(8,128)(2,1)S(1)} %get-tuple-element.77.key_ref.refs_1_.refs_0_, ...), custom_call_target="tpu_custom_call" | custom-call | bytes 2199552 | tf_op jit(solution)/shard_map/pallas_call | solution.py:535
  (35 shorter events, 2.5 us)
Async XLA Ops:
  2.2 1.5 %collective-permute-start = (f32[264,128]{1,0:T(8,128)S(1)}, f32[264,128]{1,0:T(8,128)S(1)}, u32[]{:S(2)}, u32[]{:S(2)}) collective-permute-start(f32[264,128]{1,0:T(8,128)S(1)} %get-tuple-element.76), channel_id=1, source_target_pairs={{0,4},{4,0},{8,12},{12,8},{16,20},{20,16},{24,28},{28,24},{1,5},{5... | collective-permute-start | bytes 405512 | tf_op jit(solution)/shard_map/ppermute | solution.py:563
  3.8 5.2 %copy-start = (bf16[1,128,1024]{2,1,0:T(8,128)(2,1)S(1)}, bf16[1,128,1024]{2,1,0:T(8,128)(2,1)}, u32[]{:S(2)}) copy-start(bf16[1,128,1024]{2,1,0:T(8,128)(2,1)} %query_ref.7) | copy-start | bytes 786436
  3.8 5.2 %copy-start.1 = (bf16[1,128,1024]{2,1,0:T(8,128)(2,1)S(1)}, bf16[1,128,1024]{2,1,0:T(8,128)(2,1)}, u32[]{:S(2)}) copy-start(bf16[1,128,1024]{2,1,0:T(8,128)(2,1)} %upstream_ref.5) | copy-start | bytes 786436
  3.9 9.1 %collective-permute-start.1 = (f32[264,128]{1,0:T(8,128)S(1)}, f32[264,128]{1,0:T(8,128)S(1)}, u32[]{:S(2)}, u32[]{:S(2)}) collective-permute-start(f32[264,128]{1,0:T(8,128)S(1)} %maximum_maximum_fusion), channel_id=1, source_target_pairs={{0,24},{4,12},{8,16},{12,4},{16,8},{20,28},{24,0},{28,20},{1,25},{... | collective-permute-start | bytes 405512 | tf_op jit(solution)/shard_map/ppermute | solution.py:575
  9.0 0.7 %copy-start.2 = (f32[1024]{0:T(1024)S(1)}, f32[1024]{0:T(1024)}, u32[]{:S(2)}) copy-start(f32[1024]{0:T(1024)} %param.12) | copy-start | bytes 12292
  13.2 5.1 %collective-permute-start.2 = (f32[264,128]{1,0:T(8,128)S(1)}, f32[264,128]{1,0:T(8,128)S(1)}, u32[]{:S(2)}, u32[]{:S(2)}) collective-permute-start(f32[264,128]{1,0:T(8,128)S(1)} %maximum_maximum_fusion.1), channel_id=1, source_target_pairs={{0,8},{4,28},{8,0},{12,20},{16,24},{20,12},{24,16},{28,4},{1,9},{5... | collective-permute-start | bytes 405512 | tf_op jit(solution)/shard_map/ppermute | solution.py:575
  18.3 1.4 %collective-permute-start.3 = (f32[256,128]{1,0:T(8,128)S(1)}, f32[256,128]{1,0:T(8,128)S(1)}, u32[]{:S(2)}, u32[]{:S(2)}) collective-permute-start(f32[256,128]{1,0:T(8,128)S(1)} %get-tuple-element.149), channel_id=1, source_target_pairs={{0,4},{4,0},{8,12},{12,8},{16,20},{20,16},{24,28},{28,24},{1,5},{5... | collective-permute-start | bytes 393224 | tf_op jit(solution)/shard_map/ppermute | solution.py:563
  20.5 1.4 %collective-permute-start.4 = (f32[264,128]{1,0:T(8,128)S(1)}, f32[264,128]{1,0:T(8,128)S(1)}, u32[]{:S(2)}, u32[]{:S(2)}) collective-permute-start(f32[264,128]{1,0:T(8,128)S(1)} %get-tuple-element.105), channel_id=1, source_target_pairs={{0,4},{4,0},{8,12},{12,8},{16,20},{20,16},{24,28},{28,24},{1,5},{5... | collective-permute-start | bytes 405512 | tf_op jit(solution)/shard_map/ppermute | solution.py:563
  22.0 6.9 %collective-permute-start.5 = (f32[264,128]{1,0:T(8,128)S(1)}, f32[264,128]{1,0:T(8,128)S(1)}, u32[]{:S(2)}, u32[]{:S(2)}) collective-permute-start(f32[264,128]{1,0:T(8,128)S(1)} %pad_maximum_fusion), channel_id=1, source_target_pairs={{0,24},{4,12},{8,16},{12,4},{16,8},{20,28},{24,0},{28,20},{1,25},{... | collective-permute-start | bytes 405512 | tf_op jit(solution)/shard_map/ppermute | solution.py:575
  24.8 5.8 %collective-permute-start.9 = (f32[8,128]{1,0:T(8,128)S(1)}, f32[8,128]{1,0:T(8,128)S(1)}, u32[]{:S(2)}, u32[]{:S(2)}) collective-permute-start(f32[8,128]{1,0:T(8,128)S(1)} %slice_add_fusion.1), channel_id=1, source_target_pairs={{0,11},{1,10},{2,9},{3,8},{4,13},{5,12},{6,15},{7,14},{8,3},{9,2},... | collective-permute-start | bytes 12296 | tf_op jit(solution)/shard_map/ppermute | solution.py:571
  25.8 4.8 %collective-permute-start.8 = (f32[8,128]{1,0:T(8,128)S(1)}, f32[8,128]{1,0:T(8,128)S(1)}, u32[]{:S(2)}, u32[]{:S(2)}) collective-permute-start(f32[8,128]{1,0:T(8,128)S(1)} %slice_add_fusion.1), channel_id=1, source_target_pairs={{0,2},{1,3},{2,0},{3,1},{4,14},{5,15},{6,12},{7,13},{8,10},{9,11},... | collective-permute-start | bytes 12296 | tf_op jit(solution)/shard_map/ppermute | solution.py:571
  26.3 4.3 %collective-permute-start.7 = (f32[8,128]{1,0:T(8,128)S(1)}, f32[8,128]{1,0:T(8,128)S(1)}, u32[]{:S(2)}, u32[]{:S(2)}) collective-permute-start(f32[8,128]{1,0:T(8,128)S(1)} %slice_add_fusion.1), channel_id=1, source_target_pairs={{0,1},{1,0},{2,3},{3,2},{4,7},{5,6},{6,5},{7,4},{8,9},{9,8},{10,11... | collective-permute-start | bytes 12296 | tf_op jit(solution)/shard_map/ppermute | solution.py:571
  28.9 6.7 %collective-permute-start.6 = (f32[256,128]{1,0:T(8,128)S(1)}, f32[256,128]{1,0:T(8,128)S(1)}, u32[]{:S(2)}, u32[]{:S(2)}) collective-permute-start(f32[256,128]{1,0:T(8,128)S(1)} %fusion.24), channel_id=1, source_target_pairs={{0,8},{4,28},{8,0},{12,20},{16,24},{20,12},{24,16},{28,4},{1,9},{5... | collective-permute-start | bytes 393224 | tf_op jit(solution)/shard_map/ppermute | solution.py:575
  30.6 5.0 %collective-permute-start.10 = (f32[8,128]{1,0:T(8,128)S(1)}, f32[8,128]{1,0:T(8,128)S(1)}, u32[]{:S(2)}, u32[]{:S(2)}) collective-permute-start(f32[8,128]{1,0:T(8,128)S(1)} %fusion.29), channel_id=1, source_target_pairs={{0,16},{4,20},{8,24},{12,28},{16,0},{20,4},{24,8},{28,12},{1,17},{... | collective-permute-start | bytes 12296 | tf_op jit(solution)/shard_map/ppermute | solution.py:563
  35.7 1.4 %collective-permute-start.11 = (f32[264,128]{1,0:T(8,128)S(1)}, f32[264,128]{1,0:T(8,128)S(1)}, u32[]{:S(2)}, u32[]{:S(2)}) collective-permute-start(f32[264,128]{1,0:T(8,128)S(1)} %pad_maximum_fusion.1), channel_id=1, source_target_pairs={{0,4},{4,0},{8,12},{12,8},{16,20},{20,16},{24,28},{28,24},{1,5},{5... | collective-permute-start | bytes 405512 | tf_op jit(solution)/shard_map/ppermute | solution.py:563

commit v8 on v7

--- a/solution.py
+++ b/solution.py
@@ -271,7 +271,7 @@
     half = own_half(mine)
     gains = pick_gains(gain_ref, half)
     own = left_lanes((LANES, LANES)) == (lax.broadcasted_iota(jnp.int32, (LANES, LANES), 0) < 64)
-    average = twice(jnp.where(own, 1.0 / 64.0, 0.0).astype(BF16), 0)
+    average = jnp.where(own, 1.0 / 64.0, 0.0).astype(BF16)
     places = [pl.ds(pair * LANES, LANES) for pair in range(PAIRS)]
     lanes = [pair_lanes(half, width, pair) for pair in range(PAIRS)]
     states = [
@@ -285,7 +285,7 @@
         for pair in range(PAIRS)
     ]
     squares = dot(
-        jnp.concatenate([stacked(mixture * mixture, 1) for mixture in mixtures], axis=0), average
+        jnp.concatenate([(mixture * mixture).astype(BF16) for mixture in mixtures], axis=0), average
     )
     normeds, inverses, grads, products, gain_parts = [], [], [], [], []
     for pair in range(PAIRS):
@@ -294,7 +294,7 @@
         gain = gains[pair : pair + 1]
         upstream = upstream_ref[0, :, lanes[pair]].astype(F32)
         grad_normed = grad_ref[:, places[pair]]
-        products.append(stacked(grad_normed * normed, 1))
+        products.append((grad_normed * normed).astype(BF16))
         layer_ref[:, places[pair]] = (normed * gain).astype(BF16)
         gain_parts.append(jnp.sum(upstream * normed, axis=0, keepdims=True))
         normeds.append(normed)

time: 38.6 us -> 38.6 us (level)
  transfers between devices with their start and end apart: 12 -> 12, of which waited for: 8 -> 8; matrix products, arithmetic and copies ran while one was open for 0% -> 0% of each run, Pallas kernels for 16% -> 15%
where the time goes in v8:
time: 38.6 us; the launch traced here: 38.4 us
  starting transfers between devices  14.6 us (38%)
  waiting for transfers between devices  12.2 us (32%)
  Pallas kernels  9.45 us (24%)
  between operations  0.82 us (2%)
  local copies, waits for them, and re-layouts  0.77 us (2%)
  other arithmetic  0.57 us (1%)
    pallas_call x10, Pallas kernels, call(): pl.pallas_call(kernel, in_specs=[pl.BlockSpec(memory_space=memory) for a,...  9.45 us
    ppermute x4, starting transfers between devices, exchange_by_core(): return lax.ppermute(x, 'seq', [(i, i ^ bits[i & 1]) for i in range(blocks)])  8.83 us
    ppermute x4, waiting for transfers between devices, exchange_by_core(): return lax.ppermute(x, 'seq', [(i, i ^ bits[i & 1]) for i in range(blocks)])  8.33 us
    ppermute x5, waiting for transfers between devices, exchange(): return lax.ppermute(x, axis, [(i, i ^ bit) for i in range(size)])  3.08 us
    ppermute x3, starting transfers between devices, exchange_mixed(): return lax.ppermute(x, ('seq', 'dp'), pairs)  3.01 us
    ppermute x5, starting transfers between devices, exchange(): return lax.ppermute(x, axis, [(i, i ^ bit) for i in range(size)])  2.75 us
  transfers between devices with their start and end apart: 12, of which 8 were waited for; matrix products, arithmetic and copies ran while one was open for 0% of the time, Pallas kernels for 15%

profile of v8, /device:TPU:0, one launch (start us, length us, event | category | flops | bytes accessed | tf_op | source)
XLA Modules:
  0.0 38.4 jit_solution(1882198747666315021)
XLA Ops:
  0.6 1.6 %shard_map.118 = (f32[264,128]{1,0:T(8,128)S(1)}, f32[168,128]{1,0:T(8,128)S(1)}, bf16[1,128,1024]{2,1,0:T(8,128)(2,1)S(1)}, bf16[1,128,1024]{2,1,0:T(8,128)(2,1)S(1)}) custom-call(bf16[1,128,1024]{2,1,0:T(8,128)(2,1)} %key_ref.1, bf16[1,128,1024]{2,1,0:T(8,128)(2,1)} %value_ref.1, f32[1,16,128]{2,1,0:T(8,128)} %bitcast.111, s32[1,128]{1,0:T(1,128)} %restart_ref.1), custom_call_target="tpu_custom_call" | custom-call | tf_op jit(solution)/shard_map/pallas_call | solution.py:535
  2.2 0.5 %collective-permute-start = (f32[264,128]{1,0:T(8,128)S(1)}, f32[264,128]{1,0:T(8,128)S(1)}, u32[]{:S(2)}, u32[]{:S(2)}) collective-permute-start(f32[264,128]{1,0:T(8,128)S(1)} %get-tuple-element.76), channel_id=1, source_target_pairs={{0,4},{4,0},{8,12},{12,8},{16,20},{20,16},{24,28},{28,24},{1,5},{5... | collective-permute-start | bytes 405512 | tf_op jit(solution)/shard_map/ppermute | solution.py:563
  3.9 5.0 %collective-permute-start.1 = (f32[264,128]{1,0:T(8,128)S(1)}, f32[264,128]{1,0:T(8,128)S(1)}, u32[]{:S(2)}, u32[]{:S(2)}) collective-permute-start(f32[264,128]{1,0:T(8,128)S(1)} %maximum_maximum_fusion), channel_id=1, source_target_pairs={{0,24},{4,12},{8,16},{12,4},{16,8},{20,28},{24,0},{28,20},{1,25},{... | collective-permute-start | bytes 405512 | tf_op jit(solution)/shard_map/ppermute | solution.py:575
  9.0 0.7 %copy-done.2 = f32[1024]{0:T(1024)S(1)} copy-done((f32[1024]{0:T(1024)S(1)}, f32[1024]{0:T(1024)}, u32[]{:S(2)}) %copy-start.2) | copy-done | bytes 4120
  9.6 0.6 %shard_map.120 = (f32[128,512]{1,0:T(8,128)S(1)}, bf16[512,128]{1,0:T(8,128)(2,1)S(1)}, f32[128,512]{1,0:T(8,128)S(1)}, f32[128,512]{1,0:T(8,128)S(1)}) custom-call(bf16[1,128,1024]{2,1,0:T(8,128)(2,1)S(1)} %copy-done, bf16[1,128,1024]{2,1,0:T(8,128)(2,1)S(1)} %get-tuple-element.77.key_ref.refs_1_.refs_0_, ...), custom_call_target="tpu_custom_call" | custom-call | bytes 1204224 | tf_op jit(solution)/shard_map/pallas_call | solution.py:535
  10.2 2.8 %collective-permute-done.1 = f32[264,128]{1,0:T(8,128)S(1)} collective-permute-done((f32[264,128]{1,0:T(8,128)S(1)}, f32[264,128]{1,0:T(8,128)S(1)}, u32[]{:S(2)}, u32[]{:S(2)}) %collective-permute-start.1) | collective-permute-done | bytes 135200 | tf_op jit(solution)/shard_map/ppermute | solution.py:575
  13.2 0.6 %shard_map.121 = (f32[128,512]{1,0:T(8,128)S(1)}, bf16[512,128]{1,0:T(8,128)(2,1)S(1)}, f32[128,512]{1,0:T(8,128)S(1)}, f32[128,512]{1,0:T(8,128)S(1)}) custom-call(bf16[1,128,1024]{2,1,0:T(8,128)(2,1)S(1)} %copy-done, bf16[1,128,1024]{2,1,0:T(8,128)(2,1)S(1)} %get-tuple-element.77.key_ref.refs_1_.refs_0_, ...), custom_call_target="tpu_custom_call" | custom-call | bytes 1204224 | tf_op jit(solution)/shard_map/pallas_call | solution.py:535
  13.8 4.4 %collective-permute-done.2 = f32[264,128]{1,0:T(8,128)S(1)} collective-permute-done((f32[264,128]{1,0:T(8,128)S(1)}, f32[264,128]{1,0:T(8,128)S(1)}, u32[]{:S(2)}, u32[]{:S(2)}) %collective-permute-start.2) | collective-permute-done | bytes 135200 | tf_op jit(solution)/shard_map/ppermute | solution.py:575
  18.4 0.7 %shard_map.122 = (bf16[128,512]{1,0:T(8,128)(2,1)S(1)}, bf16[128,512]{1,0:T(8,128)(2,1)S(1)}, f32[264,128]{1,0:T(8,128)S(1)}) custom-call(f32[128,512]{1,0:T(8,128)S(1)} %get-tuple-element.88.refs_0_, bf16[512,128]{1,0:T(8,128)(2,1)S(1)} %get-tuple-element.89.refs_1_, f32[128,512]{1,0:T(8,128)S(1)} %get-tuple-element.90.refs_2_.entry_ref, ...), custom_call_target="tpu_custom_call" | custom-call | bytes 1576960 | tf_op jit(solution)/shard_map/pallas_call | solution.py:535
  19.1 0.6 %collective-permute-done.3.state_ref.refs_4_.refs_6_ = f32[256,128]{1,0:T(8,128)S(1)} collective-permute-done((f32[256,128]{1,0:T(8,128)S(1)}, f32[256,128]{1,0:T(8,128)S(1)}, u32[]{:S(2)}, u32[]{:S(2)}) %collective-permute-start.3) | collective-permute-done | bytes 131104 | tf_op jit(solution)/shard_map/ppermute | solution.py:563
  19.7 0.7 %shard_map.123 = (bf16[128,512]{1,0:T(8,128)(2,1)S(1)}, bf16[128,512]{1,0:T(8,128)(2,1)S(1)}, f32[264,128]{1,0:T(8,128)S(1)}) custom-call(f32[128,512]{1,0:T(8,128)S(1)} %get-tuple-element.101.mixed_ref, bf16[512,128]{1,0:T(8,128)(2,1)S(1)} %get-tuple-element.102.turned_ref, f32[128,512]{1,0:T(8,128)S(1)} %get-tuple-element.103.entry_ref.refs_5_, ...), custom_call_target="tpu_custom_call" | custom-call | bytes 1712128 | tf_op jit(solution)/shard_map/pallas_call | solution.py:535
  20.6 1.2 %collective-permute-done.4 = f32[264,128]{1,0:T(8,128)S(1)} collective-permute-done((f32[264,128]{1,0:T(8,128)S(1)}, f32[264,128]{1,0:T(8,128)S(1)}, u32[]{:S(2)}, u32[]{:S(2)}) %collective-permute-start.4) | collective-permute-done | bytes 135200 | tf_op jit(solution)/shard_map/ppermute | solution.py:563
  21.9 2.8 %collective-permute-start.5 = (f32[264,128]{1,0:T(8,128)S(1)}, f32[264,128]{1,0:T(8,128)S(1)}, u32[]{:S(2)}, u32[]{:S(2)}) collective-permute-start(f32[264,128]{1,0:T(8,128)S(1)} %pad_maximum_fusion), channel_id=1, source_target_pairs={{0,24},{4,12},{8,16},{12,4},{16,8},{20,28},{24,0},{28,20},{1,25},{... | collective-permute-start | bytes 405512 | tf_op jit(solution)/shard_map/ppermute | solution.py:575
  24.7 1.0 %collective-permute-start.9 = (f32[8,128]{1,0:T(8,128)S(1)}, f32[8,128]{1,0:T(8,128)S(1)}, u32[]{:S(2)}, u32[]{:S(2)}) collective-permute-start(f32[8,128]{1,0:T(8,128)S(1)} %slice_add_fusion.1), channel_id=1, source_target_pairs={{0,11},{1,10},{2,9},{3,8},{4,13},{5,12},{6,15},{7,14},{8,3},{9,2},... | collective-permute-start | bytes 12296 | tf_op jit(solution)/shard_map/ppermute | solution.py:571
  25.7 0.5 %collective-permute-start.8 = (f32[8,128]{1,0:T(8,128)S(1)}, f32[8,128]{1,0:T(8,128)S(1)}, u32[]{:S(2)}, u32[]{:S(2)}) collective-permute-start(f32[8,128]{1,0:T(8,128)S(1)} %slice_add_fusion.1), channel_id=1, source_target_pairs={{0,2},{1,3},{2,0},{3,1},{4,14},{5,15},{6,12},{7,13},{8,10},{9,11},... | collective-permute-start | bytes 12296 | tf_op jit(solution)/shard_map/ppermute | solution.py:571
  26.2 1.5 %collective-permute-start.7 = (f32[8,128]{1,0:T(8,128)S(1)}, f32[8,128]{1,0:T(8,128)S(1)}, u32[]{:S(2)}, u32[]{:S(2)}) collective-permute-start(f32[8,128]{1,0:T(8,128)S(1)} %slice_add_fusion.1), channel_id=1, source_target_pairs={{0,1},{1,0},{2,3},{3,2},{4,7},{5,6},{6,5},{7,4},{8,9},{9,8},{10,11... | collective-permute-start | bytes 12296 | tf_op jit(solution)/shard_map/ppermute | solution.py:571
  27.7 1.1 %collective-permute-done.5 = f32[264,128]{1,0:T(8,128)S(1)} collective-permute-done((f32[264,128]{1,0:T(8,128)S(1)}, f32[264,128]{1,0:T(8,128)S(1)}, u32[]{:S(2)}, u32[]{:S(2)}) %collective-permute-start.5) | collective-permute-done | bytes 135200 | tf_op jit(solution)/shard_map/ppermute | solution.py:575
  28.9 0.9 %collective-permute-start.6 = (f32[256,128]{1,0:T(8,128)S(1)}, f32[256,128]{1,0:T(8,128)S(1)}, u32[]{:S(2)}, u32[]{:S(2)}) collective-permute-start(f32[256,128]{1,0:T(8,128)S(1)} %fusion.24), channel_id=1, source_target_pairs={{0,8},{4,28},{8,0},{12,20},{16,24},{20,12},{24,16},{28,4},{1,9},{5... | collective-permute-start | bytes 393224 | tf_op jit(solution)/shard_map/ppermute | solution.py:575
  29.8 0.7 %collective-permute-done.9 = f32[8,128]{1,0:T(8,128)S(1)} collective-permute-done((f32[8,128]{1,0:T(8,128)S(1)}, f32[8,128]{1,0:T(8,128)S(1)}, u32[]{:S(2)}, u32[]{:S(2)}) %collective-permute-start.9) | collective-permute-done | bytes 4128 | tf_op jit(solution)/shard_map/ppermute | solution.py:571
  30.5 1.9 %collective-permute-start.10 = (f32[8,128]{1,0:T(8,128)S(1)}, f32[8,128]{1,0:T(8,128)S(1)}, u32[]{:S(2)}, u32[]{:S(2)}) collective-permute-start(f32[8,128]{1,0:T(8,128)S(1)} %fusion.29), channel_id=1, source_target_pairs={{0,16},{4,20},{8,24},{12,28},{16,0},{20,4},{24,8},{28,12},{1,17},{... | collective-permute-start | bytes 12296 | tf_op jit(solution)/shard_map/ppermute | solution.py:563
  32.4 1.5 %shard_map.125 = (bf16[128,512]{1,0:T(8,128)(2,1)S(1)}, f32[128,512]{1,0:T(8,128)S(1)}, f32[128,512]{1,0:T(8,128)S(1)}, f32[8,128]{1,0:T(8,128)S(1)}, f32[128,512]{1,0:T(8,128)S(1)}) custom-call(bf16[1,128,1024]{2,1,0:T(8,128)(2,1)S(1)} %copy-done, bf16[1,128,1024]{2,1,0:T(8,128)(2,1)S(1)} %get-tuple-element.77.key_ref.refs_1_.refs_0_, ...), custom_call_target="tpu_custom_call" | custom-call | bytes 1462272 | tf_op jit(solution)/shard_map/pallas_call | solution.py:535
  33.9 1.6 %shard_map.124 = (bf16[1,128,1024]{2,1,0:T(8,128)(2,1)}, bf16[128,512]{1,0:T(8,128)(2,1)S(1)}, f32[128,512]{1,0:T(8,128)S(1)}, f32[128,512]{1,0:T(8,128)S(1)}, f...) custom-call(bf16[1,128,1024]{2,1,0:T(8,128)(2,1)S(1)} %copy-done, ...), custom_call_target="tpu_custom_call" | custom-call | bytes 1724416 | tf_op jit(solution)/shard_map/pallas_call | solution.py:535
  36.2 0.8 %collective-permute-done.11.refs_7_ = f32[264,128]{1,0:T(8,128)S(1)} collective-permute-done((f32[264,128]{1,0:T(8,128)S(1)}, f32[264,128]{1,0:T(8,128)S(1)}, u32[]{:S(2)}, u32[]{:S(2)}) %collective-permute-start.11) | collective-permute-done | bytes 135200 | tf_op jit(solution)/shard_map/ppermute | solution.py:563
  37.1 1.3 %shard_map.127 = (bf16[1,128,1024]{2,1,0:T(8,128)(2,1)}, bf16[1,128,1024]{2,1,0:T(8,128)(2,1)}, bf16[1,128,1024]{2,1,0:T(8,128)(2,1)}, f32[1,16,128]{2,1,0:T(8,128)}, f32[8,128]{1,0:T(8,128)}) custom-call(bf16[1,128,1024]{2,1,0:T(8,128)(2,1)S(1)} %get-tuple-element.77.key_ref.refs_1_.refs_0_, ...), custom_call_target="tpu_custom_call" | custom-call | bytes 2199552 | tf_op jit(solution)/shard_map/pallas_call | solution.py:535
  (35 shorter events, 2.5 us)
Async XLA Ops:
  2.2 1.5 %collective-permute-start = (f32[264,128]{1,0:T(8,128)S(1)}, f32[264,128]{1,0:T(8,128)S(1)}, u32[]{:S(2)}, u32[]{:S(2)}) collective-permute-start(f32[264,128]{1,0:T(8,128)S(1)} %get-tuple-element.76), channel_id=1, source_target_pairs={{0,4},{4,0},{8,12},{12,8},{16,20},{20,16},{24,28},{28,24},{1,5},{5... | collective-permute-start | bytes 405512 | tf_op jit(solution)/shard_map/ppermute | solution.py:563
  3.8 5.2 %copy-start = (bf16[1,128,1024]{2,1,0:T(8,128)(2,1)S(1)}, bf16[1,128,1024]{2,1,0:T(8,128)(2,1)}, u32[]{:S(2)}) copy-start(bf16[1,128,1024]{2,1,0:T(8,128)(2,1)} %query_ref.7) | copy-start | bytes 786436
  3.8 5.2 %copy-start.1 = (bf16[1,128,1024]{2,1,0:T(8,128)(2,1)S(1)}, bf16[1,128,1024]{2,1,0:T(8,128)(2,1)}, u32[]{:S(2)}) copy-start(bf16[1,128,1024]{2,1,0:T(8,128)(2,1)} %upstream_ref.5) | copy-start | bytes 786436
  3.9 9.1 %collective-permute-start.1 = (f32[264,128]{1,0:T(8,128)S(1)}, f32[264,128]{1,0:T(8,128)S(1)}, u32[]{:S(2)}, u32[]{:S(2)}) collective-permute-start(f32[264,128]{1,0:T(8,128)S(1)} %maximum_maximum_fusion), channel_id=1, source_target_pairs={{0,24},{4,12},{8,16},{12,4},{16,8},{20,28},{24,0},{28,20},{1,25},{... | collective-permute-start | bytes 405512 | tf_op jit(solution)/shard_map/ppermute | solution.py:575
  9.0 0.7 %copy-start.2 = (f32[1024]{0:T(1024)S(1)}, f32[1024]{0:T(1024)}, u32[]{:S(2)}) copy-start(f32[1024]{0:T(1024)} %param.12) | copy-start | bytes 12292
  13.2 5.1 %collective-permute-start.2 = (f32[264,128]{1,0:T(8,128)S(1)}, f32[264,128]{1,0:T(8,128)S(1)}, u32[]{:S(2)}, u32[]{:S(2)}) collective-permute-start(f32[264,128]{1,0:T(8,128)S(1)} %maximum_maximum_fusion.1), channel_id=1, source_target_pairs={{0,8},{4,28},{8,0},{12,20},{16,24},{20,12},{24,16},{28,4},{1,9},{5... | collective-permute-start | bytes 405512 | tf_op jit(solution)/shard_map/ppermute | solution.py:575
  18.3 1.4 %collective-permute-start.3 = (f32[256,128]{1,0:T(8,128)S(1)}, f32[256,128]{1,0:T(8,128)S(1)}, u32[]{:S(2)}, u32[]{:S(2)}) collective-permute-start(f32[256,128]{1,0:T(8,128)S(1)} %get-tuple-element.149), channel_id=1, source_target_pairs={{0,4},{4,0},{8,12},{12,8},{16,20},{20,16},{24,28},{28,24},{1,5},{5... | collective-permute-start | bytes 393224 | tf_op jit(solution)/shard_map/ppermute | solution.py:563
  20.4 1.4 %collective-permute-start.4 = (f32[264,128]{1,0:T(8,128)S(1)}, f32[264,128]{1,0:T(8,128)S(1)}, u32[]{:S(2)}, u32[]{:S(2)}) collective-permute-start(f32[264,128]{1,0:T(8,128)S(1)} %get-tuple-element.105), channel_id=1, source_target_pairs={{0,4},{4,0},{8,12},{12,8},{16,20},{20,16},{24,28},{28,24},{1,5},{5... | collective-permute-start | bytes 405512 | tf_op jit(solution)/shard_map/ppermute | solution.py:563
  21.9 6.9 %collective-permute-start.5 = (f32[264,128]{1,0:T(8,128)S(1)}, f32[264,128]{1,0:T(8,128)S(1)}, u32[]{:S(2)}, u32[]{:S(2)}) collective-permute-start(f32[264,128]{1,0:T(8,128)S(1)} %pad_maximum_fusion), channel_id=1, source_target_pairs={{0,24},{4,12},{8,16},{12,4},{16,8},{20,28},{24,0},{28,20},{1,25},{... | collective-permute-start | bytes 405512 | tf_op jit(solution)/shard_map/ppermute | solution.py:575
  24.7 5.8 %collective-permute-start.9 = (f32[8,128]{1,0:T(8,128)S(1)}, f32[8,128]{1,0:T(8,128)S(1)}, u32[]{:S(2)}, u32[]{:S(2)}) collective-permute-start(f32[8,128]{1,0:T(8,128)S(1)} %slice_add_fusion.1), channel_id=1, source_target_pairs={{0,11},{1,10},{2,9},{3,8},{4,13},{5,12},{6,15},{7,14},{8,3},{9,2},... | collective-permute-start | bytes 12296 | tf_op jit(solution)/shard_map/ppermute | solution.py:571
  25.7 4.8 %collective-permute-start.8 = (f32[8,128]{1,0:T(8,128)S(1)}, f32[8,128]{1,0:T(8,128)S(1)}, u32[]{:S(2)}, u32[]{:S(2)}) collective-permute-start(f32[8,128]{1,0:T(8,128)S(1)} %slice_add_fusion.1), channel_id=1, source_target_pairs={{0,2},{1,3},{2,0},{3,1},{4,14},{5,15},{6,12},{7,13},{8,10},{9,11},... | collective-permute-start | bytes 12296 | tf_op jit(solution)/shard_map/ppermute | solution.py:571
  26.2 4.3 %collective-permute-start.7 = (f32[8,128]{1,0:T(8,128)S(1)}, f32[8,128]{1,0:T(8,128)S(1)}, u32[]{:S(2)}, u32[]{:S(2)}) collective-permute-start(f32[8,128]{1,0:T(8,128)S(1)} %slice_add_fusion.1), channel_id=1, source_target_pairs={{0,1},{1,0},{2,3},{3,2},{4,7},{5,6},{6,5},{7,4},{8,9},{9,8},{10,11... | collective-permute-start | bytes 12296 | tf_op jit(solution)/shard_map/ppermute | solution.py:571
  28.9 6.7 %collective-permute-start.6 = (f32[256,128]{1,0:T(8,128)S(1)}, f32[256,128]{1,0:T(8,128)S(1)}, u32[]{:S(2)}, u32[]{:S(2)}) collective-permute-start(f32[256,128]{1,0:T(8,128)S(1)} %fusion.24), channel_id=1, source_target_pairs={{0,8},{4,28},{8,0},{12,20},{16,24},{20,12},{24,16},{28,4},{1,9},{5... | collective-permute-start | bytes 393224 | tf_op jit(solution)/shard_map/ppermute | solution.py:575
  30.5 5.0 %collective-permute-start.10 = (f32[8,128]{1,0:T(8,128)S(1)}, f32[8,128]{1,0:T(8,128)S(1)}, u32[]{:S(2)}, u32[]{:S(2)}) collective-permute-start(f32[8,128]{1,0:T(8,128)S(1)} %fusion.29), channel_id=1, source_target_pairs={{0,16},{4,20},{8,24},{12,28},{16,0},{20,4},{24,8},{28,12},{1,17},{... | collective-permute-start | bytes 12296 | tf_op jit(solution)/shard_map/ppermute | solution.py:563
  35.7 1.4 %collective-permute-start.11 = (f32[264,128]{1,0:T(8,128)S(1)}, f32[264,128]{1,0:T(8,128)S(1)}, u32[]{:S(2)}, u32[]{:S(2)}) collective-permute-start(f32[264,128]{1,0:T(8,128)S(1)} %pad_maximum_fusion.1), channel_id=1, source_target_pairs={{0,4},{4,0},{8,12},{12,8},{16,20},{20,16},{24,28},{28,24},{1,5},{5... | collective-permute-start | bytes 405512 | tf_op jit(solution)/shard_map/ppermute | solution.py:563
